TPU v7x, 128 devices: a whole 4x4x4 slice. The times are simulated.
128 devices in a mesh: layer: 2 (over x_lo), row: 8 (over y, core), col: 8 (over x_hi, z).
Axes of the slice: x: 4 (x_hi: 2, x_lo: 2; x = x_hi * 2 + x_lo), y: 4, z: 4, core: 2. Of those that a mesh axis runs over, the one named last changes fastest.
Arguments:
- owner_blocks: float32 [256, 64, 2048], P(('layer', 'row', 'col')), may hold values from -0.625 to 0.625
- owner_counts: int32 [8, 16], P('row'), may hold values from 1 to 2, 20 in all within a row
- block_cols: int32 [160, 32], replicated, may hold values from 0 to 159, as said below
- filter_mask: int32 [160, 32], replicated, may hold values 0 or 1
- gamma: float32 [1], replicated, may hold values from 0.5 to 2.5
Outputs:
- purified: float32 [160, 64, 2048], P('row', None, 'col')
Inputs may be any that keep to these rules, and one draw needn't show every extreme that they name: `block_cols`: slots g * 4 to (g + 1) * 4 - 1 of each block row hold distinct block columns of g * 20 to (g + 1) * 20 - 1; block row i holds block column i. `owner_counts`: each row sums to 20.
All inputs are finite; a program needn't handle non-finite values.
Results may differ from a plain program's by a relative error of at most 0.0003.
Values sent between devices are 32-bit elements; how exact they have to be, the bound alone decides.
No kernel may reach another device: no remote copies, remote signals or barrier semaphores. Data moves between devices by JAX's collectives and lax.ppermute only.
A program may use at most 256 MiB of HBM per device.

v0:
```python
import jax
import jax.numpy as jnp
from jax import lax
from jax.sharding import PartitionSpec as P


def from_behind(x, axis, by):
    count = lax.axis_size(axis)
    return lax.ppermute(x, axis, [(i, (i + by) % count) for i in range(count)])


def skew_along_cols(panel, amount):
    for bit in range(lax.axis_size("col").bit_length() - 1):
        moved = from_behind(panel, "col", -(1 << bit))
        panel = jnp.where(amount >> bit & 1 == 1, moved, panel)
    return panel


def skew_along_rows(panel, amount):
    for bit in range(lax.axis_size("row").bit_length() - 1):
        moved = from_behind(panel, "row", -(1 << bit))
        panel = jnp.where(amount >> bit & 1 == 1, moved, panel)
    return panel


def panel_product(total, left, right, group, block_cols, grid_row, grid_col, out_cols):
    rows = total.shape[0]
    width = total.shape[1]
    span = out_cols.shape[1]
    left_cols = (
        lax.dynamic_slice(block_cols, (grid_row * rows, group * span), (rows, span)) - group * rows
    )
    right_cols = lax.dynamic_slice(block_cols, (group * rows, grid_col * span), (rows, span))
    flat_cols = left_cols.reshape(-1)
    picked = jnp.take(right, flat_cols, axis=0).reshape(rows, span, width, span, width)
    picked_cols = jnp.take(right_cols, flat_cols, axis=0).reshape(rows, span, span)
    match = (picked_cols[:, :, :, None] == out_cols[:, None, None, :]).astype(jnp.float32)
    moved = jnp.einsum("ikdlc,iklm->ikdmc", picked, match, precision=lax.Precision.HIGHEST)
    factor = left.reshape(rows, width, span, width)
    term = jnp.einsum("iakd,ikdmc->iamc", factor, moved, precision=lax.Precision.HIGHEST)
    return total + term.reshape(rows, width, span * width)


def shifting_product(left, right, first, steps, block_cols, grid_row, grid_col, out_cols):
    total = jnp.zeros(left.shape, jnp.float32)
    count = lax.axis_size("col")
    for step in range(steps):
        group = (first + step) % count
        total = panel_product(total, left, right, group, block_cols, grid_row, grid_col, out_cols)
        if step + 1 < steps:
            left = from_behind(left, "col", -1)
            right = from_behind(right, "row", -1)
    return total


def body(owner_blocks, owner_counts, block_cols, filter_mask, gamma):
    count = lax.axis_size("row")
    layers = lax.axis_size("layer")
    ncol = lax.axis_size("col")
    steps = count // layers
    layer = lax.axis_index("layer")
    grid_row = lax.axis_index("row")
    grid_col = lax.axis_index("col")
    cap = owner_blocks.shape[0]
    width = owner_blocks.shape[1]
    span = block_cols.shape[1] // ncol
    rows = block_cols.shape[0] // count
    counts = owner_counts[0]
    ends = jnp.cumsum(counts)
    local = jnp.arange(rows, dtype=jnp.int32)
    which = jnp.sum((ends[None, :] <= local[:, None]).astype(jnp.int32), axis=1)
    slot = local - (jnp.take(ends, which) - jnp.take(counts, which))
    source = which * cap + slot
    grouped = owner_blocks.reshape(cap, width, ncol, span * width).transpose(2, 0, 1, 3)
    plain_send = jnp.tile(grouped, (layers, 1, 1, 1)).reshape(
        layers * ncol * cap, width, span * width
    )
    first = (grid_row + grid_col + layer * steps) % ncol
    plain_got = lax.all_to_all(
        plain_send, ("layer", "col"), split_axis=0, concat_axis=0, tiled=True
    )
    density = jnp.take(plain_got, source, axis=0)
    left = skew_along_cols(density, (grid_row + layer * steps) % ncol)
    right = skew_along_rows(density, (grid_col + layer * steps) % count)
    out_cols = lax.dynamic_slice(block_cols, (grid_row * rows, grid_col * span), (rows, span))
    keep = lax.dynamic_slice(filter_mask, (grid_row * rows, grid_col * span), (rows, span)).astype(
        jnp.float32
    )
    partial_value = shifting_product(
        left, right, first, steps, block_cols, grid_row, grid_col, out_cols
    )
    square = lax.psum(partial_value, "layer")
    square = (square.reshape(rows, width, span, width) * keep[:, None, :, None]).reshape(
        rows, width, span * width
    )
    global_rows = grid_row * rows + local
    own = (out_cols == global_rows[:, None]).astype(jnp.float32)
    unit = (own[:, None, :, None] * jnp.eye(width, dtype=jnp.float32)[None, :, None, :]).reshape(
        rows, width, span * width
    )
    mix = gamma[0]
    mixed = mix * unit + (4.0 - 2.0 * mix) * density + (mix - 3.0) * square
    left_panel = skew_along_cols(square, (grid_row + layer * steps) % ncol)
    right_panel = skew_along_rows(mixed, (grid_col + layer * steps) % count)
    total = shifting_product(
        left_panel, right_panel, first, steps, block_cols, grid_row, grid_col, out_cols
    )
    return lax.psum(total, "layer")


def solution(mesh):
    placed = (P(("layer", "row", "col"), None, None), P("row", None), P(), P(), P())
    return jax.shard_map(
        body, mesh=mesh, in_specs=placed, out_specs=P("row", None, "col"), check_vma=False
    )
```

profile of v0, /device:TPU:1, one launch (start us, length us, event | category | flops | bytes accessed | tf_op | source)
XLA Modules:
  0.0 775.9 jit_solution(6869017857305051186)
XLA Ops:
  20.5 23.8 %all-to-all-done = f32[32,64,256]{2,1,0:T(8,128)S(1)} async-done(((f32[32,64,256]{2,1,0:T(8,128)}), f32[32,64,256]{2,1,0:T(8,128)S(1)}, u32[]{:S(2)}, u32[]{:S(2)}) %all-to-all-start) | async-done | bytes 2097184 | tf_op jit(solution)/shard_map/all_to_all | solution.py:79
  54.0 23.0 %collective-permute-done = f32[20,64,256]{2,1,0:T(8,128)} collective-permute-done((f32[20,64,256]{2,1,0:T(8,128)S(1)}, f32[20,64,256]{2,1,0:T(8,128)}, u32[]{:S(2)}, u32[]{:S(2)}) %collective-permute-start) | collective-permute-done | bytes 1310752 | tf_op jit(solution)/shard_map/ppermute | solution.py:9
  87.1 22.8 %collective-permute-done.4 = f32[20,64,256]{2,1,0:T(8,128)S(1)} collective-permute-done((f32[20,64,256]{2,1,0:T(8,128)S(1)}, f32[20,64,256]{2,1,0:T(8,128)S(1)}, u32[]{:S(2)}, u32[]{:S(2)}) %collective-permute-start.4) | collective-permute-done | bytes 1310752 | tf_op jit(solution)/shard_map/ppermute | solution.py:9
  117.9 24.1 %collective-permute-done.5 = f32[20,64,256]{2,1,0:T(8,128)} collective-permute-done((f32[20,64,256]{2,1,0:T(8,128)S(1)}, f32[20,64,256]{2,1,0:T(8,128)}, u32[]{:S(2)}, u32[]{:S(2)}) %collective-permute-start.5) | collective-permute-done | bytes 1310752 | tf_op jit(solution)/shard_map/ppermute | solution.py:9
  171.9 15.2 %convolution_bitcast_fusion.7 = f32[20,4,64,4,64]{4,3,2,1,0:T(4,128)} fusion(f32[20,4,64,4,64]{4,3,2,1,0:T(4,128)} %reshape.159, s32[20,4]{1,0:T(8,128)S(1)} %copy.46, s32[20,4,4]{2,1,0:T(4,128)S(1)} %bitcast.129), kind=kOutput, calls=%fused_computation.38 | convolution fusion | flops 62915840 | bytes 10487360 | tf_op jit(solution)/shard_map/ikdlc,iklm->ikdmc/dot_general | solution.py:38
  190.5 13.7 %fusion.14 = f32[20,64,4,64,1]{3,1,4,2,0:T(8,128)} fusion(f32[20,4,64,4,64]{4,3,2,1,0:T(4,128)} %convolution_bitcast_fusion.7, f32[20,64,4,64,1]{3,2,1,0,4:T(4,128)} %bitcast.117), kind=kOutput, calls=%fused_computation.29 | convolution fusion | flops 1006632960 | bytes 7864320 | tf_op jit(solution)/shard_map/iakd,ikdmc->iamc/dot_general | solution.py:40
  226.5 15.1 %convolution_bitcast_fusion.6 = f32[20,4,64,4,64]{4,3,2,1,0:T(4,128)} fusion(f32[20,4,64,4,64]{4,3,2,1,0:T(4,128)} %reshape.162, s32[20,4,4]{2,1,0:T(4,128)S(1)} %bitcast.127, s32[20,4]{1,0:T(8,128)S(1)} %copy.46), kind=kOutput, calls=%fused_computation.37 | convolution fusion | flops 62915840 | bytes 10487360 | tf_op jit(solution)/shard_map/ikdlc,iklm->ikdmc/dot_general | solution.py:38
  244.9 13.4 %fusion.12 = f32[20,64,4,64,1]{3,1,4,2,0:T(8,128)} fusion(f32[20,4,64,4,64]{4,3,2,1,0:T(4,128)} %convolution_bitcast_fusion.6, f32[20,64,4,64,1]{3,2,1,0,4:T(4,128)} %bitcast.118), kind=kOutput, calls=%fused_computation.27 | convolution fusion | flops 1006632960 | bytes 7864320 | tf_op jit(solution)/shard_map/iakd,ikdmc->iamc/dot_general | solution.py:40
  280.3 12.8 %convolution_bitcast_fusion.5 = f32[20,4,64,4,64]{4,3,2,1,0:T(4,128)S(1)} fusion(f32[20,4,64,4,64]{4,3,2,1,0:T(4,128)} %reshape.165, s32[20,4,4]{2,1,0:T(4,128)S(1)} %bitcast.125, s32[20,4]{1,0:T(8,128)S(1)} %copy.46), kind=kOutput, calls=%fused_computation.36 | convolution fusion | flops 62915840 | bytes 10487360 | tf_op jit(solution)/shard_map/ikdlc,iklm->ikdmc/dot_general | solution.py:38
  320.7 15.4 %convolution_bitcast_fusion.4 = f32[20,4,64,4,64]{4,3,2,1,0:T(4,128)} fusion(f32[20,4,64,4,64]{4,3,2,1,0:T(4,128)} %reshape.168, s32[20,4,4]{2,1,0:T(4,128)S(1)} %bitcast.123, s32[20,4]{1,0:T(8,128)S(1)} %copy.46), kind=kOutput, calls=%fused_computation.35 | convolution fusion | flops 62915840 | bytes 10487360 | tf_op jit(solution)/shard_map/ikdlc,iklm->ikdmc/dot_general | solution.py:38
  338.4 12.1 %bitcast_add_fusion.3 = f32[20,64,4,64]{3,1,2,0:T(8,128)S(1)} fusion(f32[20,64,4,64,1]{3,1,4,2,0:T(8,128)} %fusion.10, f32[20,64,4,64,1]{3,1,4,2,0:T(8,128)} %fusion.12, f32[20,64,4,64,1]{3,1,4,2,0:T(8,128)} %fusion.14, f32[20,4,64,4,64]{4,3,2,1,0:T(4,128)} %convolution_bitcast_fusion.4, f32[20,64,4,64,1]{3,2,1,0,4:T(4,128)S(1)} %bitcast.115), kind=kOutput, calls=%fused_computation.46 | convolution fusion | flops 1007616000 | bytes 11796480 | tf_op jit(solution)/shard_map/iakd,ikdmc->iamc/dot_general | solution.py:40
  359.0 48.9 %all-reduce.3.cloned.1.call-done = f32[20,64,256]{2,1,0:T(8,128)} async-done(((f32[20,64,256]{2,1,0:T(8,128)}), f32[20,64,256]{2,1,0:T(8,128)}) %all-reduce.3.cloned.1.call-update) | async-done | bytes 1310736 | tf_op jit(solution)/shard_map/psum | solution.py:92
  415.3 11.9 %collective-permute-done.15 = f32[20,64,256]{2,1,0:T(8,128)S(1)} collective-permute-done((f32[20,64,256]{2,1,0:T(8,128)S(1)}, f32[20,64,256]{2,1,0:T(8,128)S(1)}, u32[]{:S(2)}, u32[]{:S(2)}) %collective-permute-start.15) | collective-permute-done | bytes 1310752 | tf_op jit(solution)/shard_map/ppermute | solution.py:9
  430.7 10.4 %collective-permute-done.12 = f32[20,64,256]{2,1,0:T(8,128)S(1)} collective-permute-done((f32[20,64,256]{2,1,0:T(8,128)S(1)}, f32[20,64,256]{2,1,0:T(8,128)S(1)}, u32[]{:S(2)}, u32[]{:S(2)}) %collective-permute-start.12) | collective-permute-done | bytes 1310752 | tf_op jit(solution)/shard_map/ppermute | solution.py:9
  443.8 13.8 %collective-permute-done.16 = f32[20,64,256]{2,1,0:T(8,128)S(1)} collective-permute-done((f32[20,64,256]{2,1,0:T(8,128)S(1)}, f32[20,64,256]{2,1,0:T(8,128)S(1)}, u32[]{:S(2)}, u32[]{:S(2)}) %collective-permute-start.16) | collective-permute-done | bytes 1310752 | tf_op jit(solution)/shard_map/ppermute | solution.py:9
  471.9 17.0 %collective-permute-done.17 = f32[20,64,256]{2,1,0:T(8,128)S(1)} collective-permute-done((f32[20,64,256]{2,1,0:T(8,128)S(1)}, f32[20,64,256]{2,1,0:T(8,128)S(1)}, u32[]{:S(2)}, u32[]{:S(2)}) %collective-permute-start.17) | collective-permute-done | bytes 1310752 | tf_op jit(solution)/shard_map/ppermute | solution.py:9
  525.1 15.2 %convolution_bitcast_fusion.3 = f32[20,4,64,4,64]{4,3,2,1,0:T(4,128)} fusion(f32[20,4,64,4,64]{4,3,2,1,0:T(4,128)} %reshape.170, s32[20,4]{1,0:T(8,128)S(1)} %copy.46, s32[20,4,4]{2,1,0:T(4,128)S(1)} %bitcast.130), kind=kOutput, calls=%fused_computation.34 | convolution fusion | flops 62915840 | bytes 10487360 | tf_op jit(solution)/shard_map/ikdlc,iklm->ikdmc/dot_general | solution.py:38
  543.7 13.7 %fusion.6 = f32[20,64,4,64,1]{3,1,4,2,0:T(8,128)} fusion(f32[20,4,64,4,64]{4,3,2,1,0:T(4,128)} %convolution_bitcast_fusion.3, f32[20,64,4,64,1]{3,2,1,0,4:T(4,128)} %bitcast.119), kind=kOutput, calls=%fused_computation.21 | convolution fusion | flops 1006632960 | bytes 7864320 | tf_op jit(solution)/shard_map/iakd,ikdmc->iamc/dot_general | solution.py:40
  581.3 15.1 %convolution_bitcast_fusion.2 = f32[20,4,64,4,64]{4,3,2,1,0:T(4,128)} fusion(f32[20,4,64,4,64]{4,3,2,1,0:T(4,128)} %reshape.172, s32[20,4,4]{2,1,0:T(4,128)S(1)} %bitcast.128, s32[20,4]{1,0:T(8,128)S(1)} %copy.46), kind=kOutput, calls=%fused_computation.33 | convolution fusion | flops 62915840 | bytes 10487360 | tf_op jit(solution)/shard_map/ikdlc,iklm->ikdmc/dot_general | solution.py:38
  599.7 13.4 %fusion.4 = f32[20,64,4,64,1]{3,1,4,2,0:T(8,128)} fusion(f32[20,4,64,4,64]{4,3,2,1,0:T(4,128)} %convolution_bitcast_fusion.2, f32[20,64,4,64,1]{3,2,1,0,4:T(4,128)} %bitcast.120), kind=kOutput, calls=%fused_computation.19 | convolution fusion | flops 1006632960 | bytes 7864320 | tf_op jit(solution)/shard_map/iakd,ikdmc->iamc/dot_general | solution.py:40
  639.0 12.8 %convolution_bitcast_fusion.1 = f32[20,4,64,4,64]{4,3,2,1,0:T(4,128)S(1)} fusion(f32[20,4,64,4,64]{4,3,2,1,0:T(4,128)} %reshape.174, s32[20,4,4]{2,1,0:T(4,128)S(1)} %bitcast.126, s32[20,4]{1,0:T(8,128)S(1)} %copy.46), kind=kOutput, calls=%fused_computation.32 | convolution fusion | flops 62915840 | bytes 10487360 | tf_op jit(solution)/shard_map/ikdlc,iklm->ikdmc/dot_general | solution.py:38
  679.4 15.4 %convolution_bitcast_fusion = f32[20,4,64,4,64]{4,3,2,1,0:T(4,128)} fusion(f32[20,4,64,4,64]{4,3,2,1,0:T(4,128)} %reshape.176, s32[20,4,4]{2,1,0:T(4,128)S(1)} %bitcast.124, s32[20,4]{1,0:T(8,128)S(1)} %copy.46), kind=kOutput, calls=%fused_computation.31 | convolution fusion | flops 62915840 | bytes 10487360 | tf_op jit(solution)/shard_map/ikdlc,iklm->ikdmc/dot_general | solution.py:38
  697.0 11.9 %bitcast_add_fusion = f32[20,64,4,64]{3,1,2,0:T(8,128)S(1)} fusion(f32[20,64,4,64,1]{3,1,4,2,0:T(8,128)} %fusion.2, f32[20,64,4,64,1]{3,1,4,2,0:T(8,128)} %fusion.4, f32[20,64,4,64,1]{3,1,4,2,0:T(8,128)} %fusion.6, f32[20,4,64,4,64]{4,3,2,1,0:T(4,128)} %convolution_bitcast_fusion, f32[20,64,4,64,1]{3,2,1,0,4:T(4,128)S(1)} %bitcast.116), kind=kOutput, calls=%fused_computation.39 | convolution fusion | flops 1007616000 | bytes 11796480 | tf_op jit(solution)/shard_map/iakd,ikdmc->iamc/dot_general | solution.py:40
  713.4 52.8 %all-reduce.5.cloned.1.call-done = f32[20,64,256]{2,1,0:T(8,128)} async-done(((f32[20,64,256]{2,1,0:T(8,128)}), f32[20,64,256]{2,1,0:T(8,128)}) %all-reduce.5.cloned.1.call-update) | async-done | bytes 1310736 | tf_op jit(solution)/shard_map/psum | solution.py:108
  (168 shorter events, 317.4 us)
Async XLA Ops:
  10.1 34.2 %all-to-all-start = ((f32[32,64,256]{2,1,0:T(8,128)}), f32[32,64,256]{2,1,0:T(8,128)S(1)}, u32[]{:S(2)}, u32[]{:S(2)}) async-start(f32[32,64,256]{2,1,0:T(8,128)} %bitcast.3), calls=%async_computation | async-start | bytes 4194304 | tf_op jit(solution)/shard_map/all_to_all | solution.py:79
  18.7 389.3 %all-reduce.3.cloned.1.call-start = ((), (), s32[]{:S(2)}) async-start(), calls=%async_computation.1 | async-start | bytes 2621440 | tf_op jit(solution)/shard_map/psum | solution.py:92
  45.1 31.9 %collective-permute-start = (f32[20,64,256]{2,1,0:T(8,128)S(1)}, f32[20,64,256]{2,1,0:T(8,128)}, u32[]{:S(2)}, u32[]{:S(2)}) collective-permute-start(f32[20,64,256]{2,1,0:T(8,128)S(1)} %broadcast_select_fusion.8), channel_id=1, source_target_pairs={{0,7},{1,0},{2,1},{3,2},{4,3},{5,4},{6,5},{7,6},{8,15},{9,8},{10,9... | collective-permute-start | bytes 3932168 | tf_op jit(solution)/shard_map/ppermute | solution.py:9
  79.7 30.3 %collective-permute-start.4 = (f32[20,64,256]{2,1,0:T(8,128)S(1)}, f32[20,64,256]{2,1,0:T(8,128)S(1)}, u32[]{:S(2)}, u32[]{:S(2)}) collective-permute-start(f32[20,64,256]{2,1,0:T(8,128)S(1)} %get-tuple-element.15), channel_id=1, source_target_pairs={{0,48},{8,56},{16,0},{24,8},{32,16},{40,24},{48,32},{56,40},{1,49}... | collective-permute-start | bytes 3932168 | tf_op jit(solution)/shard_map/ppermute | solution.py:9
  83.0 31.3 %collective-permute-start.1 = (f32[20,64,256]{2,1,0:T(8,128)}, f32[20,64,256]{2,1,0:T(8,128)}, u32[]{:S(2)}, u32[]{:S(2)}) collective-permute-start(f32[20,64,256]{2,1,0:T(8,128)} %get-tuple-element.14), channel_id=1, source_target_pairs={{0,6},{1,7},{2,0},{3,1},{4,2},{5,3},{6,4},{7,5},{8,14},{9,15},{10,... | collective-permute-start | bytes 3932168 | tf_op jit(solution)/shard_map/ppermute | solution.py:9
  111.4 30.5 %collective-permute-start.5 = (f32[20,64,256]{2,1,0:T(8,128)S(1)}, f32[20,64,256]{2,1,0:T(8,128)}, u32[]{:S(2)}, u32[]{:S(2)}) collective-permute-start(f32[20,64,256]{2,1,0:T(8,128)S(1)} %broadcast_select_fusion.12), channel_id=1, source_target_pairs={{0,32},{8,40},{16,48},{24,56},{32,0},{40,8},{48,16},{56,24},{1,33}... | collective-permute-start | bytes 3932168 | tf_op jit(solution)/shard_map/ppermute | solution.py:9
  116.9 30.8 %collective-permute-start.2 = (f32[20,64,256]{2,1,0:T(8,128)}, f32[20,64,256]{2,1,0:T(8,128)}, u32[]{:S(2)}, u32[]{:S(2)}) collective-permute-start(f32[20,64,256]{2,1,0:T(8,128)} %broadcast_select_fusion.18), channel_id=1, source_target_pairs={{0,4},{1,5},{2,6},{3,7},{4,0},{5,1},{6,2},{7,3},{8,12},{9,13},{10,... | collective-permute-start | bytes 3932168 | tf_op jit(solution)/shard_map/ppermute | solution.py:9
  142.1 62.1 %collective-permute-start.7 = (f32[20,64,256]{2,1,0:T(8,128)S(1)}, f32[20,64,256]{2,1,0:T(8,128)S(1)}, u32[]{:S(2)}, u32[]{:S(2)}) collective-permute-start(f32[20,64,256]{2,1,0:T(8,128)S(1)} %broadcast_select_fusion.14), channel_id=1, source_target_pairs={{0,56},{8,0},{16,8},{24,16},{32,24},{40,32},{48,40},{56,48},{1,57}... | collective-permute-start | bytes 3932168 | tf_op jit(solution)/shard_map/ppermute | solution.py:9
  150.3 76.2 %collective-permute-start.6 = (f32[20,64,256]{2,1,0:T(8,128)}, f32[20,64,256]{2,1,0:T(8,128)}, u32[]{:S(2)}, u32[]{:S(2)}) collective-permute-start(f32[20,64,256]{2,1,0:T(8,128)} %broadcast_select_fusion.20), channel_id=1, source_target_pairs={{0,7},{1,0},{2,1},{3,2},{4,3},{5,4},{6,5},{7,6},{8,15},{9,8},{10,9... | collective-permute-start | bytes 3932168 | tf_op jit(solution)/shard_map/ppermute | solution.py:9
  222.6 35.7 %collective-permute-start.9 = (f32[20,64,256]{2,1,0:T(8,128)S(1)}, f32[20,64,256]{2,1,0:T(8,128)S(1)}, u32[]{:S(2)}, u32[]{:S(2)}) collective-permute-start(f32[20,64,256]{2,1,0:T(8,128)S(1)} %collective-permute-done.7), channel_id=1, source_target_pairs={{0,56},{8,0},{16,8},{24,16},{32,24},{40,32},{48,40},{56,48},{1,57}... | collective-permute-start | bytes 3932168 | tf_op jit(solution)/shard_map/ppermute | solution.py:9
  226.5 50.4 %collective-permute-start.8 = (f32[20,64,256]{2,1,0:T(8,128)}, f32[20,64,256]{2,1,0:T(8,128)}, u32[]{:S(2)}, u32[]{:S(2)}) collective-permute-start(f32[20,64,256]{2,1,0:T(8,128)} %collective-permute-done.6), channel_id=1, source_target_pairs={{0,7},{1,0},{2,1},{3,2},{4,3},{5,4},{6,5},{7,6},{8,15},{9,8},{10,9... | collective-permute-start | bytes 3932168 | tf_op jit(solution)/shard_map/ppermute | solution.py:9
  280.3 55.7 %collective-permute-start.10 = (f32[20,64,256]{2,1,0:T(8,128)}, f32[20,64,256]{2,1,0:T(8,128)}, u32[]{:S(2)}, u32[]{:S(2)}) collective-permute-start(f32[20,64,256]{2,1,0:T(8,128)} %collective-permute-done.8), channel_id=1, source_target_pairs={{0,7},{1,0},{2,1},{3,2},{4,3},{5,4},{6,5},{7,6},{8,15},{9,8},{10,9... | collective-permute-start | bytes 3932168 | tf_op jit(solution)/shard_map/ppermute | solution.py:9
  357.6 408.7 %all-reduce.5.cloned.1.call-start = ((), (), s32[]{:S(2)}) async-start(), calls=%async_computation.2 | async-start | bytes 2621440 | tf_op jit(solution)/shard_map/psum | solution.py:108
  410.5 30.7 %collective-permute-start.12 = (f32[20,64,256]{2,1,0:T(8,128)S(1)}, f32[20,64,256]{2,1,0:T(8,128)S(1)}, u32[]{:S(2)}, u32[]{:S(2)}) collective-permute-start(f32[20,64,256]{2,1,0:T(8,128)S(1)} %get-tuple-element.8), channel_id=1, source_target_pairs={{0,7},{1,0},{2,1},{3,2},{4,3},{5,4},{6,5},{7,6},{8,15},{9,8},{10,9... | collective-permute-start | bytes 3932168 | tf_op jit(solution)/shard_map/ppermute | solution.py:9
  427.3 30.3 %collective-permute-start.16 = (f32[20,64,256]{2,1,0:T(8,128)S(1)}, f32[20,64,256]{2,1,0:T(8,128)S(1)}, u32[]{:S(2)}, u32[]{:S(2)}) collective-permute-start(f32[20,64,256]{2,1,0:T(8,128)S(1)} %broadcast_select_fusion.9), channel_id=1, source_target_pairs={{0,48},{8,56},{16,0},{24,8},{32,16},{40,24},{48,32},{56,40},{1,49}... | collective-permute-start | bytes 3932168 | tf_op jit(solution)/shard_map/ppermute | solution.py:9
  441.3 28.7 %collective-permute-start.13 = (f32[20,64,256]{2,1,0:T(8,128)S(1)}, f32[20,64,256]{2,1,0:T(8,128)S(1)}, u32[]{:S(2)}, u32[]{:S(2)}) collective-permute-start(f32[20,64,256]{2,1,0:T(8,128)S(1)} %broadcast_select_fusion.15), channel_id=1, source_target_pairs={{0,6},{1,7},{2,0},{3,1},{4,2},{5,3},{6,4},{7,5},{8,14},{9,15},{10,... | collective-permute-start | bytes 3932168 | tf_op jit(solution)/shard_map/ppermute | solution.py:9
  457.8 31.0 %collective-permute-start.17 = (f32[20,64,256]{2,1,0:T(8,128)S(1)}, f32[20,64,256]{2,1,0:T(8,128)S(1)}, u32[]{:S(2)}, u32[]{:S(2)}) collective-permute-start(f32[20,64,256]{2,1,0:T(8,128)S(1)} %broadcast_select_fusion.11), channel_id=1, source_target_pairs={{0,32},{8,40},{16,48},{24,56},{32,0},{40,8},{48,16},{56,24},{1,33}... | collective-permute-start | bytes 3932168 | tf_op jit(solution)/shard_map/ppermute | solution.py:9
  471.3 28.1 %collective-permute-start.14 = (f32[20,64,256]{2,1,0:T(8,128)}, f32[20,64,256]{2,1,0:T(8,128)}, u32[]{:S(2)}, u32[]{:S(2)}) collective-permute-start(f32[20,64,256]{2,1,0:T(8,128)} %broadcast_select_fusion.17), channel_id=1, source_target_pairs={{0,4},{1,5},{2,6},{3,7},{4,0},{5,1},{6,2},{7,3},{8,12},{9,13},{10,... | collective-permute-start | bytes 3932168 | tf_op jit(solution)/shard_map/ppermute | solution.py:9
  489.0 68.4 %collective-permute-start.19 = (f32[20,64,256]{2,1,0:T(8,128)S(1)}, f32[20,64,256]{2,1,0:T(8,128)S(1)}, u32[]{:S(2)}, u32[]{:S(2)}) collective-permute-start(f32[20,64,256]{2,1,0:T(8,128)S(1)} %broadcast_select_fusion.13), channel_id=1, source_target_pairs={{0,56},{8,0},{16,8},{24,16},{32,24},{40,32},{48,40},{56,48},{1,57}... | collective-permute-start | bytes 3932168 | tf_op jit(solution)/shard_map/ppermute | solution.py:9
  501.9 79.4 %collective-permute-start.18 = (f32[20,64,256]{2,1,0:T(8,128)}, f32[20,64,256]{2,1,0:T(8,128)}, u32[]{:S(2)}, u32[]{:S(2)}) collective-permute-start(f32[20,64,256]{2,1,0:T(8,128)} %broadcast_select_fusion.19), channel_id=1, source_target_pairs={{0,7},{1,0},{2,1},{3,2},{4,3},{5,4},{6,5},{7,6},{8,15},{9,8},{10,9... | collective-permute-start | bytes 3932168 | tf_op jit(solution)/shard_map/ppermute | solution.py:9
  575.8 37.4 %collective-permute-start.21 = (f32[20,64,256]{2,1,0:T(8,128)S(1)}, f32[20,64,256]{2,1,0:T(8,128)S(1)}, u32[]{:S(2)}, u32[]{:S(2)}) collective-permute-start(f32[20,64,256]{2,1,0:T(8,128)S(1)} %collective-permute-done.19), channel_id=1, source_target_pairs={{0,56},{8,0},{16,8},{24,16},{32,24},{40,32},{48,40},{56,48},{1,57}... | collective-permute-start | bytes 3932168 | tf_op jit(solution)/shard_map/ppermute | solution.py:9
  581.3 54.3 %collective-permute-start.20 = (f32[20,64,256]{2,1,0:T(8,128)}, f32[20,64,256]{2,1,0:T(8,128)}, u32[]{:S(2)}, u32[]{:S(2)}) collective-permute-start(f32[20,64,256]{2,1,0:T(8,128)} %collective-permute-done.18), channel_id=1, source_target_pairs={{0,7},{1,0},{2,1},{3,2},{4,3},{5,4},{6,5},{7,6},{8,15},{9,8},{10,9... | collective-permute-start | bytes 3932168 | tf_op jit(solution)/shard_map/ppermute | solution.py:9
  631.7 29.4 %collective-permute-start.23 = (f32[20,64,256]{2,1,0:T(8,128)S(1)}, f32[20,64,256]{2,1,0:T(8,128)S(1)}, u32[]{:S(2)}, u32[]{:S(2)}) collective-permute-start(f32[20,64,256]{2,1,0:T(8,128)S(1)} %collective-permute-done.21), channel_id=1, source_target_pairs={{0,56},{8,0},{16,8},{24,16},{32,24},{40,32},{48,40},{56,48},{1,57}... | collective-permute-start | bytes 3932168 | tf_op jit(solution)/shard_map/ppermute | solution.py:9
  639.0 55.7 %collective-permute-start.22 = (f32[20,64,256]{2,1,0:T(8,128)}, f32[20,64,256]{2,1,0:T(8,128)}, u32[]{:S(2)}, u32[]{:S(2)}) collective-permute-start(f32[20,64,256]{2,1,0:T(8,128)} %collective-permute-done.20), channel_id=1, source_target_pairs={{0,7},{1,0},{2,1},{3,2},{4,3},{5,4},{6,5},{7,6},{8,15},{9,8},{10,9... | collective-permute-start | bytes 3932168 | tf_op jit(solution)/shard_map/ppermute | solution.py:9
  (8 other events, 205.4 us)
Sparse Core Ops, SparseCore 0:
  357.7 50.2 all-reduce.2
  713.5 52.6 all-reduce.4
where the time goes:
time: 783 us; the launch traced here: 776 us
  waiting for transfers between devices  264 us (34%)
  matrix products  214 us (27%)
  local copies, waits for them, and re-layouts  154 us (20%)
  starting transfers between devices  69.5 us (9%)
  other arithmetic  59.4 us (8%)
  between operations  14.7 us (2%)
    ppermute x24, waiting for transfers between devices, from_behind(): return lax.ppermute(x, axis, [(i, (i + by) % count) for i in range(count)])  139 us
    dot_general x8, matrix products, panel_product(): jnp.einsum('ikdlc,iklm->ikdmc', picked, match, precision=lax.Precision.HI...  117 us
    dot_general x8, matrix products, panel_product(): jnp.einsum('iakd,ikdmc->iamc', factor, moved, precision=lax.Precision.HIG...  96.7 us
    reshape x8, local copies, waits for them, and re-layouts, panel_product(): jnp.take(right, flat_cols, axis=0).reshape(rows, span, width, span, width)  79.6 us
    ppermute x24, starting transfers between devices, from_behind(): return lax.ppermute(x, axis, [(i, (i + by) % count) for i in range(count)])  60.9 us
    psum x1, waiting for transfers between devices, body(): return lax.psum(total, 'layer')  52.8 us
    psum x1, waiting for transfers between devices, body(): square = lax.psum(partial_value, 'layer')  48.9 us
    select_n x8, other arithmetic, panel_product(): jnp.take(right, flat_cols, axis=0).reshape(rows, span, width, span, width)  41.9 us
  transfers between devices with their start and end apart: 27, of which 13 were waited for; matrix products, arithmetic and copies ran while one was open for 48% of the time, Pallas kernels for 0%

commit v1 on v0

v1 whole, which is shorter than its diff:
```python
import functools

import jax
import jax.numpy as jnp
from jax import lax
from jax.experimental import pallas as pl
from jax.experimental.pallas import tpu as pltpu
from jax.sharding import PartitionSpec as P

AXES = ("layer", "row", "col")
N_LAYER, N_Y, N_CORE, N_Q, N_Z = 2, 4, 2, 2, 4
N_GROUP = 8
N_SLOT = 4
HALF = 10


def moves(target):
    pairs = []
    for layer in range(N_LAYER):
        for y in range(N_Y):
            for core in range(N_CORE):
                for q in range(N_Q):
                    for z in range(N_Z):
                        there = target(layer, y, core, q, z)
                        if there is not None:
                            pairs.append((flat(layer, y, core, q, z), flat(*there)))
    return pairs


def flat(layer, y, core, q, z):
    row = (y % N_Y) * N_CORE + core % N_CORE
    return ((layer % N_LAYER) * N_Y * N_CORE + row) * N_Q * N_Z + (q % N_Q) * N_Z + z % N_Z


def source_a(layer, y, core, q, z):
    return core == z % 2


def source_b(layer, y, core, q, z):
    return core == layer ^ q


def always(*place):
    return True


def send(x, who, dlayer=0, dy=0, dcore=0, dq=0, dz=0):
    def target(layer, y, core, q, z):
        if who(layer, y, core, q, z):
            return layer + dlayer, y + dy, core + dcore, q + dq, z + dz
        return None

    return lax.ppermute(x, AXES, moves(target))


def other(who):
    return lambda *place: not who(*place)


def gather_left(own):
    rest = other(source_a)
    far = send(own, source_a, dlayer=1, dq=1)
    below = send(own, source_a, dz=1)
    above = send(own, source_a, dz=-1)
    first = send(below[:HALF], rest, dz=1)
    second = send(above[HALF:], rest, dz=-1)
    far_below = send(far, source_a, dz=1)
    far_above = send(far, source_a, dz=-1)
    far_first = send(first, source_a, dlayer=1, dq=1)
    far_second = send(second, source_a, dlayer=1, dq=1)
    return own, below, first, second, above, far, far_below, far_first, far_second, far_above


def gather_right(own, who):
    below = send(own, who, dy=1)
    above = send(own, who, dy=-1)
    first = send(below[:HALF], who, dy=1)
    second = send(above[HALF:], who, dy=-1)
    return own, above, first, second, below


def gather_right_pair(mine):
    rest = other(source_b)
    own = send(mine, source_b, dlayer=1)
    mine, above, first, second, below = gather_right(mine, source_b)
    own_below = send(own, rest, dy=1)
    own_above = send(own, rest, dy=-1)
    own_first = send(first, source_b, dlayer=1)
    own_second = send(second, source_b, dlayer=1)
    return (mine, above, first, second, below), (own, own_above, own_first, own_second, own_below)


def product_kernel(pair, rows, width, span, pick_ref, flag_ref, *refs):
    left, refs = refs[:10], refs[10:]
    count = 10 if pair else 5
    right, refs = refs[:count], refs[count:]
    out_ref, left_buf, right_buf, high, low, left_sem, right_sem = refs
    own, below, first, second, above, far, far_below, far_first, far_second, far_above = left
    is_source = flag_ref[0] == 1
    is_mine = flag_ref[1] == 1

    def bring(buf, sem, place, part, src, start, begin):
        copy = pltpu.make_async_copy(
            src.at[pl.ds(begin, HALF)], buf.at[place, pl.ds(part * HALF, HALF)], sem.at[place, part]
        )
        if start:
            copy.start()
        else:
            copy.wait()

    def right_start(sources):
        own_, above_, first_, second_, below_ = sources
        for place, src in ((0, own_), (1, above_), (3, below_)):
            for part in range(2):
                bring(right_buf, right_sem, place, part, src, True, part * HALF)
        bring(right_buf, right_sem, 2, 0, first_, True, 0)
        bring(right_buf, right_sem, 2, 1, second_, True, 0)

    if pair:

        @pl.when(is_mine)
        def _():
            right_start(right[:5])

        @pl.when(jnp.logical_not(is_mine))
        def _():
            right_start(right[5:])
    else:
        right_start(right)

    @pl.when(is_source)
    def _():
        for place, src in ((0, own), (2, far)):
            for part in range(2):
                bring(left_buf, left_sem, place, part, src, True, part * HALF)
        for place, part, src in ((1, 0, first), (1, 1, second), (3, 0, far_first), (3, 1, far_second)):
            bring(left_buf, left_sem, place, part, src, True, 0)

    @pl.when(jnp.logical_not(is_source))
    def _():
        for place, src in ((0, below), (1, above), (2, far_below), (3, far_above)):
            for part in range(2):
                bring(left_buf, left_sem, place, part, src, True, part * HALF)

    none = 4 * rows * span
    high[none] = jnp.zeros(high.shape[1:], high.dtype)
    low[none] = jnp.zeros(low.shape[1:], low.dtype)

    for place in range(4):
        for part in range(2):
            bring(right_buf, right_sem, place, part, right[0], False, 0)

            @pl.loop(0, HALF)
            def _(row):
                at = (place * rows + part * HALF + row) * span
                x = right_buf[place, part * HALF + row]
                for v in range(2):
                    piece = x[:, v * 2 * width : (v + 1) * 2 * width]
                    top = piece.astype(jnp.bfloat16).astype(jnp.float32)
                    rest = piece - top
                    high[at + 2 * v] = top.astype(jnp.bfloat16)
                    low[at + 2 * v] = rest.astype(jnp.bfloat16)
                    high[at + 2 * v + 1] = pltpu.roll(top, width, 1).astype(jnp.bfloat16)
                    low[at + 2 * v + 1] = pltpu.roll(rest, width, 1).astype(jnp.bfloat16)

    for place in range(4):
        for part in range(2):
            bring(left_buf, left_sem, place, part, own, False, 0)

    lane = lax.broadcasted_iota(jnp.int32, (width, 2 * width), 1) < width

    @pl.loop(0, rows)
    def _(row):
        both = jnp.zeros((2 * width, span * width), jnp.float32)
        single = jnp.zeros((width, span * width), jnp.float32)
        for place in range(4):
            top_rows, low_rows = [], []
            for k in range(span):
                at = ((row * 4 + place) * span + k) * span
                picks = [pick_ref[at + m] for m in range(span)]
                for table, rows_of in ((high, top_rows), (low, low_rows)):
                    rows_of.append(
                        jnp.concatenate(
                            [
                                jnp.where(lane, table[picks[0]], table[picks[1]]),
                                jnp.where(lane, table[picks[2]], table[picks[3]]),
                            ],
                            axis=1,
                        )
                    )
            x = left_buf[place, row]
            top = x.astype(jnp.bfloat16)
            rest = (x - top.astype(jnp.float32)).astype(jnp.bfloat16)
            both += jnp.dot(
                jnp.concatenate([top, rest], axis=0),
                jnp.concatenate(top_rows, axis=0),
                preferred_element_type=jnp.float32,
            )
            single += jnp.dot(
                top, jnp.concatenate(low_rows, axis=0), preferred_element_type=jnp.float32
            )
        out_ref[row] = both[:width] + both[width:] + single


def product(left, right, picks, flags):
    rows, width, wide = left[0].shape
    span = wide // width
    pair = len(right) == 10
    table = pltpu.VMEM((4 * rows * span + 1, width, 2 * width), jnp.bfloat16)
    return pl.pallas_call(
        functools.partial(product_kernel, pair, rows, width, span),
        out_shape=jax.ShapeDtypeStruct((rows, width, wide), jnp.float32),
        in_specs=[pl.BlockSpec(memory_space=pltpu.SMEM)] * 2
        + [pl.BlockSpec(memory_space=pl.ANY)] * (len(left) + len(right)),
        out_specs=pl.BlockSpec(memory_space=pltpu.VMEM),
        scratch_shapes=[
            pltpu.VMEM((4, rows, width, wide), jnp.float32),
            pltpu.VMEM((4, rows, width, wide), jnp.float32),
            table,
            table,
            pltpu.SemaphoreType.DMA((4, 2)),
            pltpu.SemaphoreType.DMA((4, 2)),
        ],
        compiler_params=pltpu.CompilerParams(vmem_limit_bytes=48 * 1024 * 1024),
        cost_estimate=pl.CostEstimate(flops=10**9, bytes_accessed=12 * 10**6, transcendentals=0),
    )(picks, flags, *left, *right)


def pick_table(block_cols, out_cols, grid_row, grid_col, core, y, q, z, rows, span):
    cols = block_cols.reshape(N_GROUP, rows, N_GROUP, span)
    left_cols = lax.dynamic_slice(block_cols, (grid_row * rows, 0), (rows, N_GROUP * span))
    left_cols = left_cols.reshape(rows, N_GROUP, span)
    source = core == z % 2
    z_first = jnp.where(source, z, (z + N_Z - 1) % N_Z)
    z_second = jnp.where(source, (z + 2) % N_Z, (z + 1) % N_Z)
    groups = jnp.stack(
        [q * N_Z + z_first, q * N_Z + z_second, (1 - q) * N_Z + z_first, (1 - q) * N_Z + z_second]
    )
    names = jnp.arange(N_GROUP, dtype=jnp.int32)
    chosen = (groups[:, None] == names[None, :]).astype(jnp.int32)
    local = left_cols - names[None, :, None] * rows
    slots = jnp.sum(local[:, None] * chosen[None, :, :, None], axis=2)
    right_cols = jnp.sum(
        cols * (names == grid_col).astype(jnp.int32)[None, None, :, None], axis=2
    )
    right_cols = jnp.sum(right_cols[None] * chosen[:, :, None, None], axis=1)
    hit = (slots[..., None] == jnp.arange(rows, dtype=jnp.int32)).astype(jnp.int32)
    found = jnp.sum(hit[..., None] * right_cols[None, :, None], axis=3)
    place = (groups // 2 - y) % N_Y
    base = ((place[None, :, None] * rows + slots) * 2)[..., None]
    match = found[..., :, None] == out_cols[:, None, None, None, :]
    piece = jnp.arange(span, dtype=jnp.int32)
    swap = (piece[:, None] + piece[None, :]) % 2
    entry = (base[..., None] + (piece // 2)[:, None]) * 2 + swap
    none = 4 * rows * span
    picked = none + jnp.sum(jnp.where(match, entry - none, 0), axis=3)
    return picked.reshape(-1).astype(jnp.int32)


def body(owner_blocks, owner_counts, block_cols, filter_mask, gamma):
    layer = lax.axis_index("layer")
    grid_row = lax.axis_index("row")
    grid_col = lax.axis_index("col")
    y, core = grid_row // N_CORE, grid_row % N_CORE
    q, z = grid_col // N_Z, grid_col % N_Z
    part = (layer + q) % 2
    cap, width, _ = owner_blocks.shape
    span = N_SLOT
    rows = block_cols.shape[0] // N_GROUP

    counts = owner_counts[0]
    ends = jnp.cumsum(counts)
    local = jnp.arange(rows, dtype=jnp.int32)
    which = jnp.sum((ends[None, :] <= local[:, None]).astype(jnp.int32), axis=1)
    slot = local - (jnp.take(ends, which) - jnp.take(counts, which))
    source = which * cap + slot
    grouped = owner_blocks.reshape(cap, width, N_GROUP, span * width).transpose(2, 0, 1, 3)
    plain_send = jnp.tile(grouped, (N_LAYER, 1, 1, 1)).reshape(
        N_LAYER * N_GROUP * cap, width, span * width
    )
    plain_got = lax.all_to_all(
        plain_send, ("layer", "col"), split_axis=0, concat_axis=0, tiled=True
    )
    density = jnp.take(plain_got, source, axis=0)

    row_here = 2 * y + part
    out_cols = lax.dynamic_slice(block_cols, (row_here * rows, grid_col * span), (rows, span))
    keep = lax.dynamic_slice(filter_mask, (row_here * rows, grid_col * span), (rows, span))
    picks = pick_table(block_cols, out_cols, row_here, grid_col, core, y, q, z, rows, span)
    flags = jnp.stack([core == z % 2, core == part]).astype(jnp.int32)

    across = send(density, always, dcore=1)
    mine = jnp.where(core == part, density, across)
    right = gather_right(density, always)
    left = gather_left(mine)
    partial_value = product(left, right, picks, flags)
    square = partial_value + send(partial_value, always, dcore=1)
    keep_wide = jnp.repeat(keep.astype(jnp.float32), width, axis=1)[:, None, :]
    square = square * keep_wide
    own = (out_cols == (row_here * rows + local)[:, None]).astype(jnp.float32)
    unit = (own[:, None, :, None] * jnp.eye(width, dtype=jnp.float32)[None, :, None, :]).reshape(
        rows, width, span * width
    )
    mix = gamma[0]
    mixed = mix * unit + (4.0 - 2.0 * mix) * mine + (mix - 3.0) * square

    pair_mine, pair_other = gather_right_pair(mixed)
    left = gather_left(square)
    total = product(left, pair_mine + pair_other, picks, flags)
    total = total + send(total, always, dcore=1)
    swapped = send(total, source_b, dlayer=1)
    return jnp.where(core == part, total, swapped)


def solution(mesh):
    placed = (P(("layer", "row", "col"), None, None), P("row", None), P(), P(), P())
    return jax.shard_map(
        body, mesh=mesh, in_specs=placed, out_specs=P("row", None, "col"), check_vma=False
    )
```

time: 783 us -> 273 us (0.35)
  matrix products: 214 us -> 0 us
  waiting for transfers between devices: 264 us -> 122 us
  local copies, waits for them, and re-layouts: 154 us -> 16.8 us
  other arithmetic: 59.4 us -> 15.4 us
  Pallas kernels: 0 us -> 35.4 us
  between operations: 14.7 us -> 1.44 us
  starting transfers between devices: 69.5 us -> 80.5 us
    dot_general x16 -> x0, matrix products: 214 us -> none  [the longest x8 117 us: panel_product(): jnp.einsum('ikdlc,iklm->ikdmc', picked, match, precision=lax.Precision.HI...]
    reshape x20 -> x1, local copies, waits for them, and re-layouts: 105 us -> 0.09 us  [pick_table(): cols = block_cols.reshape(N_GROUP, rows, N_GROUP, span)]
    psum x2 -> x0, waiting for transfers between devices: 102 us -> none  [the longest x1 52.8 us: body(): return lax.psum(total, 'layer')]
    select_n x27 -> x4, other arithmetic: 56.2 us -> 2.74 us  [the longest x1 1.5 us: body(): mine = jnp.where(core == part, density, across)]
    ppermute x24 -> x35, waiting for transfers between devices: 139 us -> 97.9 us  [send(): return lax.ppermute(x, AXES, moves(target))]
    pallas_call x0 -> x2, Pallas kernels: none -> 35.4 us  [product(): pl.pallas_call(functools.partial(product_kernel, pair, rows, width, span)...]
    gather x12 -> x0, local copies, waits for them, and re-layouts: 28.2 us -> none  [the longest x8 25.8 us: panel_product(): jnp.take(right, flat_cols, axis=0).reshape(rows, span, width, span, width)]
    add x4 -> x2, local copies, waits for them, and re-layouts: 11.6 us -> 0.4 us  [pick_table(): picked = none + jnp.sum(jnp.where(match, entry - none, 0), axis=3)]
  transfers between devices with their start and end apart: 27 -> 36, of which waited for: 13 -> 17; matrix products, arithmetic and copies ran while one was open for 48% -> 6% of each run, Pallas kernels for 0% -> 0%
where the time goes in v1:
time: 273 us; the launch traced here: 271 us
  waiting for transfers between devices  122 us (45%)
  starting transfers between devices  80.5 us (29%)
  Pallas kernels  35.4 us (13%)
  local copies, waits for them, and re-layouts  16.8 us (6%)
  other arithmetic  15.4 us (6%)
    ppermute x35, waiting for transfers between devices, send(): return lax.ppermute(x, AXES, moves(target))  97.9 us
    ppermute x35, starting transfers between devices, send(): return lax.ppermute(x, AXES, moves(target))  72 us
    pallas_call x2, Pallas kernels, product(): pl.pallas_call(functools.partial(product_kernel, pair, rows, width, span)...  35.4 us
    all_to_all x1, waiting for transfers between devices, body(): lax.all_to_all(plain_send, ('layer', 'col'), split_axis=0, concat_axis=0,...  23.8 us
    all_to_all x1, starting transfers between devices, body(): lax.all_to_all(plain_send, ('layer', 'col'), split_axis=0, concat_axis=0,...  8.56 us
    unnamed x41, local copies, waits for them, and re-layouts  6.57 us
    reduce_sum x1, other arithmetic, pick_table(): found = jnp.sum(hit[..., None] * right_cols[None, :, None], axis=3)  5.6 us
  transfers between devices with their start and end apart: 36, of which 17 were waited for; matrix products, arithmetic and copies ran while one was open for 6% of the time, Pallas kernels for 0%

profile of v1, /device:TPU:1, one launch (start us, length us, event | category | flops | bytes accessed | tf_op | source)
XLA Modules:
  0.0 271.3 jit_solution(7884874793320722503)
XLA Ops:
  3.6 8.6 %all-to-all-start = ((f32[32,64,256]{2,1,0:T(8,128)}), f32[32,64,256]{2,1,0:T(8,128)S(1)}, u32[]{:S(2)}, u32[]{:S(2)}) async-start(f32[32,64,256]{2,1,0:T(8,128)} %bitcast.10), calls=%async_computation | async-start | bytes 4194304 | tf_op jit(solution)/shard_map/all_to_all | solution.py:281
  14.0 23.8 %all-to-all-done = f32[32,64,256]{2,1,0:T(8,128)S(1)} async-done(((f32[32,64,256]{2,1,0:T(8,128)}), f32[32,64,256]{2,1,0:T(8,128)S(1)}, u32[]{:S(2)}, u32[]{:S(2)}) %all-to-all-start) | async-done | bytes 2097184 | tf_op jit(solution)/shard_map/all_to_all | solution.py:281
  39.7 2.8 %collective-permute-start = (f32[20,64,256]{2,1,0:T(8,128)}, f32[20,64,256]{2,1,0:T(8,128)}, u32[]{:S(2)}, u32[]{:S(2)}) collective-permute-start(f32[20,64,256]{2,1,0:T(8,128)} %broadcast_select_fusion.refs_10_), channel_id=1, source_target_pairs={{0,8},{1,9},{2,10},{3,11},{4,12},{5,13},{6,14},{7,15},{8,0},{9,1},... | collective-permute-start | bytes 3932168 | tf_op jit(solution)/shard_map/ppermute | solution.py:53
  52.3 5.6 %multiply_reduce_fusion = s32[20,4,4,4]{3,2,1,0:T(4,128)S(1)} fusion(s32[4,20,4]{1,2,0:T(4,128)S(1)} %multiply_reduce_fusion.2, s32[20,4,4,20]{3,2,1,0:T(4,128)S(1)} %fusion), kind=kLoop, calls=%fused_computation.7 | loop fusion | flops 49920 | bytes 32000 | tf_op jit(solution)/shard_map/reduce_sum | solution.py:248
  58.1 16.5 %collective-permute-done.11.refs_14_ = f32[20,64,256]{2,1,0:T(8,128)} collective-permute-done((f32[20,64,256]{2,1,0:T(8,128)}, f32[20,64,256]{2,1,0:T(8,128)}, u32[]{:S(2)}, u32[]{:S(2)}) %collective-permute-start.11) | collective-permute-done | bytes 1310752 | tf_op jit(solution)/shard_map/ppermute | solution.py:53
  77.0 4.1 %collective-permute-start.4 = (f32[10,64,256]{2,1,0:T(8,128)S(1)}, f32[10,64,256]{2,1,0:T(8,128)S(1)}, u32[]{:S(2)}, u32[]{:S(2)}) collective-permute-start(f32[10,64,256]{2,1,0:T(8,128)S(1)} %slice.39), channel_id=1, source_target_pairs={{1,0},{3,2},{5,4},{7,6},{8,11},{10,9},{12,15},{14,13},{17,16},{19,... | collective-permute-start | bytes 1966088 | tf_op jit(solution)/shard_map/ppermute | solution.py:53
  88.4 4.2 %collective-permute-done.12.refs_12_ = f32[10,64,256]{2,1,0:T(8,128)S(1)} collective-permute-done((f32[10,64,256]{2,1,0:T(8,128)S(1)}, f32[10,64,256]{2,1,0:T(8,128)S(1)}, u32[]{:S(2)}, u32[]{:S(2)}) %collective-permute-start.12) | collective-permute-done | bytes 655392 | tf_op jit(solution)/shard_map/ppermute | solution.py:53
  95.7 11.8 %collective-permute-done.13.refs_13_ = f32[10,64,256]{2,1,0:T(8,128)S(1)} collective-permute-done((f32[10,64,256]{2,1,0:T(8,128)}, f32[10,64,256]{2,1,0:T(8,128)S(1)}, u32[]{:S(2)}, u32[]{:S(2)}) %collective-permute-start.13) | collective-permute-done | bytes 655392 | tf_op jit(solution)/shard_map/ppermute | solution.py:53
  111.3 17.1 %shard_map.55 = f32[20,64,256]{2,1,0:T(8,128)S(1)} custom-call(s32[1280]{0:T(1024)S(1)} %add.228.pick_ref, s32[2]{0:T(128)S(1)} %add_convert_fusion.flag_ref, f32[20,64,256]{2,1,0:T(8,128)} %copy-done.5, f32[20,64,256]{2,1,0:T(8,128)} %collective-permute-done.1.refs_1_, f32[10,64,256]{2,1,0:T(8,128)S(1)} %collective-permute-done.2.refs_2_, ...), custom_call_target="tpu_custom_call" | custom-call | flops 1000000000 | bytes 12000000 | tf_op jit(solution)/shard_map/pallas_call | solution.py:210
  128.5 8.3 %collective-permute-start.14 = (f32[20,64,256]{2,1,0:T(8,128)S(1)}, f32[20,64,256]{2,1,0:T(8,128)}, u32[]{:S(2)}, u32[]{:S(2)}) collective-permute-start(f32[20,64,256]{2,1,0:T(8,128)S(1)} %shard_map.55), channel_id=1, source_target_pairs={{0,8},{1,9},{2,10},{3,11},{4,12},{5,13},{6,14},{7,15},{8,0},{9,1},... | collective-permute-start | bytes 3932168 | tf_op jit(solution)/shard_map/ppermute | solution.py:53
  149.1 13.1 %collective-permute-done.17.refs_4_ = f32[20,64,256]{2,1,0:T(8,128)S(1)} collective-permute-done((f32[20,64,256]{2,1,0:T(8,128)S(1)}, f32[20,64,256]{2,1,0:T(8,128)S(1)}, u32[]{:S(2)}, u32[]{:S(2)}) %collective-permute-start.17) | collective-permute-done | bytes 1310752 | tf_op jit(solution)/shard_map/ppermute | solution.py:53
  162.9 2.4 collective-permute-done.28.refs_15_
  165.3 3.7 %collective-permute-start.18 = (f32[10,64,256]{2,1,0:T(8,128)S(1)}, f32[10,64,256]{2,1,0:T(8,128)S(1)}, u32[]{:S(2)}, u32[]{:S(2)}) collective-permute-start(f32[10,64,256]{2,1,0:T(8,128)S(1)} %slice.43), channel_id=1, source_target_pairs={{1,0},{3,2},{5,4},{7,6},{8,11},{10,9},{12,15},{14,13},{17,16},{19,... | collective-permute-start | bytes 1966088 | tf_op jit(solution)/shard_map/ppermute | solution.py:53
  170.9 4.6 %collective-permute-start.29 = (f32[20,64,256]{2,1,0:T(8,128)S(1)}, f32[20,64,256]{2,1,0:T(8,128)S(1)}, u32[]{:S(2)}, u32[]{:S(2)}) collective-permute-start(f32[20,64,256]{2,1,0:T(8,128)S(1)} %collective-permute-done.28.refs_15_), channel_id=1, source_target_pairs={{4,52},{5,53},{6,54},{7,55},{8,56},{9,57},{10,58},{11,59},{20,4},{... | collective-permute-start | bytes 3932168 | tf_op jit(solution)/shard_map/ppermute | solution.py:53
  176.9 4.1 %collective-permute-start.16 = (f32[10,64,256]{2,1,0:T(8,128)S(1)}, f32[10,64,256]{2,1,0:T(8,128)S(1)}, u32[]{:S(2)}, u32[]{:S(2)}) collective-permute-start(f32[10,64,256]{2,1,0:T(8,128)S(1)} %slice.42), channel_id=1, source_target_pairs={{1,2},{3,0},{5,6},{7,4},{8,9},{10,11},{12,13},{14,15},{17,18},{19,... | collective-permute-start | bytes 1966088 | tf_op jit(solution)/shard_map/ppermute | solution.py:53
  182.3 6.2 %collective-permute-done.16.refs_2_ = f32[10,64,256]{2,1,0:T(8,128)S(1)} collective-permute-done((f32[10,64,256]{2,1,0:T(8,128)S(1)}, f32[10,64,256]{2,1,0:T(8,128)S(1)}, u32[]{:S(2)}, u32[]{:S(2)}) %collective-permute-start.16) | collective-permute-done | bytes 655392 | tf_op jit(solution)/shard_map/ppermute | solution.py:53
  189.8 2.4 collective-permute-done.32.refs_19_
  194.4 3.8 %collective-permute-done.23.refs_9_ = f32[20,64,256]{2,1,0:T(8,128)S(1)} collective-permute-done((f32[20,64,256]{2,1,0:T(8,128)S(1)}, f32[20,64,256]{2,1,0:T(8,128)S(1)}, u32[]{:S(2)}, u32[]{:S(2)}) %collective-permute-start.23) | collective-permute-done | bytes 1310752 | tf_op jit(solution)/shard_map/ppermute | solution.py:53
  198.9 8.7 %collective-permute-done.20.refs_6_ = f32[20,64,256]{2,1,0:T(8,128)S(1)} collective-permute-done((f32[20,64,256]{2,1,0:T(8,128)S(1)}, f32[20,64,256]{2,1,0:T(8,128)S(1)}, u32[]{:S(2)}, u32[]{:S(2)}) %collective-permute-start.20) | collective-permute-done | bytes 1310752 | tf_op jit(solution)/shard_map/ppermute | solution.py:53
  208.2 7.3 %collective-permute-done.31.refs_18_ = f32[10,64,256]{2,1,0:T(8,128)S(1)} collective-permute-done((f32[10,64,256]{2,1,0:T(8,128)S(1)}, f32[10,64,256]{2,1,0:T(8,128)S(1)}, u32[]{:S(2)}, u32[]{:S(2)}) %collective-permute-start.31) | collective-permute-done | bytes 655392 | tf_op jit(solution)/shard_map/ppermute | solution.py:53
  215.6 18.2 %shard_map.56 = f32[20,64,256]{2,1,0:T(8,128)} custom-call(s32[1280]{0:T(1024)S(1)} %add.228.pick_ref, s32[2]{0:T(128)S(1)} %add_convert_fusion.flag_ref, f32[20,64,256]{2,1,0:T(8,128)} %copy-done.7, f32[20,64,256]{2,1,0:T(8,128)} %copy-done.12, f32[10,64,256]{2,1,0:T(8,128)S(1)} %collective-permute-done.16.refs_2_, ...), custom_call_target="tpu_custom_call" | custom-call | flops 1000000000 | bytes 12000000 | tf_op jit(solution)/shard_map/pallas_call | solution.py:210
  233.9 13.5 %collective-permute-start.33 = (f32[20,64,256]{2,1,0:T(8,128)}, f32[20,64,256]{2,1,0:T(8,128)S(1)}, u32[]{:S(2)}, u32[]{:S(2)}) collective-permute-start(f32[20,64,256]{2,1,0:T(8,128)} %shard_map.56), channel_id=1, source_target_pairs={{0,8},{1,9},{2,10},{3,11},{4,12},{5,13},{6,14},{7,15},{8,0},{9,1},... | collective-permute-start | bytes 3932168 | tf_op jit(solution)/shard_map/ppermute | solution.py:53
  247.4 2.9 %collective-permute-done.33 = f32[20,64,256]{2,1,0:T(8,128)S(1)} collective-permute-done((f32[20,64,256]{2,1,0:T(8,128)}, f32[20,64,256]{2,1,0:T(8,128)S(1)}, u32[]{:S(2)}, u32[]{:S(2)}) %collective-permute-start.33) | collective-permute-done | bytes 1310752 | tf_op jit(solution)/shard_map/ppermute | solution.py:53
  253.0 17.1 %collective-permute-done.34 = f32[20,64,256]{2,1,0:T(8,128)S(1)} collective-permute-done((f32[20,64,256]{2,1,0:T(8,128)S(1)}, f32[20,64,256]{2,1,0:T(8,128)S(1)}, u32[]{:S(2)}, u32[]{:S(2)}) %collective-permute-start.34) | collective-permute-done | bytes 1310752 | tf_op jit(solution)/shard_map/ppermute | solution.py:53
  (154 shorter events, 59.2 us)
Async XLA Ops:
  3.6 34.2 %all-to-all-start = ((f32[32,64,256]{2,1,0:T(8,128)}), f32[32,64,256]{2,1,0:T(8,128)S(1)}, u32[]{:S(2)}, u32[]{:S(2)}) async-start(f32[32,64,256]{2,1,0:T(8,128)} %bitcast.10), calls=%async_computation | async-start | bytes 4194304 | tf_op jit(solution)/shard_map/all_to_all | solution.py:281
  42.6 32.1 %collective-permute-start.11 = (f32[20,64,256]{2,1,0:T(8,128)}, f32[20,64,256]{2,1,0:T(8,128)}, u32[]{:S(2)}, u32[]{:S(2)}) collective-permute-start(f32[20,64,256]{2,1,0:T(8,128)} %broadcast_select_fusion.refs_10_), channel_id=1, source_target_pairs={{0,16},{1,17},{2,18},{3,19},{4,20},{5,21},{6,22},{7,23},{8,24},{9,... | collective-permute-start | bytes 3932168 | tf_op jit(solution)/shard_map/ppermute | solution.py:53
  43.9 41.1 %collective-permute-start.10 = (f32[20,64,256]{2,1,0:T(8,128)}, f32[20,64,256]{2,1,0:T(8,128)}, u32[]{:S(2)}, u32[]{:S(2)}) collective-permute-start(f32[20,64,256]{2,1,0:T(8,128)} %broadcast_select_fusion.refs_10_), channel_id=1, source_target_pairs={{0,48},{1,49},{2,50},{3,51},{4,52},{5,53},{6,54},{7,55},{8,56},{9,... | collective-permute-start | bytes 3932168 | tf_op jit(solution)/shard_map/ppermute | solution.py:53
  47.0 36.6 %collective-permute-start.5 = (f32[20,64,256]{2,1,0:T(8,128)S(1)}, f32[20,64,256]{2,1,0:T(8,128)}, u32[]{:S(2)}, u32[]{:S(2)}) collective-permute-start(f32[20,64,256]{2,1,0:T(8,128)S(1)} %broadcast_select_fusion.2.refs_0_), channel_id=1, source_target_pairs={{0,68},{2,70},{4,64},{6,66},{9,77},{11,79},{13,73},{15,75},{16,84}... | collective-permute-start | bytes 3932168 | tf_op jit(solution)/shard_map/ppermute | solution.py:53
  48.8 27.1 %collective-permute-start.3 = (f32[20,64,256]{2,1,0:T(8,128)S(1)}, f32[20,64,256]{2,1,0:T(8,128)S(1)}, u32[]{:S(2)}, u32[]{:S(2)}) collective-permute-start(f32[20,64,256]{2,1,0:T(8,128)S(1)} %broadcast_select_fusion.2.refs_0_), channel_id=1, source_target_pairs={{0,3},{2,1},{4,7},{6,5},{9,8},{11,10},{13,12},{15,14},{16,19},{18,... | collective-permute-start | bytes 3932168 | tf_op jit(solution)/shard_map/ppermute | solution.py:53
  50.1 31.1 %collective-permute-start.1 = (f32[20,64,256]{2,1,0:T(8,128)S(1)}, f32[20,64,256]{2,1,0:T(8,128)}, u32[]{:S(2)}, u32[]{:S(2)}) collective-permute-start(f32[20,64,256]{2,1,0:T(8,128)S(1)} %broadcast_select_fusion.2.refs_0_), channel_id=1, source_target_pairs={{0,1},{2,3},{4,5},{6,7},{9,10},{11,8},{13,14},{15,12},{16,17},{18,... | collective-permute-start | bytes 3932168 | tf_op jit(solution)/shard_map/ppermute | solution.py:53
  75.8 16.8 %collective-permute-start.12 = (f32[10,64,256]{2,1,0:T(8,128)S(1)}, f32[10,64,256]{2,1,0:T(8,128)S(1)}, u32[]{:S(2)}, u32[]{:S(2)}) collective-permute-start(f32[10,64,256]{2,1,0:T(8,128)S(1)} %slice.40), channel_id=1, source_target_pairs={{0,16},{1,17},{2,18},{3,19},{4,20},{5,21},{6,22},{7,23},{8,24},{9,... | collective-permute-start | bytes 1966088 | tf_op jit(solution)/shard_map/ppermute | solution.py:53
  83.7 24.7 %collective-permute-start.9 = (f32[20,64,256]{2,1,0:T(8,128)}, f32[20,64,256]{2,1,0:T(8,128)}, u32[]{:S(2)}, u32[]{:S(2)}) collective-permute-start(f32[20,64,256]{2,1,0:T(8,128)} %collective-permute-done.5.refs_5_), channel_id=1, source_target_pairs={{0,3},{2,1},{4,7},{6,5},{9,8},{11,10},{13,12},{15,14},{16,19},{18,... | collective-permute-start | bytes 3932168 | tf_op jit(solution)/shard_map/ppermute | solution.py:53
  85.0 23.4 %collective-permute-start.6 = (f32[20,64,256]{2,1,0:T(8,128)}, f32[20,64,256]{2,1,0:T(8,128)}, u32[]{:S(2)}, u32[]{:S(2)}) collective-permute-start(f32[20,64,256]{2,1,0:T(8,128)} %collective-permute-done.5.refs_5_), channel_id=1, source_target_pairs={{0,1},{2,3},{4,5},{6,7},{9,10},{11,8},{13,14},{15,12},{16,17},{18,... | collective-permute-start | bytes 3932168 | tf_op jit(solution)/shard_map/ppermute | solution.py:53
  143.5 18.6 %collective-permute-start.17 = (f32[20,64,256]{2,1,0:T(8,128)S(1)}, f32[20,64,256]{2,1,0:T(8,128)S(1)}, u32[]{:S(2)}, u32[]{:S(2)}) collective-permute-start(f32[20,64,256]{2,1,0:T(8,128)S(1)} %get-tuple-element.7.refs_0_), channel_id=1, source_target_pairs={{0,3},{2,1},{4,7},{6,5},{9,8},{11,10},{13,12},{15,14},{16,19},{18,... | collective-permute-start | bytes 3932168 | tf_op jit(solution)/shard_map/ppermute | solution.py:53
  144.8 20.5 %collective-permute-start.28 = (f32[20,64,256]{2,1,0:T(8,128)S(1)}, f32[20,64,256]{2,1,0:T(8,128)S(1)}, u32[]{:S(2)}, u32[]{:S(2)}) collective-permute-start(f32[20,64,256]{2,1,0:T(8,128)S(1)} %get-tuple-element.6.refs_10_), channel_id=1, source_target_pairs={{0,64},{1,65},{2,66},{3,67},{12,76},{13,77},{14,78},{15,79},{16,80... | collective-permute-start | bytes 3932168 | tf_op jit(solution)/shard_map/ppermute | solution.py:53
  146.1 22.8 %collective-permute-start.19 = (f32[20,64,256]{2,1,0:T(8,128)S(1)}, f32[20,64,256]{2,1,0:T(8,128)S(1)}, u32[]{:S(2)}, u32[]{:S(2)}) collective-permute-start(f32[20,64,256]{2,1,0:T(8,128)S(1)} %get-tuple-element.7.refs_0_), channel_id=1, source_target_pairs={{0,68},{2,70},{4,64},{6,66},{9,77},{11,79},{13,73},{15,75},{16,84}... | collective-permute-start | bytes 3932168 | tf_op jit(solution)/shard_map/ppermute | solution.py:53
  146.9 24.0 %collective-permute-start.15 = (f32[20,64,256]{2,1,0:T(8,128)S(1)}, f32[20,64,256]{2,1,0:T(8,128)S(1)}, u32[]{:S(2)}, u32[]{:S(2)}) collective-permute-start(f32[20,64,256]{2,1,0:T(8,128)S(1)} %get-tuple-element.7.refs_0_), channel_id=1, source_target_pairs={{0,1},{2,3},{4,5},{6,7},{9,10},{11,8},{13,14},{15,12},{16,17},{18,... | collective-permute-start | bytes 3932168 | tf_op jit(solution)/shard_map/ppermute | solution.py:53
  148.3 27.3 %collective-permute-start.26 = (f32[10,64,256]{2,1,0:T(8,128)S(1)}, f32[10,64,256]{2,1,0:T(8,128)S(1)}, u32[]{:S(2)}, u32[]{:S(2)}) collective-permute-start(f32[10,64,256]{2,1,0:T(8,128)S(1)} %slice.44), channel_id=1, source_target_pairs={{0,16},{1,17},{2,18},{3,19},{12,28},{13,29},{14,30},{15,31},{16,32... | collective-permute-start | bytes 1966088 | tf_op jit(solution)/shard_map/ppermute | solution.py:53
  169.0 23.2 %collective-permute-start.32 = (f32[20,64,256]{2,1,0:T(8,128)S(1)}, f32[20,64,256]{2,1,0:T(8,128)S(1)}, u32[]{:S(2)}, u32[]{:S(2)}) collective-permute-start(f32[20,64,256]{2,1,0:T(8,128)S(1)} %collective-permute-done.28.refs_15_), channel_id=1, source_target_pairs={{4,20},{5,21},{6,22},{7,23},{8,24},{9,25},{10,26},{11,27},{20,36},... | collective-permute-start | bytes 3932168 | tf_op jit(solution)/shard_map/ppermute | solution.py:53
  170.9 22.8 %collective-permute-start.29 = (f32[20,64,256]{2,1,0:T(8,128)S(1)}, f32[20,64,256]{2,1,0:T(8,128)S(1)}, u32[]{:S(2)}, u32[]{:S(2)}) collective-permute-start(f32[20,64,256]{2,1,0:T(8,128)S(1)} %collective-permute-done.28.refs_15_), channel_id=1, source_target_pairs={{4,52},{5,53},{6,54},{7,55},{8,56},{9,57},{10,58},{11,59},{20,4},{... | collective-permute-start | bytes 3932168 | tf_op jit(solution)/shard_map/ppermute | solution.py:53
  175.5 22.7 %collective-permute-start.23 = (f32[20,64,256]{2,1,0:T(8,128)S(1)}, f32[20,64,256]{2,1,0:T(8,128)S(1)}, u32[]{:S(2)}, u32[]{:S(2)}) collective-permute-start(f32[20,64,256]{2,1,0:T(8,128)S(1)} %collective-permute-done.19.refs_5_), channel_id=1, source_target_pairs={{0,3},{2,1},{4,7},{6,5},{9,8},{11,10},{13,12},{15,14},{16,19},{18,... | collective-permute-start | bytes 3932168 | tf_op jit(solution)/shard_map/ppermute | solution.py:53
  181.0 26.6 %collective-permute-start.20 = (f32[20,64,256]{2,1,0:T(8,128)S(1)}, f32[20,64,256]{2,1,0:T(8,128)S(1)}, u32[]{:S(2)}, u32[]{:S(2)}) collective-permute-start(f32[20,64,256]{2,1,0:T(8,128)S(1)} %collective-permute-done.19.refs_5_), channel_id=1, source_target_pairs={{0,1},{2,3},{4,5},{6,7},{9,10},{11,8},{13,14},{15,12},{16,17},{18,... | collective-permute-start | bytes 3932168 | tf_op jit(solution)/shard_map/ppermute | solution.py:53
  188.5 19.8 %collective-permute-start.30 = (f32[10,64,256]{2,1,0:T(8,128)S(1)}, f32[10,64,256]{2,1,0:T(8,128)S(1)}, u32[]{:S(2)}, u32[]{:S(2)}) collective-permute-start(f32[10,64,256]{2,1,0:T(8,128)S(1)} %collective-permute-done.26.refs_12_), channel_id=1, source_target_pairs={{0,64},{1,65},{2,66},{3,67},{12,76},{13,77},{14,78},{15,79},{16,80... | collective-permute-start | bytes 1966088 | tf_op jit(solution)/shard_map/ppermute | solution.py:53
  192.2 23.4 %collective-permute-start.31 = (f32[10,64,256]{2,1,0:T(8,128)S(1)}, f32[10,64,256]{2,1,0:T(8,128)S(1)}, u32[]{:S(2)}, u32[]{:S(2)}) collective-permute-start(f32[10,64,256]{2,1,0:T(8,128)S(1)} %collective-permute-done.27.refs_13_), channel_id=1, source_target_pairs={{0,64},{1,65},{2,66},{3,67},{12,76},{13,77},{14,78},{15,79},{16,80... | collective-permute-start | bytes 1966088 | tf_op jit(solution)/shard_map/ppermute | solution.py:53
  193.7 21.8 %collective-permute-start.22 = (f32[10,64,256]{2,1,0:T(8,128)S(1)}, f32[10,64,256]{2,1,0:T(8,128)S(1)}, u32[]{:S(2)}, u32[]{:S(2)}) collective-permute-start(f32[10,64,256]{2,1,0:T(8,128)S(1)} %collective-permute-done.18.refs_3_), channel_id=1, source_target_pairs={{0,68},{2,70},{4,64},{6,66},{9,77},{11,79},{13,73},{15,75},{16,84}... | collective-permute-start | bytes 1966088 | tf_op jit(solution)/shard_map/ppermute | solution.py:53
  198.2 17.3 %collective-permute-start.21 = (f32[10,64,256]{2,1,0:T(8,128)S(1)}, f32[10,64,256]{2,1,0:T(8,128)S(1)}, u32[]{:S(2)}, u32[]{:S(2)}) collective-permute-start(f32[10,64,256]{2,1,0:T(8,128)S(1)} %collective-permute-done.16.refs_2_), channel_id=1, source_target_pairs={{0,68},{2,70},{4,64},{6,66},{9,77},{11,79},{13,73},{15,75},{16,84}... | collective-permute-start | bytes 1966088 | tf_op jit(solution)/shard_map/ppermute | solution.py:53
  233.9 16.4 %collective-permute-start.33 = (f32[20,64,256]{2,1,0:T(8,128)}, f32[20,64,256]{2,1,0:T(8,128)S(1)}, u32[]{:S(2)}, u32[]{:S(2)}) collective-permute-start(f32[20,64,256]{2,1,0:T(8,128)} %shard_map.56), channel_id=1, source_target_pairs={{0,8},{1,9},{2,10},{3,11},{4,12},{5,13},{6,14},{7,15},{8,0},{9,1},... | collective-permute-start | bytes 3932168 | tf_op jit(solution)/shard_map/ppermute | solution.py:53
  251.7 18.4 %collective-permute-start.34 = (f32[20,64,256]{2,1,0:T(8,128)S(1)}, f32[20,64,256]{2,1,0:T(8,128)S(1)}, u32[]{:S(2)}, u32[]{:S(2)}) collective-permute-start(f32[20,64,256]{2,1,0:T(8,128)S(1)} %add.236), channel_id=1, source_target_pairs={{0,64},{1,65},{2,66},{3,67},{12,76},{13,77},{14,78},{15,79},{16,80... | collective-permute-start | bytes 3932168 | tf_op jit(solution)/shard_map/ppermute | solution.py:53
  (32 other events, 552.5 us)

commit v2 on v1

v2 whole, which is shorter than its diff:
```python
import functools

import jax
import jax.numpy as jnp
from jax import lax
from jax.experimental import pallas as pl
from jax.experimental.pallas import tpu as pltpu
from jax.sharding import PartitionSpec as P

AXES = ("layer", "row", "col")
N_LAYER, N_Y, N_CORE, N_Q, N_Z = 2, 4, 2, 2, 4
N_GROUP = 8
N_SLOT = 4
TABLE_STEP = 4
ROW_STEP = 4
VMEM_BYTES = 60 * 1024 * 1024


def moves(target):
    pairs = []
    for layer in range(N_LAYER):
        for y in range(N_Y):
            for core in range(N_CORE):
                for q in range(N_Q):
                    for z in range(N_Z):
                        there = target(layer, y, core, q, z)
                        if there is not None:
                            pairs.append((flat(layer, y, core, q, z), flat(*there)))
    return pairs


def flat(layer, y, core, q, z):
    row = (y % N_Y) * N_CORE + core % N_CORE
    return ((layer % N_LAYER) * N_Y * N_CORE + row) * N_Q * N_Z + (q % N_Q) * N_Z + z % N_Z


def home_right(layer, y, core, q, z):
    return ((layer ^ q) + y // 2) % 2


def home_left(layer, y, core, q, z):
    return (z + q) % 2


def send(x, target):
    return lax.ppermute(x, AXES, moves(target))


def step(x, dy=0, dz=0):
    return send(x, lambda layer, y, core, q, z: (layer, y + dy, core, q, z + dz))


def swap_cores(x):
    return send(x, lambda layer, y, core, q, z: (layer, y, 1 - core, q, z))


def after(x, *done):
    return lax.optimization_barrier((x, *done))[0]


def first_round(density):
    def right_own(layer, y, core, q, z):
        return layer, y, core + y // 2, q, z

    def left_own(layer, y, core, q, z):
        if core == layer ^ q:
            return layer, y, z + q, q, z
        return layer, y, z + q, 1 - q, z

    def right_across(layer, y, core, q, z):
        return (layer, y + 2, core + y // 2, q, z) if core == layer ^ q else None

    def left_across(layer, y, core, q, z):
        return (layer, y, z + q, q, z + 2) if core == layer ^ q else None

    return (
        send(density, right_across),
        send(density, left_own),
        send(density, left_across),
        send(density, right_own),
    )


def second_round(square, mixed):
    def right_own(layer, y, core, q, z):
        home = home_right(layer, y, core, q, z)
        return (1 - layer, y, core, q, z) if core == home else (layer, y, home, q, z)

    def left_own(layer, y, core, q, z):
        home = home_left(layer, y, core, q, z)
        return (1 - layer, y, core, 1 - q, z) if core == home else (layer, y, home, q, z)

    def right_across(layer, y, core, q, z):
        return (layer, y + 2, core, q, z) if core == home_right(layer, y, core, q, z) else None

    def left_across(layer, y, core, q, z):
        return (layer, y, core, q, z + 2) if core == home_left(layer, y, core, q, z) else None

    return (
        send(mixed, right_across),
        send(square, left_own),
        send(square, left_across),
        send(mixed, right_own),
    )


def gather(right_across, left_own, left_across, right_own):
    def right_pass(layer, y, core, q, z):
        return (1 - layer, y, core, q, z) if core != home_right(layer, y, core, q, z) else None

    def left_pass(layer, y, core, q, z):
        return (1 - layer, y, core, 1 - q, z) if core == home_left(layer, y, core, q, z) else None

    right_now = after(right_own, right_across)
    left_now = after(left_own, right_across, left_across)
    right_below = step(right_now, dy=1)
    right_above = step(right_now, dy=-1)
    left_below = step(left_now, dz=1)
    left_above = step(left_now, dz=-1)
    right_pair = send(right_across, right_pass)
    left_pair = send(after(left_across, right_pair), left_pass)
    left = (left_own, left_below, left_above, left_across, left_pair)
    right = (right_own, right_above, right_across, right_below, right_pair)
    return left, right


def product_kernel(rows, width, span, pick_ref, flag_ref, *refs):
    left, right = refs[:5], refs[5:10]
    out_ref, left_buf, right_buf, high, low, left_sem, right_sem = refs[10:]

    def bring(buf, sem, place, src):
        return pltpu.make_async_copy(src, buf.at[place], sem.at[place])

    for place in (0, 1, 3):
        bring(right_buf, right_sem, place, right[place]).start()

    @pl.when(flag_ref[1] == 1)
    def _():
        bring(right_buf, right_sem, 2, right[2]).start()

    @pl.when(flag_ref[1] == 0)
    def _():
        bring(right_buf, right_sem, 2, right[4]).start()

    for place in (0, 1, 2):
        bring(left_buf, left_sem, place, left[place]).start()

    @pl.when(flag_ref[0] == 1)
    def _():
        bring(left_buf, left_sem, 3, left[3]).start()

    @pl.when(flag_ref[0] == 0)
    def _():
        bring(left_buf, left_sem, 3, left[4]).start()

    none = 4 * rows * span
    high[none] = jnp.zeros(high.shape[1:], high.dtype)
    low[none] = jnp.zeros(low.shape[1:], low.dtype)

    for place in range(4):
        bring(right_buf, right_sem, place, right[place]).wait()

        @pl.loop(0, rows // TABLE_STEP)
        def _(step):
            for j in range(TABLE_STEP):
                row = step * TABLE_STEP + j
                at = (place * rows + row) * span
                x = right_buf[place, row]
                for v in range(2):
                    piece = x[:, v * 2 * width : (v + 1) * 2 * width]
                    top = piece.astype(jnp.bfloat16).astype(jnp.float32)
                    rest = piece - top
                    high[at + 2 * v] = top.astype(jnp.bfloat16)
                    low[at + 2 * v] = rest.astype(jnp.bfloat16)
                    high[at + 2 * v + 1] = pltpu.roll(top, width, 1).astype(jnp.bfloat16)
                    low[at + 2 * v + 1] = pltpu.roll(rest, width, 1).astype(jnp.bfloat16)

    for place in range(4):
        bring(left_buf, left_sem, place, left[0]).wait()

    lane = lax.broadcasted_iota(jnp.int32, (width, 2 * width), 1) < width

    def one_row(row):
        both = jnp.zeros((2 * width, span * width), jnp.float32)
        single = jnp.zeros((width, span * width), jnp.float32)
        for place in range(4):
            top_rows, low_rows = [], []
            for k in range(span):
                at = ((row * 4 + place) * span + k) * span
                picks = [pick_ref[at + m] for m in range(span)]
                for table, rows_of in ((high, top_rows), (low, low_rows)):
                    rows_of.append(
                        jnp.concatenate(
                            [
                                jnp.where(lane, table[picks[0]], table[picks[1]]),
                                jnp.where(lane, table[picks[2]], table[picks[3]]),
                            ],
                            axis=1,
                        )
                    )
            x = left_buf[place, row]
            top = x.astype(jnp.bfloat16)
            rest = (x - top.astype(jnp.float32)).astype(jnp.bfloat16)
            both += jnp.dot(
                jnp.concatenate([top, rest], axis=0),
                jnp.concatenate(top_rows, axis=0),
                preferred_element_type=jnp.float32,
            )
            single += jnp.dot(
                top, jnp.concatenate(low_rows, axis=0), preferred_element_type=jnp.float32
            )
        out_ref[row] = both[:width] + both[width:] + single

    @pl.loop(0, rows // ROW_STEP)
    def _(step):
        for j in range(ROW_STEP):
            one_row(step * ROW_STEP + j)


def product(left, right, picks, flags):
    rows, width, wide = left[0].shape
    span = wide // width
    table = pltpu.VMEM((4 * rows * span + 1, width, 2 * width), jnp.bfloat16)
    return pl.pallas_call(
        functools.partial(product_kernel, rows, width, span),
        out_shape=jax.ShapeDtypeStruct((rows, width, wide), jnp.float32),
        in_specs=[pl.BlockSpec(memory_space=pltpu.SMEM)] * 2
        + [pl.BlockSpec(memory_space=pl.ANY)] * (len(left) + len(right)),
        out_specs=pl.BlockSpec(memory_space=pltpu.VMEM),
        scratch_shapes=[
            pltpu.VMEM((4, rows, width, wide), jnp.float32),
            pltpu.VMEM((4, rows, width, wide), jnp.float32),
            table,
            table,
            pltpu.SemaphoreType.DMA((4,)),
            pltpu.SemaphoreType.DMA((4,)),
        ],
        compiler_params=pltpu.CompilerParams(vmem_limit_bytes=VMEM_BYTES),
        cost_estimate=pl.CostEstimate(flops=10**9, bytes_accessed=12 * 10**6, transcendentals=0),
    )(picks, flags, *left, *right)


def pick_table(block_cols, out_cols, grid_row, grid_col, core, y, z, rows, span):
    cols = block_cols.reshape(N_GROUP, rows, N_GROUP, span)
    left_cols = lax.dynamic_slice(block_cols, (grid_row * rows, 0), (rows, N_GROUP * span))
    left_cols = left_cols.reshape(rows, N_GROUP, span)
    z_from = (z + jnp.array([0, 3, 1, 2], dtype=jnp.int32)) % N_Z
    groups = (core + z_from) % 2 * N_Z + z_from
    names = jnp.arange(N_GROUP, dtype=jnp.int32)
    chosen = (groups[:, None] == names[None, :]).astype(jnp.int32)
    local = left_cols - names[None, :, None] * rows
    slots = jnp.sum(local[:, None] * chosen[None, :, :, None], axis=2)
    right_cols = jnp.sum(
        cols * (names == grid_col).astype(jnp.int32)[None, None, :, None], axis=2
    )
    right_cols = jnp.sum(right_cols[None] * chosen[:, :, None, None], axis=1)
    hit = (slots[..., None] == jnp.arange(rows, dtype=jnp.int32)).astype(jnp.int32)
    found = jnp.sum(hit[..., None] * right_cols[None, :, None], axis=3)
    place = (groups // 2 - y) % N_Y
    base = ((place[None, :, None] * rows + slots) * 2)[..., None]
    match = found[..., :, None] == out_cols[:, None, None, None, :]
    piece = jnp.arange(span, dtype=jnp.int32)
    swap = (piece[:, None] + piece[None, :]) % 2
    entry = (base[..., None] + (piece // 2)[:, None]) * 2 + swap
    none = 4 * rows * span
    picked = none + jnp.sum(jnp.where(match, entry - none, 0), axis=3)
    return picked.reshape(-1).astype(jnp.int32)


def body(owner_blocks, owner_counts, block_cols, filter_mask, gamma):
    layer = lax.axis_index("layer")
    grid_row = lax.axis_index("row")
    grid_col = lax.axis_index("col")
    y, core = grid_row // N_CORE, grid_row % N_CORE
    q, z = grid_col // N_Z, grid_col % N_Z
    part = (layer + q) % 2
    cap, width, _ = owner_blocks.shape
    span = N_SLOT
    rows = block_cols.shape[0] // N_GROUP

    counts = owner_counts[0]
    ends = jnp.cumsum(counts)
    local = jnp.arange(rows, dtype=jnp.int32)
    which = jnp.sum((ends[None, :] <= local[:, None]).astype(jnp.int32), axis=1)
    slot = local - (jnp.take(ends, which) - jnp.take(counts, which))
    source = which * cap + slot
    grouped = owner_blocks.reshape(cap, width, N_GROUP, span * width).transpose(2, 0, 1, 3)
    plain_send = jnp.tile(grouped, (N_LAYER, 1, 1, 1)).reshape(
        N_LAYER * N_GROUP * cap, width, span * width
    )
    plain_got = lax.all_to_all(
        plain_send, ("layer", "col"), split_axis=0, concat_axis=0, tiled=True
    )
    row_here = 2 * y + part
    out_cols = lax.dynamic_slice(block_cols, (row_here * rows, grid_col * span), (rows, span))
    keep = lax.dynamic_slice(filter_mask, (row_here * rows, grid_col * span), (rows, span))
    picks = pick_table(block_cols, out_cols, row_here, grid_col, core, y, z, rows, span)
    flags = jnp.stack([core == (z + q) % 2, core != (part + y // 2) % 2]).astype(jnp.int32)

    plain_got, picks, flags = lax.optimization_barrier((plain_got, picks, flags))
    density = jnp.take(plain_got, source, axis=0)

    left, right = gather(*first_round(density))
    mine = jnp.where(core == part, density, swap_cores(after(density, left[4])))
    partial_value = product(left, right, picks, flags)
    square = partial_value + swap_cores(partial_value)
    keep_wide = jnp.repeat(keep.astype(jnp.float32), width, axis=1)[:, None, :]
    square = square * keep_wide
    own = (out_cols == (row_here * rows + local)[:, None]).astype(jnp.float32)
    unit = (own[:, None, :, None] * jnp.eye(width, dtype=jnp.float32)[None, :, None, :]).reshape(
        rows, width, span * width
    )
    mix = gamma[0]
    mixed = mix * unit + (4.0 - 2.0 * mix) * mine + (mix - 3.0) * square

    left, right = gather(*second_round(square, mixed))
    total = product(left, right, picks, flags)
    total = total + swap_cores(total)

    def output(layer, y, core, q, z):
        return (1 - layer, y, core, q, z) if core == layer ^ q else None

    swapped = send(total, output)
    return jnp.where(core == part, total, swapped)


def solution(mesh):
    placed = (P(("layer", "row", "col"), None, None), P("row", None), P(), P(), P())
    return jax.shard_map(
        body, mesh=mesh, in_specs=placed, out_specs=P("row", None, "col"), check_vma=False
    )
```

time: 273 us -> 224 us (0.82)
  starting transfers between devices: 80.5 us -> 51.6 us
  Pallas kernels: 35.4 us -> 27.2 us
  local copies, waits for them, and re-layouts: 16.8 us -> 10.7 us
  waiting for transfers between devices: 122 us -> 118 us
    ppermute x35 -> x24, starting transfers between devices: 72 us -> 43.1 us  [send(): return lax.ppermute(x, AXES, moves(target))]
    all_to_all x1, waiting for transfers between devices: 23.8 us -> 14.8 us  [body(): lax.all_to_all(plain_send, ('layer', 'col'), split_axis=0, concat_axis=0,...]
    pallas_call x2, Pallas kernels: 35.4 us -> 27.2 us  [product(): pl.pallas_call(functools.partial(product_kernel, rows, width, span), out_...]
    ppermute x35 -> x24, waiting for transfers between devices: 97.9 us -> 104 us  [send(): return lax.ppermute(x, AXES, moves(target))]
    slice x8 -> x0, local copies, waits for them, and re-layouts: 4.46 us -> none  [the longest x2 2.01 us: gather_right(): second = send(above[HALF:], who, dy=-1)]
    unnamed x41 -> x47, local copies, waits for them, and re-layouts: 6.57 us -> 4.39 us
  transfers between devices with their start and end apart: 36 -> 25, of which waited for: 17 -> 16; matrix products, arithmetic and copies ran while one was open for 6% -> 5% of each run, Pallas kernels for 0% -> 0%
where the time goes in v2:
time: 224 us; the launch traced here: 223 us
  waiting for transfers between devices  118 us (53%)
  starting transfers between devices  51.6 us (23%)
  Pallas kernels  27.2 us (12%)
  other arithmetic  13.9 us (6%)
  local copies, waits for them, and re-layouts  10.7 us (5%)
    ppermute x24, waiting for transfers between devices, send(): return lax.ppermute(x, AXES, moves(target))  104 us
    ppermute x24, starting transfers between devices, send(): return lax.ppermute(x, AXES, moves(target))  43.1 us
    pallas_call x2, Pallas kernels, product(): pl.pallas_call(functools.partial(product_kernel, rows, width, span), out_...  27.2 us
    all_to_all x1, waiting for transfers between devices, body(): lax.all_to_all(plain_send, ('layer', 'col'), split_axis=0, concat_axis=0,...  14.8 us
    all_to_all x1, starting transfers between devices, body(): lax.all_to_all(plain_send, ('layer', 'col'), split_axis=0, concat_axis=0,...  8.56 us
    reduce_sum x1, other arithmetic, pick_table(): found = jnp.sum(hit[..., None] * right_cols[None, :, None], axis=3)  5.6 us
  transfers between devices with their start and end apart: 25, of which 16 were waited for; matrix products, arithmetic and copies ran while one was open for 5% of the time, Pallas kernels for 0%

profile of v2, /device:TPU:1, one launch (start us, length us, event | category | flops | bytes accessed | tf_op | source)
XLA Modules:
  0.0 223.1 jit_solution(5062482413324409179)
XLA Ops:
  3.6 8.6 %all-to-all-start = ((f32[32,64,256]{2,1,0:T(8,128)}), f32[32,64,256]{2,1,0:T(8,128)S(1)}, u32[]{:S(2)}, u32[]{:S(2)}) async-start(f32[32,64,256]{2,1,0:T(8,128)} %bitcast.1), calls=%async_computation | async-start | bytes 4194304 | tf_op jit(solution)/shard_map/all_to_all | solution.py:291
  13.3 5.6 %multiply_reduce_fusion = s32[20,4,4,4]{3,2,1,0:T(4,128)S(1)} fusion(s32[4,20,4]{1,2,0:T(4,128)S(1)} %multiply_reduce_fusion.2, s32[20,4,4,20]{3,2,1,0:T(4,128)S(1)} %fusion), kind=kLoop, calls=%fused_computation.7 | loop fusion | flops 49920 | bytes 32000 | tf_op jit(solution)/shard_map/reduce_sum | solution.py:258
  23.0 14.8 %all-to-all-done = f32[32,64,256]{2,1,0:T(8,128)S(1)} async-done(((f32[32,64,256]{2,1,0:T(8,128)}), f32[32,64,256]{2,1,0:T(8,128)S(1)}, u32[]{:S(2)}, u32[]{:S(2)}) %all-to-all-start) | async-done | bytes 2097184 | tf_op jit(solution)/shard_map/all_to_all | solution.py:291
  40.6 7.4 %collective-permute-start = (f32[20,64,256]{2,1,0:T(8,128)S(1)}, f32[20,64,256]{2,1,0:T(8,128)S(1)}, u32[]{:S(2)}, u32[]{:S(2)}) collective-permute-start(f32[20,64,256]{2,1,0:T(8,128)S(1)} %broadcast_select_fusion), channel_id=1, source_target_pairs={{0,0},{1,9},{2,2},{3,11},{4,8},{5,1},{6,10},{7,3},{8,4},{9,13},{10... | collective-permute-start | bytes 3932168 | tf_op jit(solution)/shard_map/ppermute | solution.py:46
  48.8 12.9 %collective-permute-done.1.refs_7_ = f32[20,64,256]{2,1,0:T(8,128)S(1)} collective-permute-done((f32[20,64,256]{2,1,0:T(8,128)S(1)}, f32[20,64,256]{2,1,0:T(8,128)S(1)}, u32[]{:S(2)}, u32[]{:S(2)}) %collective-permute-start.1) | collective-permute-done | bytes 1310752 | tf_op jit(solution)/shard_map/ppermute | solution.py:46
  63.2 4.6 %collective-permute-start.9 = (f32[20,64,256]{2,1,0:T(8,128)S(1)}, f32[20,64,256]{2,1,0:T(8,128)S(1)}, u32[]{:S(2)}, u32[]{:S(2)}) collective-permute-start(f32[20,64,256]{2,1,0:T(8,128)S(1)} %collective-permute-done.7.refs_5_), channel_id=1, source_target_pairs={{0,16},{1,17},{2,18},{3,19},{4,20},{5,21},{6,22},{7,23},{8,24},{9,... | collective-permute-start | bytes 3932168 | tf_op jit(solution)/shard_map/ppermute | solution.py:46
  69.7 2.1 collective-permute-start.4
  71.8 5.8 %collective-permute-done.5.refs_9_ = f32[20,64,256]{2,1,0:T(8,128)S(1)} collective-permute-done((f32[20,64,256]{2,1,0:T(8,128)S(1)}, f32[20,64,256]{2,1,0:T(8,128)S(1)}, u32[]{:S(2)}, u32[]{:S(2)}) %collective-permute-start.5) | collective-permute-done | bytes 1310752 | tf_op jit(solution)/shard_map/ppermute | solution.py:46
  78.8 15.4 %collective-permute-done.8.refs_6_ = f32[20,64,256]{2,1,0:T(8,128)S(1)} collective-permute-done((f32[20,64,256]{2,1,0:T(8,128)S(1)}, f32[20,64,256]{2,1,0:T(8,128)S(1)}, u32[]{:S(2)}, u32[]{:S(2)}) %collective-permute-start.8) | collective-permute-done | bytes 1310752 | tf_op jit(solution)/shard_map/ppermute | solution.py:46
  95.9 4.6 %collective-permute-done.3.refs_1_ = f32[20,64,256]{2,1,0:T(8,128)S(1)} collective-permute-done((f32[20,64,256]{2,1,0:T(8,128)S(1)}, f32[20,64,256]{2,1,0:T(8,128)S(1)}, u32[]{:S(2)}, u32[]{:S(2)}) %collective-permute-start.3) | collective-permute-done | bytes 1310752 | tf_op jit(solution)/shard_map/ppermute | solution.py:46
  102.7 13.6 %shard_map.64 = f32[20,64,256]{2,1,0:T(8,128)} custom-call(s32[1280]{0:T(1024)} %add.218.pick_ref, s32[2]{0:T(128)} %add_convert_fusion.flag_ref, f32[20,64,256]{2,1,0:T(8,128)} %copy-done.9, f32[20,64,256]{2,1,0:T(8,128)} %copy-done.18, f32[20,64,256]{2,1,0:T(8,128)} %copy-done.20, f32[20,64,256]{2,1,0:T(8,128)} %copy-done.10, ...), custom_call_target="tpu_custom_call" | custom-call | flops 1000000000 | bytes 12000000 | tf_op jit(solution)/shard_map/pallas_call | solution.py:224
  122.5 2.7 %multiply_add_fusion = (f32[20,64,256]{2,1,0:T(8,128)S(1)}, f32[20,64,256]{2,1,0:T(8,128)S(1)}) fusion(f32[20,64,256]{2,1,0:T(8,128)} %collective-permute-done.12, f32[]{:T(128)S(6)} %sub.64, f32[]{:T(128)S(6)} %sub.63, f32[64,256]{1,0:T(8,128)S(1)} %mul.179, f32[20,256]{1,0:T(8,128)S(1)} %mul.176, f32[]{:T(128)} %bitcast.17, pred[]{:T(512)S(6)} %eq.95, ...), kind=kLoop, calls=%fused_computation.3 | loop fusion | flops 3276800 | bytes 7970849 | tf_op jit(solution)/shard_map/add | solution.py:314
  126.5 2.1 collective-permute-start.19
  129.3 3.7 %collective-permute-start.11 = (f32[20,64,256]{2,1,0:T(8,128)S(1)}, f32[20,64,256]{2,1,0:T(8,128)S(1)}, u32[]{:S(2)}, u32[]{:S(2)}) collective-permute-start(f32[20,64,256]{2,1,0:T(8,128)S(1)} %get-tuple-element.27), channel_id=1, source_target_pairs={{0,68},{1,9},{2,70},{3,11},{4,12},{5,65},{6,14},{7,67},{8,0},{9,77... | collective-permute-start | bytes 3932168 | tf_op jit(solution)/shard_map/ppermute | solution.py:46
  133.0 12.3 %collective-permute-done.13.refs_7_ = f32[20,64,256]{2,1,0:T(8,128)S(1)} collective-permute-done((f32[20,64,256]{2,1,0:T(8,128)S(1)}, f32[20,64,256]{2,1,0:T(8,128)S(1)}, u32[]{:S(2)}, u32[]{:S(2)}) %collective-permute-start.13) | collective-permute-done | bytes 1310752 | tf_op jit(solution)/shard_map/ppermute | solution.py:46
  146.7 3.0 %collective-permute-start.20 = (f32[20,64,256]{2,1,0:T(8,128)S(1)}, f32[20,64,256]{2,1,0:T(8,128)S(1)}, u32[]{:S(2)}, u32[]{:S(2)}) collective-permute-start(f32[20,64,256]{2,1,0:T(8,128)S(1)} %collective-permute-done.19.refs_5_), channel_id=1, source_target_pairs={{0,48},{1,49},{2,50},{3,51},{4,52},{5,53},{6,54},{7,55},{8,56},{9,... | collective-permute-start | bytes 3932168 | tf_op jit(solution)/shard_map/ppermute | solution.py:46
  151.3 2.9 %collective-permute-start.16 = (f32[20,64,256]{2,1,0:T(8,128)S(1)}, f32[20,64,256]{2,1,0:T(8,128)S(1)}, u32[]{:S(2)}, u32[]{:S(2)}) collective-permute-start(f32[20,64,256]{2,1,0:T(8,128)S(1)} %collective-permute-done.11.refs_0_), channel_id=1, source_target_pairs={{0,3},{1,0},{2,1},{3,2},{4,7},{5,4},{6,5},{7,6},{8,11},{9,8},{10,9... | collective-permute-start | bytes 3932168 | tf_op jit(solution)/shard_map/ppermute | solution.py:46
  154.1 7.0 %collective-permute-done.17.refs_9_ = f32[20,64,256]{2,1,0:T(8,128)S(1)} collective-permute-done((f32[20,64,256]{2,1,0:T(8,128)S(1)}, f32[20,64,256]{2,1,0:T(8,128)S(1)}, u32[]{:S(2)}, u32[]{:S(2)}) %collective-permute-start.17) | collective-permute-done | bytes 1310752 | tf_op jit(solution)/shard_map/ppermute | solution.py:46
  162.4 14.6 %collective-permute-done.20.refs_6_ = f32[20,64,256]{2,1,0:T(8,128)S(1)} collective-permute-done((f32[20,64,256]{2,1,0:T(8,128)S(1)}, f32[20,64,256]{2,1,0:T(8,128)S(1)}, u32[]{:S(2)}, u32[]{:S(2)}) %collective-permute-start.20) | collective-permute-done | bytes 1310752 | tf_op jit(solution)/shard_map/ppermute | solution.py:46
  177.0 3.1 %collective-permute-done.21.refs_8_ = f32[20,64,256]{2,1,0:T(8,128)S(1)} collective-permute-done((f32[20,64,256]{2,1,0:T(8,128)S(1)}, f32[20,64,256]{2,1,0:T(8,128)S(1)}, u32[]{:S(2)}, u32[]{:S(2)}) %collective-permute-start.21) | collective-permute-done | bytes 1310752 | tf_op jit(solution)/shard_map/ppermute | solution.py:46
  180.1 3.1 %collective-permute-done.15.refs_1_ = f32[20,64,256]{2,1,0:T(8,128)S(1)} collective-permute-done((f32[20,64,256]{2,1,0:T(8,128)S(1)}, f32[20,64,256]{2,1,0:T(8,128)S(1)}, u32[]{:S(2)}, u32[]{:S(2)}) %collective-permute-start.15) | collective-permute-done | bytes 1310752 | tf_op jit(solution)/shard_map/ppermute | solution.py:46
  184.7 13.6 %shard_map.65 = f32[20,64,256]{2,1,0:T(8,128)} custom-call(s32[1280]{0:T(1024)} %add.218.pick_ref, s32[2]{0:T(128)} %add_convert_fusion.flag_ref, f32[20,64,256]{2,1,0:T(8,128)} %copy-done.8, f32[20,64,256]{2,1,0:T(8,128)} %copy-done.17, f32[20,64,256]{2,1,0:T(8,128)} %copy-done.19, f32[20,64,256]{2,1,0:T(8,128)} %copy-done.6, ...), custom_call_target="tpu_custom_call" | custom-call | flops 1000000000 | bytes 12000000 | tf_op jit(solution)/shard_map/pallas_call | solution.py:224
  199.2 2.9 %collective-permute-done.22 = f32[20,64,256]{2,1,0:T(8,128)S(1)} collective-permute-done((f32[20,64,256]{2,1,0:T(8,128)}, f32[20,64,256]{2,1,0:T(8,128)S(1)}, u32[]{:S(2)}, u32[]{:S(2)}) %collective-permute-start.22) | collective-permute-done | bytes 1310752 | tf_op jit(solution)/shard_map/ppermute | solution.py:46
  204.8 17.1 %collective-permute-done.23 = f32[20,64,256]{2,1,0:T(8,128)S(1)} collective-permute-done((f32[20,64,256]{2,1,0:T(8,128)S(1)}, f32[20,64,256]{2,1,0:T(8,128)S(1)}, u32[]{:S(2)}, u32[]{:S(2)}) %collective-permute-start.23) | collective-permute-done | bytes 1310752 | tf_op jit(solution)/shard_map/ppermute | solution.py:46
  (129 shorter events, 38.5 us)
Async XLA Ops:
  3.6 34.2 %all-to-all-start = ((f32[32,64,256]{2,1,0:T(8,128)}), f32[32,64,256]{2,1,0:T(8,128)S(1)}, u32[]{:S(2)}, u32[]{:S(2)}) async-start(f32[32,64,256]{2,1,0:T(8,128)} %bitcast.1), calls=%async_computation | async-start | bytes 4194304 | tf_op jit(solution)/shard_map/all_to_all | solution.py:291
  38.6 23.1 %collective-permute-start.1 = (f32[20,64,256]{2,1,0:T(8,128)S(1)}, f32[20,64,256]{2,1,0:T(8,128)S(1)}, u32[]{:S(2)}, u32[]{:S(2)}) collective-permute-start(f32[20,64,256]{2,1,0:T(8,128)S(1)} %broadcast_select_fusion), channel_id=1, source_target_pairs={{0,32},{1,33},{2,34},{3,35},{12,44},{13,45},{14,46},{15,47},{16,48... | collective-permute-start | bytes 3932168 | tf_op jit(solution)/shard_map/ppermute | solution.py:46
  39.9 23.2 %collective-permute-start.7 = (f32[20,64,256]{2,1,0:T(8,128)S(1)}, f32[20,64,256]{2,1,0:T(8,128)S(1)}, u32[]{:S(2)}, u32[]{:S(2)}) collective-permute-start(f32[20,64,256]{2,1,0:T(8,128)S(1)} %broadcast_select_fusion), channel_id=1, source_target_pairs={{0,0},{1,1},{2,2},{3,3},{4,4},{5,5},{6,6},{7,7},{8,8},{9,9},{10,10... | collective-permute-start | bytes 3932168 | tf_op jit(solution)/shard_map/ppermute | solution.py:46
  40.6 27.2 %collective-permute-start = (f32[20,64,256]{2,1,0:T(8,128)S(1)}, f32[20,64,256]{2,1,0:T(8,128)S(1)}, u32[]{:S(2)}, u32[]{:S(2)}) collective-permute-start(f32[20,64,256]{2,1,0:T(8,128)S(1)} %broadcast_select_fusion), channel_id=1, source_target_pairs={{0,0},{1,9},{2,2},{3,11},{4,8},{5,1},{6,10},{7,3},{8,4},{9,13},{10... | collective-permute-start | bytes 3932168 | tf_op jit(solution)/shard_map/ppermute | solution.py:46
  48.0 19.8 %collective-permute-start.2 = (f32[20,64,256]{2,1,0:T(8,128)S(1)}, f32[20,64,256]{2,1,0:T(8,128)S(1)}, u32[]{:S(2)}, u32[]{:S(2)}) collective-permute-start(f32[20,64,256]{2,1,0:T(8,128)S(1)} %broadcast_select_fusion), channel_id=1, source_target_pairs={{0,2},{1,11},{2,0},{3,9},{12,14},{13,7},{14,12},{15,5},{16,18},{17... | collective-permute-start | bytes 3932168 | tf_op jit(solution)/shard_map/ppermute | solution.py:46
  61.7 15.8 %collective-permute-start.5 = (f32[20,64,256]{2,1,0:T(8,128)S(1)}, f32[20,64,256]{2,1,0:T(8,128)S(1)}, u32[]{:S(2)}, u32[]{:S(2)}) collective-permute-start(f32[20,64,256]{2,1,0:T(8,128)S(1)} %collective-permute-done.1.refs_7_), channel_id=1, source_target_pairs={{4,68},{5,69},{6,70},{7,71},{8,72},{9,73},{10,74},{11,75},{20,84},... | collective-permute-start | bytes 3932168 | tf_op jit(solution)/shard_map/ppermute | solution.py:46
  63.1 31.2 %collective-permute-start.8 = (f32[20,64,256]{2,1,0:T(8,128)S(1)}, f32[20,64,256]{2,1,0:T(8,128)S(1)}, u32[]{:S(2)}, u32[]{:S(2)}) collective-permute-start(f32[20,64,256]{2,1,0:T(8,128)S(1)} %collective-permute-done.7.refs_5_), channel_id=1, source_target_pairs={{0,48},{1,49},{2,50},{3,51},{4,52},{5,53},{6,54},{7,55},{8,56},{9,... | collective-permute-start | bytes 3932168 | tf_op jit(solution)/shard_map/ppermute | solution.py:46
  63.2 32.7 %collective-permute-start.9 = (f32[20,64,256]{2,1,0:T(8,128)S(1)}, f32[20,64,256]{2,1,0:T(8,128)S(1)}, u32[]{:S(2)}, u32[]{:S(2)}) collective-permute-start(f32[20,64,256]{2,1,0:T(8,128)S(1)} %collective-permute-done.7.refs_5_), channel_id=1, source_target_pairs={{0,16},{1,17},{2,18},{3,19},{4,20},{5,21},{6,22},{7,23},{8,24},{9,... | collective-permute-start | bytes 3932168 | tf_op jit(solution)/shard_map/ppermute | solution.py:46
  67.8 32.6 %collective-permute-start.3 = (f32[20,64,256]{2,1,0:T(8,128)S(1)}, f32[20,64,256]{2,1,0:T(8,128)S(1)}, u32[]{:S(2)}, u32[]{:S(2)}) collective-permute-start(f32[20,64,256]{2,1,0:T(8,128)S(1)} %collective-permute-done.refs_0_), channel_id=1, source_target_pairs={{0,1},{1,2},{2,3},{3,0},{4,5},{5,6},{6,7},{7,4},{8,9},{9,10},{10,1... | collective-permute-start | bytes 3932168 | tf_op jit(solution)/shard_map/ppermute | solution.py:46
  69.7 31.6 %collective-permute-start.4 = (f32[20,64,256]{2,1,0:T(8,128)S(1)}, f32[20,64,256]{2,1,0:T(8,128)S(1)}, u32[]{:S(2)}, u32[]{:S(2)}) collective-permute-start(f32[20,64,256]{2,1,0:T(8,128)S(1)} %collective-permute-done.refs_0_), channel_id=1, source_target_pairs={{0,3},{1,0},{2,1},{3,2},{4,7},{5,4},{6,5},{7,6},{8,11},{9,8},{10,9... | collective-permute-start | bytes 3932168 | tf_op jit(solution)/shard_map/ppermute | solution.py:46
  77.6 25.1 %collective-permute-start.6 = (f32[20,64,256]{2,1,0:T(8,128)S(1)}, f32[20,64,256]{2,1,0:T(8,128)}, u32[]{:S(2)}, u32[]{:S(2)}) collective-permute-start(f32[20,64,256]{2,1,0:T(8,128)S(1)} %collective-permute-done.2.refs_3_), channel_id=1, source_target_pairs={{0,68},{2,70},{5,65},{7,67},{9,77},{11,79},{12,72},{14,74},{16,84}... | collective-permute-start | bytes 3932168 | tf_op jit(solution)/shard_map/ppermute | solution.py:46
  116.2 4.3 %collective-permute-start.10 = (f32[20,64,256]{2,1,0:T(8,128)}, f32[20,64,256]{2,1,0:T(8,128)S(1)}, u32[]{:S(2)}, u32[]{:S(2)}) collective-permute-start(f32[20,64,256]{2,1,0:T(8,128)} %shard_map.64), channel_id=1, source_target_pairs={{0,8},{1,9},{2,10},{3,11},{4,12},{5,13},{6,14},{7,15},{8,0},{9,1},... | collective-permute-start | bytes 3932168 | tf_op jit(solution)/shard_map/ppermute | solution.py:46
  117.6 4.9 %collective-permute-start.12 = (f32[20,64,256]{2,1,0:T(8,128)}, f32[20,64,256]{2,1,0:T(8,128)}, u32[]{:S(2)}, u32[]{:S(2)}) collective-permute-start(f32[20,64,256]{2,1,0:T(8,128)} %copy-done.2), channel_id=1, source_target_pairs={{0,8},{1,9},{2,10},{3,11},{4,12},{5,13},{6,14},{7,15},{8,0},{9,1},... | collective-permute-start | bytes 3932168 | tf_op jit(solution)/shard_map/ppermute | solution.py:46
  125.2 20.2 %collective-permute-start.13 = (f32[20,64,256]{2,1,0:T(8,128)S(1)}, f32[20,64,256]{2,1,0:T(8,128)S(1)}, u32[]{:S(2)}, u32[]{:S(2)}) collective-permute-start(f32[20,64,256]{2,1,0:T(8,128)S(1)} %get-tuple-element.26), channel_id=1, source_target_pairs={{0,32},{1,33},{2,34},{3,35},{12,44},{13,45},{14,46},{15,47},{16,48... | collective-permute-start | bytes 3932168 | tf_op jit(solution)/shard_map/ppermute | solution.py:46
  126.5 20.2 %collective-permute-start.19 = (f32[20,64,256]{2,1,0:T(8,128)S(1)}, f32[20,64,256]{2,1,0:T(8,128)S(1)}, u32[]{:S(2)}, u32[]{:S(2)}) collective-permute-start(f32[20,64,256]{2,1,0:T(8,128)S(1)} %get-tuple-element.26), channel_id=1, source_target_pairs={{0,64},{1,65},{2,66},{3,67},{4,12},{5,13},{6,14},{7,15},{8,0},{9,1... | collective-permute-start | bytes 3932168 | tf_op jit(solution)/shard_map/ppermute | solution.py:46
  128.5 22.6 %collective-permute-start.14 = (f32[20,64,256]{2,1,0:T(8,128)S(1)}, f32[20,64,256]{2,1,0:T(8,128)S(1)}, u32[]{:S(2)}, u32[]{:S(2)}) collective-permute-start(f32[20,64,256]{2,1,0:T(8,128)S(1)} %get-tuple-element.27), channel_id=1, source_target_pairs={{0,2},{2,0},{5,7},{7,5},{9,11},{11,9},{12,14},{14,12},{16,18},{18,... | collective-permute-start | bytes 3932168 | tf_op jit(solution)/shard_map/ppermute | solution.py:46
  129.3 21.9 %collective-permute-start.11 = (f32[20,64,256]{2,1,0:T(8,128)S(1)}, f32[20,64,256]{2,1,0:T(8,128)S(1)}, u32[]{:S(2)}, u32[]{:S(2)}) collective-permute-start(f32[20,64,256]{2,1,0:T(8,128)S(1)} %get-tuple-element.27), channel_id=1, source_target_pairs={{0,68},{1,9},{2,70},{3,11},{4,12},{5,65},{6,14},{7,67},{8,0},{9,77... | collective-permute-start | bytes 3932168 | tf_op jit(solution)/shard_map/ppermute | solution.py:46
  145.3 15.8 %collective-permute-start.17 = (f32[20,64,256]{2,1,0:T(8,128)S(1)}, f32[20,64,256]{2,1,0:T(8,128)S(1)}, u32[]{:S(2)}, u32[]{:S(2)}) collective-permute-start(f32[20,64,256]{2,1,0:T(8,128)S(1)} %collective-permute-done.13.refs_7_), channel_id=1, source_target_pairs={{4,68},{5,69},{6,70},{7,71},{8,72},{9,73},{10,74},{11,75},{20,84},... | collective-permute-start | bytes 3932168 | tf_op jit(solution)/shard_map/ppermute | solution.py:46
  146.7 30.3 %collective-permute-start.20 = (f32[20,64,256]{2,1,0:T(8,128)S(1)}, f32[20,64,256]{2,1,0:T(8,128)S(1)}, u32[]{:S(2)}, u32[]{:S(2)}) collective-permute-start(f32[20,64,256]{2,1,0:T(8,128)S(1)} %collective-permute-done.19.refs_5_), channel_id=1, source_target_pairs={{0,48},{1,49},{2,50},{3,51},{4,52},{5,53},{6,54},{7,55},{8,56},{9,... | collective-permute-start | bytes 3932168 | tf_op jit(solution)/shard_map/ppermute | solution.py:46
  149.7 30.4 %collective-permute-start.21 = (f32[20,64,256]{2,1,0:T(8,128)S(1)}, f32[20,64,256]{2,1,0:T(8,128)S(1)}, u32[]{:S(2)}, u32[]{:S(2)}) collective-permute-start(f32[20,64,256]{2,1,0:T(8,128)S(1)} %collective-permute-done.19.refs_5_), channel_id=1, source_target_pairs={{0,16},{1,17},{2,18},{3,19},{4,20},{5,21},{6,22},{7,23},{8,24},{9,... | collective-permute-start | bytes 3932168 | tf_op jit(solution)/shard_map/ppermute | solution.py:46
  151.2 32.0 %collective-permute-start.15 = (f32[20,64,256]{2,1,0:T(8,128)S(1)}, f32[20,64,256]{2,1,0:T(8,128)S(1)}, u32[]{:S(2)}, u32[]{:S(2)}) collective-permute-start(f32[20,64,256]{2,1,0:T(8,128)S(1)} %collective-permute-done.11.refs_0_), channel_id=1, source_target_pairs={{0,1},{1,2},{2,3},{3,0},{4,5},{5,6},{6,7},{7,4},{8,9},{9,10},{10,1... | collective-permute-start | bytes 3932168 | tf_op jit(solution)/shard_map/ppermute | solution.py:46
  151.3 31.9 %collective-permute-start.16 = (f32[20,64,256]{2,1,0:T(8,128)S(1)}, f32[20,64,256]{2,1,0:T(8,128)S(1)}, u32[]{:S(2)}, u32[]{:S(2)}) collective-permute-start(f32[20,64,256]{2,1,0:T(8,128)S(1)} %collective-permute-done.11.refs_0_), channel_id=1, source_target_pairs={{0,3},{1,0},{2,1},{3,2},{4,7},{5,4},{6,5},{7,6},{8,11},{9,8},{10,9... | collective-permute-start | bytes 3932168 | tf_op jit(solution)/shard_map/ppermute | solution.py:46
  161.1 23.2 %collective-permute-start.18 = (f32[20,64,256]{2,1,0:T(8,128)S(1)}, f32[20,64,256]{2,1,0:T(8,128)}, u32[]{:S(2)}, u32[]{:S(2)}) collective-permute-start(f32[20,64,256]{2,1,0:T(8,128)S(1)} %collective-permute-done.14.refs_3_), channel_id=1, source_target_pairs={{0,68},{2,70},{5,65},{7,67},{9,77},{11,79},{12,72},{14,74},{16,84}... | collective-permute-start | bytes 3932168 | tf_op jit(solution)/shard_map/ppermute | solution.py:46
  203.5 18.4 %collective-permute-start.23 = (f32[20,64,256]{2,1,0:T(8,128)S(1)}, f32[20,64,256]{2,1,0:T(8,128)S(1)}, u32[]{:S(2)}, u32[]{:S(2)}) collective-permute-start(f32[20,64,256]{2,1,0:T(8,128)S(1)} %add.230), channel_id=1, source_target_pairs={{0,64},{1,65},{2,66},{3,67},{12,76},{13,77},{14,78},{15,79},{16,80... | collective-permute-start | bytes 3932168 | tf_op jit(solution)/shard_map/ppermute | solution.py:46
  (24 other events, 364.8 us)

commit v3 on v2

--- a/solution.py
+++ b/solution.py
@@ -11,9 +11,10 @@
 N_LAYER, N_Y, N_CORE, N_Q, N_Z = 2, 4, 2, 2, 4
 N_GROUP = 8
 N_SLOT = 4
-TABLE_STEP = 4
-ROW_STEP = 4
-VMEM_BYTES = 60 * 1024 * 1024
+TABLE_STEP = 10
+ROW_STEP = 5
+TABLE_BYTES = 20 * 1024 * 1024
+PRODUCT_BYTES = 20 * 1024 * 1024
 
 
 def moves(target):
@@ -58,30 +59,38 @@
     return lax.optimization_barrier((x, *done))[0]
 
 
-def first_round(density):
-    def right_own(layer, y, core, q, z):
-        return layer, y, core + y // 2, q, z
+def left_pass(layer, y, core, q, z):
+    return (1 - layer, y, core, 1 - q, z) if core == home_left(layer, y, core, q, z) else None
+
+
+def gather_first(density):
+    def right_step(dy):
+        return lambda layer, y, core, q, z: (layer, y + dy, core + y // 2, q, z)
 
     def left_own(layer, y, core, q, z):
         if core == layer ^ q:
             return layer, y, z + q, q, z
         return layer, y, z + q, 1 - q, z
 
-    def right_across(layer, y, core, q, z):
-        return (layer, y + 2, core + y // 2, q, z) if core == layer ^ q else None
-
     def left_across(layer, y, core, q, z):
         return (layer, y, z + q, q, z + 2) if core == layer ^ q else None
 
-    return (
-        send(density, right_across),
-        send(density, left_own),
-        send(density, left_across),
-        send(density, right_own),
-    )
-
-
-def second_round(square, mixed):
+    half = density.shape[0] // 2
+    below = send(density, right_step(1))
+    above = send(density, right_step(-1))
+    left = send(density, left_own)
+    across = send(density, left_across)
+    swapped = swap_cores(density)
+    left_now = after(left, across, swapped)
+    left_below = step(left_now, dz=1)
+    left_above = step(left_now, dz=-1)
+    left_pair = send(across, left_pass)
+    first = step(below[:half], dy=1)
+    second = step(above[half:], dy=-1)
+    return (left, left_below, left_above, across, left_pair), (density, above, first, below, second, swapped)
+
+
+def gather_second(square, mixed):
     def right_own(layer, y, core, q, z):
         home = home_right(layer, y, core, q, z)
         return (1 - layer, y, core, q, z) if core == home else (layer, y, home, q, z)
@@ -96,69 +105,68 @@
     def left_across(layer, y, core, q, z):
         return (layer, y, core, q, z + 2) if core == home_left(layer, y, core, q, z) else None
 
-    return (
-        send(mixed, right_across),
-        send(square, left_own),
-        send(square, left_across),
-        send(mixed, right_own),
-    )
-
-
-def gather(right_across, left_own, left_across, right_own):
     def right_pass(layer, y, core, q, z):
         return (1 - layer, y, core, q, z) if core != home_right(layer, y, core, q, z) else None
 
-    def left_pass(layer, y, core, q, z):
-        return (1 - layer, y, core, 1 - q, z) if core == home_left(layer, y, core, q, z) else None
-
-    right_now = after(right_own, right_across)
-    left_now = after(left_own, right_across, left_across)
-    right_below = step(right_now, dy=1)
-    right_above = step(right_now, dy=-1)
+    own = send(mixed, right_own)
+    left = send(square, left_own)
+    across = send(mixed, right_across)
+    left_across = send(square, left_across)
+    left_now = after(left, own)
+    below = step(own, dy=1)
+    above = step(own, dy=-1)
     left_below = step(left_now, dz=1)
     left_above = step(left_now, dz=-1)
-    right_pair = send(right_across, right_pass)
-    left_pair = send(after(left_across, right_pair), left_pass)
-    left = (left_own, left_below, left_above, left_across, left_pair)
-    right = (right_own, right_above, right_across, right_below, right_pair)
-    return left, right
-
-
-def product_kernel(rows, width, span, pick_ref, flag_ref, *refs):
-    left, right = refs[:5], refs[5:10]
-    out_ref, left_buf, right_buf, high, low, left_sem, right_sem = refs[10:]
-
-    def bring(buf, sem, place, src):
-        return pltpu.make_async_copy(src, buf.at[place], sem.at[place])
-
-    for place in (0, 1, 3):
-        bring(right_buf, right_sem, place, right[place]).start()
-
-    @pl.when(flag_ref[1] == 1)
-    def _():
-        bring(right_buf, right_sem, 2, right[2]).start()
-
-    @pl.when(flag_ref[1] == 0)
-    def _():
-        bring(right_buf, right_sem, 2, right[4]).start()
-
-    for place in (0, 1, 2):
-        bring(left_buf, left_sem, place, left[place]).start()
-
-    @pl.when(flag_ref[0] == 1)
-    def _():
-        bring(left_buf, left_sem, 3, left[3]).start()
-
-    @pl.when(flag_ref[0] == 0)
-    def _():
-        bring(left_buf, left_sem, 3, left[4]).start()
+    pair = send(after(across, left_across, own, left), right_pass)
+    left_pair = send(after(left_across, pair), left_pass)
+    return (left, left_below, left_above, left_across, left_pair), (own, above, across, below, pair)
+
+
+def table_kernel(rows, width, span, flag_ref, *refs):
+    right = refs[:-4]
+    high, low, right_buf, right_sem = refs[-4:]
+
+    def bring(place, src):
+        return pltpu.make_async_copy(src, right_buf.at[place], right_sem.at[place])
+
+    for place in (1, 3):
+        bring(place, right[place]).start()
+
+    half = right[2].shape[0]
+    if half < rows:
+        first = pltpu.make_async_copy(right[2], right_buf.at[2, pl.ds(0, half)], right_sem.at[2])
+        second = pltpu.make_async_copy(right[4], right_buf.at[2, pl.ds(half, half)], right_sem.at[4])
+        first.start()
+        second.start()
+
+        @pl.when(flag_ref[2] == 0)
+        def _():
+            bring(0, right[0]).start()
+
+        @pl.when(flag_ref[2] == 1)
+        def _():
+            bring(0, right[5]).start()
+    else:
+        bring(0, right[0]).start()
+
+        @pl.when(flag_ref[1] == 1)
+        def _():
+            bring(2, right[2]).start()
+
+        @pl.when(flag_ref[1] == 0)
+        def _():
+            bring(2, right[4]).start()
 
     none = 4 * rows * span
     high[none] = jnp.zeros(high.shape[1:], high.dtype)
     low[none] = jnp.zeros(low.shape[1:], low.dtype)
 
-    for place in range(4):
-        bring(right_buf, right_sem, place, right[place]).wait()
+    for place in (1, 3, 0, 2):
+        if place == 2 and half < rows:
+            first.wait()
+            second.wait()
+        else:
+            bring(place, right[place]).wait()
 
         @pl.loop(0, rows // TABLE_STEP)
         def _(step):
@@ -168,15 +176,51 @@
                 x = right_buf[place, row]
                 for v in range(2):
                     piece = x[:, v * 2 * width : (v + 1) * 2 * width]
-                    top = piece.astype(jnp.bfloat16).astype(jnp.float32)
-                    rest = piece - top
-                    high[at + 2 * v] = top.astype(jnp.bfloat16)
-                    low[at + 2 * v] = rest.astype(jnp.bfloat16)
-                    high[at + 2 * v + 1] = pltpu.roll(top, width, 1).astype(jnp.bfloat16)
-                    low[at + 2 * v + 1] = pltpu.roll(rest, width, 1).astype(jnp.bfloat16)
+                    for swap, part in enumerate((piece, pltpu.roll(piece, width, 1))):
+                        top = part.astype(jnp.bfloat16)
+                        high[at + 2 * v + swap] = top
+                        low[at + 2 * v + swap] = (part - top.astype(jnp.float32)).astype(jnp.bfloat16)
+
+
+def table(right, flags):
+    rows, width, wide = right[0].shape
+    span = wide // width
+    kind = pltpu.VMEM((4 * rows * span + 1, width, 2 * width), jnp.bfloat16)
+    return pl.pallas_call(
+        functools.partial(table_kernel, rows, width, span),
+        out_shape=(kind, kind),
+        in_specs=[pl.BlockSpec(memory_space=pltpu.SMEM)]
+        + [pl.BlockSpec(memory_space=pl.ANY)] * len(right),
+        out_specs=(pl.BlockSpec(memory_space=pltpu.VMEM),) * 2,
+        scratch_shapes=[
+            pltpu.VMEM((4, rows, width, wide), jnp.float32),
+            pltpu.SemaphoreType.DMA((5,)),
+        ],
+        compiler_params=pltpu.CompilerParams(vmem_limit_bytes=TABLE_BYTES),
+        cost_estimate=pl.CostEstimate(flops=4 * 10**9, bytes_accessed=10**7, transcendentals=0),
+    )(flags, *right)
+
+
+def product_kernel(rows, width, span, pick_ref, flag_ref, high, low, *refs):
+    left = refs[:5]
+    out_ref, left_buf, left_sem = refs[5:]
+
+    def bring(place, src):
+        return pltpu.make_async_copy(src, left_buf.at[place], left_sem.at[place])
+
+    for place in (0, 1, 2):
+        bring(place, left[place]).start()
+
+    @pl.when(flag_ref[0] == 1)
+    def _():
+        bring(3, left[3]).start()
+
+    @pl.when(flag_ref[0] == 0)
+    def _():
+        bring(3, left[4]).start()
 
     for place in range(4):
-        bring(left_buf, left_sem, place, left[0]).wait()
+        bring(place, left[0]).wait()
 
     lane = lax.broadcasted_iota(jnp.int32, (width, 2 * width), 1) < width
 
@@ -188,12 +232,12 @@
             for k in range(span):
                 at = ((row * 4 + place) * span + k) * span
                 picks = [pick_ref[at + m] for m in range(span)]
-                for table, rows_of in ((high, top_rows), (low, low_rows)):
+                for entries, rows_of in ((high, top_rows), (low, low_rows)):
                     rows_of.append(
                         jnp.concatenate(
                             [
-                                jnp.where(lane, table[picks[0]], table[picks[1]]),
-                                jnp.where(lane, table[picks[2]], table[picks[3]]),
+                                jnp.where(lane, entries[picks[0]], entries[picks[1]]),
+                                jnp.where(lane, entries[picks[2]], entries[picks[3]]),
                             ],
                             axis=1,
                         )
@@ -220,24 +264,21 @@
 def product(left, right, picks, flags):
     rows, width, wide = left[0].shape
     span = wide // width
-    table = pltpu.VMEM((4 * rows * span + 1, width, 2 * width), jnp.bfloat16)
+    high, low = (pltpu.with_memory_space_constraint(x, pltpu.VMEM) for x in table(right, flags))
     return pl.pallas_call(
         functools.partial(product_kernel, rows, width, span),
         out_shape=jax.ShapeDtypeStruct((rows, width, wide), jnp.float32),
         in_specs=[pl.BlockSpec(memory_space=pltpu.SMEM)] * 2
-        + [pl.BlockSpec(memory_space=pl.ANY)] * (len(left) + len(right)),
+        + [pl.BlockSpec(memory_space=pltpu.VMEM)] * 2
+        + [pl.BlockSpec(memory_space=pl.ANY)] * len(left),
         out_specs=pl.BlockSpec(memory_space=pltpu.VMEM),
         scratch_shapes=[
             pltpu.VMEM((4, rows, width, wide), jnp.float32),
-            pltpu.VMEM((4, rows, width, wide), jnp.float32),
-            table,
-            table,
-            pltpu.SemaphoreType.DMA((4,)),
             pltpu.SemaphoreType.DMA((4,)),
         ],
-        compiler_params=pltpu.CompilerParams(vmem_limit_bytes=VMEM_BYTES),
-        cost_estimate=pl.CostEstimate(flops=10**9, bytes_accessed=12 * 10**6, transcendentals=0),
-    )(picks, flags, *left, *right)
+        compiler_params=pltpu.CompilerParams(vmem_limit_bytes=PRODUCT_BYTES),
+        cost_estimate=pl.CostEstimate(flops=8 * 10**9, bytes_accessed=10**7, transcendentals=0),
+    )(picks, flags, high, low, *left)
 
 
 def pick_table(block_cols, out_cols, grid_row, grid_col, core, y, z, rows, span):
@@ -295,33 +336,34 @@
     out_cols = lax.dynamic_slice(block_cols, (row_here * rows, grid_col * span), (rows, span))
     keep = lax.dynamic_slice(filter_mask, (row_here * rows, grid_col * span), (rows, span))
     picks = pick_table(block_cols, out_cols, row_here, grid_col, core, y, z, rows, span)
-    flags = jnp.stack([core == (z + q) % 2, core != (part + y // 2) % 2]).astype(jnp.int32)
-
-    plain_got, picks, flags = lax.optimization_barrier((plain_got, picks, flags))
-    density = jnp.take(plain_got, source, axis=0)
-
-    left, right = gather(*first_round(density))
-    mine = jnp.where(core == part, density, swap_cores(after(density, left[4])))
+    flags = jnp.stack([core == (z + q) % 2, core != (part + y // 2) % 2, y >= 2]).astype(jnp.int32)
+
+    keep_wide = jnp.repeat(keep.astype(jnp.float32), width, axis=1)[:, None, :]
+    own = (out_cols == (row_here * rows + local)[:, None]).astype(jnp.float32)
+    plain_got, source, picks, flags, keep_wide, own = lax.optimization_barrier(
+        (plain_got, source, picks, flags, keep_wide, own)
+    )
+    density = plain_got.at[source].get(mode="promise_in_bounds")
+
+    left, right = gather_first(density)
+    mine = jnp.where(core == part, density, right[5])
     partial_value = product(left, right, picks, flags)
     square = partial_value + swap_cores(partial_value)
-    keep_wide = jnp.repeat(keep.astype(jnp.float32), width, axis=1)[:, None, :]
     square = square * keep_wide
-    own = (out_cols == (row_here * rows + local)[:, None]).astype(jnp.float32)
     unit = (own[:, None, :, None] * jnp.eye(width, dtype=jnp.float32)[None, :, None, :]).reshape(
         rows, width, span * width
     )
     mix = gamma[0]
     mixed = mix * unit + (4.0 - 2.0 * mix) * mine + (mix - 3.0) * square
 
-    left, right = gather(*second_round(square, mixed))
+    left, right = gather_second(square, mixed)
+
+    def output(layer, y, core, q, z):
+        return (1 - layer, y, core, q, z) if core == layer ^ q else None
+
     total = product(left, right, picks, flags)
     total = total + swap_cores(total)
-
-    def output(layer, y, core, q, z):
-        return (1 - layer, y, core, q, z) if core == layer ^ q else None
-
-    swapped = send(total, output)
-    return jnp.where(core == part, total, swapped)
+    return jnp.where(core == part, total, send(total, output))
 
 
 def solution(mesh):

time: 224 us -> 210 us (0.938)
  Pallas kernels: 27.2 us -> 21.8 us
  waiting for transfers between devices: 118 us -> 114 us
  local copies, waits for them, and re-layouts: 10.7 us -> 7.39 us
  other arithmetic: 13.9 us -> 11.5 us
    pallas_call x2, Pallas kernels: 27.2 us -> 15.7 us  [product(): pl.pallas_call(functools.partial(product_kernel, rows, width, span), out_...]
    pallas_call x0 -> x2, Pallas kernels: none -> 6.09 us  [table(): pl.pallas_call(functools.partial(table_kernel, rows, width, span), out_sh...]
    ppermute x24 -> x23, waiting for transfers between devices: 104 us -> 99.3 us  [send(): return lax.ppermute(x, AXES, moves(target))]
    unnamed x47 -> x7, local copies, waits for them, and re-layouts: 4.39 us -> 1.58 us
    ppermute x24 -> x23, starting transfers between devices: 43.1 us -> 44 us  [send(): return lax.ppermute(x, AXES, moves(target))]
  transfers between devices with their start and end apart: 25 -> 24, of which waited for: 16 -> 13; matrix products, arithmetic and copies ran while one was open for 5% -> 5% of each run, Pallas kernels for 0% -> 3%
where the time goes in v3:
time: 210 us; the launch traced here: 209 us
  waiting for transfers between devices  114 us (54%)
  starting transfers between devices  52.6 us (25%)
  Pallas kernels  21.8 us (10%)
  other arithmetic  11.5 us (5%)
  local copies, waits for them, and re-layouts  7.39 us (4%)
    ppermute x23, waiting for transfers between devices, send(): return lax.ppermute(x, AXES, moves(target))  99.3 us
    ppermute x23, starting transfers between devices, send(): return lax.ppermute(x, AXES, moves(target))  44 us
    pallas_call x2, Pallas kernels, product(): pl.pallas_call(functools.partial(product_kernel, rows, width, span), out_...  15.7 us
    all_to_all x1, waiting for transfers between devices, body(): lax.all_to_all(plain_send, ('layer', 'col'), split_axis=0, concat_axis=0,...  14.9 us
    all_to_all x1, starting transfers between devices, body(): lax.all_to_all(plain_send, ('layer', 'col'), split_axis=0, concat_axis=0,...  8.56 us
    pallas_call x2, Pallas kernels, table(): pl.pallas_call(functools.partial(table_kernel, rows, width, span), out_sh...  6.09 us
    reduce_sum x1, other arithmetic, pick_table(): found = jnp.sum(hit[..., None] * right_cols[None, :, None], axis=3)  5.6 us
  transfers between devices with their start and end apart: 24, of which 13 were waited for; matrix products, arithmetic and copies ran while one was open for 5% of the time, Pallas kernels for 3%

profile of v3, /device:TPU:1, one launch (start us, length us, event | category | flops | bytes accessed | tf_op | source)
XLA Modules:
  0.0 208.7 jit_solution(11198238508775209898)
XLA Ops:
  3.6 8.6 %all-to-all-start = ((f32[32,64,256]{2,1,0:T(8,128)}), f32[32,64,256]{2,1,0:T(8,128)S(1)}, u32[]{:S(2)}, u32[]{:S(2)}) async-start(f32[32,64,256]{2,1,0:T(8,128)} %bitcast.1), calls=%async_computation | async-start | bytes 4194304 | tf_op jit(solution)/shard_map/all_to_all | solution.py:332
  15.1 5.6 %multiply_reduce_fusion = s32[20,4,4,4]{3,2,1,0:T(4,128)S(1)} fusion(s32[4,20,4]{1,2,0:T(4,128)S(1)} %multiply_reduce_fusion.2, s32[20,4,4,20]{3,2,1,0:T(4,128)S(1)} %fusion), kind=kLoop, calls=%fused_computation.6 | loop fusion | flops 49920 | bytes 32000 | tf_op jit(solution)/shard_map/reduce_sum | solution.py:299
  22.9 14.9 %all-to-all-done = f32[32,64,256]{2,1,0:T(8,128)S(1)} async-done(((f32[32,64,256]{2,1,0:T(8,128)}), f32[32,64,256]{2,1,0:T(8,128)S(1)}, u32[]{:S(2)}, u32[]{:S(2)}) %all-to-all-start) | async-done | bytes 2097184 | tf_op jit(solution)/shard_map/all_to_all | solution.py:332
  38.4 2.9 %collective-permute-start = (f32[20,64,256]{2,1,0:T(8,128)S(1)}, f32[20,64,256]{2,1,0:T(8,128)S(1)}, u32[]{:S(2)}, u32[]{:S(2)}) collective-permute-start(f32[20,64,256]{2,1,0:T(8,128)S(1)} %gather_fusion), channel_id=1, source_target_pairs={{0,8},{1,9},{2,10},{3,11},{4,12},{5,13},{6,14},{7,15},{8,0},{9,1},... | collective-permute-start | bytes 3932168 | tf_op jit(solution)/shard_map/ppermute | solution.py:47
  41.4 4.6 %collective-permute-start.5 = (f32[20,64,256]{2,1,0:T(8,128)S(1)}, f32[20,64,256]{2,1,0:T(8,128)S(1)}, u32[]{:S(2)}, u32[]{:S(2)}) collective-permute-start(f32[20,64,256]{2,1,0:T(8,128)S(1)} %gather_fusion), channel_id=1, source_target_pairs={{0,0},{1,9},{2,2},{3,11},{4,8},{5,1},{6,10},{7,3},{8,4},{9,13},{10... | collective-permute-start | bytes 3932168 | tf_op jit(solution)/shard_map/ppermute | solution.py:47
  49.7 12.3 %collective-permute-done.5.refs_0_ = f32[20,64,256]{2,1,0:T(8,128)S(1)} collective-permute-done((f32[20,64,256]{2,1,0:T(8,128)S(1)}, f32[20,64,256]{2,1,0:T(8,128)S(1)}, u32[]{:S(2)}, u32[]{:S(2)}) %collective-permute-start.5) | collective-permute-done | bytes 1310752 | tf_op jit(solution)/shard_map/ppermute | solution.py:47
  62.1 5.0 %collective-permute-start.7 = (f32[20,64,256]{2,1,0:T(8,128)S(1)}, f32[20,64,256]{2,1,0:T(8,128)S(1)}, u32[]{:S(2)}, u32[]{:S(2)}) collective-permute-start(f32[20,64,256]{2,1,0:T(8,128)S(1)} %collective-permute-done.5.refs_0_), channel_id=1, source_target_pairs={{0,1},{1,2},{2,3},{3,0},{4,5},{5,6},{6,7},{7,4},{8,9},{9,10},{10,1... | collective-permute-start | bytes 3932168 | tf_op jit(solution)/shard_map/ppermute | solution.py:47
  68.3 10.7 %collective-permute-done.2.refs_3_ = f32[20,64,256]{2,1,0:T(8,128)S(1)} collective-permute-done((f32[20,64,256]{2,1,0:T(8,128)S(1)}, f32[20,64,256]{2,1,0:T(8,128)S(1)}, u32[]{:S(2)}, u32[]{:S(2)}) %collective-permute-start.2) | collective-permute-done | bytes 1310752 | tf_op jit(solution)/shard_map/ppermute | solution.py:47
  79.3 2.7 %collective-permute-start.4 = (f32[10,64,256]{2,1,0:T(8,128)S(1)}, f32[10,64,256]{2,1,0:T(8,128)S(1)}, u32[]{:S(2)}, u32[]{:S(2)}) collective-permute-start(f32[10,64,256]{2,1,0:T(8,128)S(1)} %slice.15), channel_id=1, source_target_pairs={{0,48},{1,49},{2,50},{3,51},{4,52},{5,53},{6,54},{7,55},{8,56},{9,... | collective-permute-start | bytes 1966088 | tf_op jit(solution)/shard_map/ppermute | solution.py:47
  82.0 14.6 %collective-permute-done.3.refs_2_ = f32[10,64,256]{2,1,0:T(8,128)S(1)} collective-permute-done((f32[10,64,256]{2,1,0:T(8,128)S(1)}, f32[10,64,256]{2,1,0:T(8,128)S(1)}, u32[]{:S(2)}, u32[]{:S(2)}) %collective-permute-start.3) | collective-permute-done | bytes 655392 | tf_op jit(solution)/shard_map/ppermute | solution.py:47
  96.6 3.2 %shard_map.64 = (bf16[321,64,128]{2,1,0:T(8,128)(2,1)S(1)}, bf16[321,64,128]{2,1,0:T(8,128)(2,1)S(1)}) custom-call(s32[3]{0:T(128)S(1)} %add_convert_fusion.flag_ref, f32[20,64,256]{2,1,0:T(8,128)S(1)} %gather_fusion, f32[20,64,256]{2,1,0:T(8,128)S(1)} %collective-permute-done.1.refs_1_, f32[10,64,256]{2,1,0:T(8,128)S(1)} %collective-permute-done.3.refs_2_, ...), custom_call_target="tpu_custom_call" | custom-call | flops 4000000000 | bytes 10000000 | tf_op jit(solution)/shard_map/pallas_call | solution.py:189
  99.8 8.5 %shard_map.65 = f32[20,64,256]{2,1,0:T(8,128)} custom-call(s32[1280]{0:T(1024)S(1)} %add.218.pick_ref, s32[3]{0:T(128)S(1)} %add_convert_fusion.flag_ref, bf16[321,64,128]{2,1,0:T(8,128)(2,1)S(1)} %get-tuple-element.25.high, bf16[321,64,128]{2,1,0:T(8,128)(2,1)S(1)} %get-tuple-element.26.low, f32[20,64,256]{2,1,0:T(8,128)S(1)} %collective-permute-done.5.refs_0_, ...), custom_call_target="tpu_custom_call" | custom-call | flops 8000000000 | bytes 10000000 | tf_op jit(solution)/shard_map/pallas_call | solution.py:268
  112.3 2.4 %multiply_add_fusion = (f32[20,64,256]{2,1,0:T(8,128)S(1)}, f32[20,64,256]{2,1,0:T(8,128)S(1)}) fusion(f32[20,64,256]{2,1,0:T(8,128)S(1)} %gather_fusion, f32[20,64,256]{2,1,0:T(8,128)S(1)} %collective-permute-done.refs_5_, f32[]{:T(128)S(6)} %sub.64, f32[]{:T(128)S(6)} %sub.63, f32[64,256]{1,0:T(8,128)S(1)} %mul.176, f32[20,256]{1,0:T(8,128)S(1)} %mul.173, ...), kind=kLoop, calls=%fused_computation.3 | loop fusion | flops 2949120 | bytes 7970829 | tf_op jit(solution)/shard_map/add | solution.py:357
  117.2 5.9 %collective-permute-start.16 = (f32[20,64,256]{2,1,0:T(8,128)S(1)}, f32[20,64,256]{2,1,0:T(8,128)S(1)}, u32[]{:S(2)}, u32[]{:S(2)}) collective-permute-start(f32[20,64,256]{2,1,0:T(8,128)S(1)} %get-tuple-element.35), channel_id=1, source_target_pairs={{0,68},{1,9},{2,70},{3,11},{4,12},{5,65},{6,14},{7,67},{8,0},{9,77... | collective-permute-start | bytes 3932168 | tf_op jit(solution)/shard_map/ppermute | solution.py:47
  123.1 9.3 %collective-permute-done.11.refs_0_ = f32[20,64,256]{2,1,0:T(8,128)S(1)} collective-permute-done((f32[20,64,256]{2,1,0:T(8,128)S(1)}, f32[20,64,256]{2,1,0:T(8,128)S(1)}, u32[]{:S(2)}, u32[]{:S(2)}) %collective-permute-start.11) | collective-permute-done | bytes 1310752 | tf_op jit(solution)/shard_map/ppermute | solution.py:47
  132.4 2.9 %collective-permute-done.13.refs_2_ = f32[20,64,256]{2,1,0:T(8,128)S(1)} collective-permute-done((f32[20,64,256]{2,1,0:T(8,128)S(1)}, f32[20,64,256]{2,1,0:T(8,128)S(1)}, u32[]{:S(2)}, u32[]{:S(2)}) %collective-permute-start.13) | collective-permute-done | bytes 1310752 | tf_op jit(solution)/shard_map/ppermute | solution.py:47
  137.5 3.3 %collective-permute-start.17 = (f32[20,64,256]{2,1,0:T(8,128)S(1)}, f32[20,64,256]{2,1,0:T(8,128)S(1)}, u32[]{:S(2)}, u32[]{:S(2)}) collective-permute-start(f32[20,64,256]{2,1,0:T(8,128)S(1)} %collective-permute-done.13.refs_2_), channel_id=1, source_target_pairs={{4,68},{5,69},{6,70},{7,71},{8,72},{9,73},{10,74},{11,75},{20,84},... | collective-permute-start | bytes 3932168 | tf_op jit(solution)/shard_map/ppermute | solution.py:47
  145.0 10.2 %collective-permute-done.17.refs_4_ = f32[20,64,256]{2,1,0:T(8,128)S(1)} collective-permute-done((f32[20,64,256]{2,1,0:T(8,128)S(1)}, f32[20,64,256]{2,1,0:T(8,128)S(1)}, u32[]{:S(2)}, u32[]{:S(2)}) %collective-permute-start.17) | collective-permute-done | bytes 1310752 | tf_op jit(solution)/shard_map/ppermute | solution.py:47
  156.5 13.9 %collective-permute-done.12.refs_1_ = f32[20,64,256]{2,1,0:T(8,128)S(1)} collective-permute-done((f32[20,64,256]{2,1,0:T(8,128)S(1)}, f32[20,64,256]{2,1,0:T(8,128)S(1)}, u32[]{:S(2)}, u32[]{:S(2)}) %collective-permute-start.12) | collective-permute-done | bytes 1310752 | tf_op jit(solution)/shard_map/ppermute | solution.py:47
  170.4 2.9 %shard_map.66 = (bf16[321,64,128]{2,1,0:T(8,128)(2,1)S(1)}, bf16[321,64,128]{2,1,0:T(8,128)(2,1)S(1)}) custom-call(s32[3]{0:T(128)S(1)} %add_convert_fusion.flag_ref, f32[20,64,256]{2,1,0:T(8,128)S(1)} %collective-permute-done.11.refs_0_, f32[20,64,256]{2,1,0:T(8,128)S(1)} %collective-permute-done.12.refs_1_, ...), custom_call_target="tpu_custom_call" | custom-call | flops 4000000000 | bytes 10000000 | tf_op jit(solution)/shard_map/pallas_call | solution.py:189
  174.8 7.2 %shard_map.67 = f32[20,64,256]{2,1,0:T(8,128)S(1)} custom-call(s32[1280]{0:T(1024)S(1)} %add.218.pick_ref, s32[3]{0:T(128)S(1)} %add_convert_fusion.flag_ref, bf16[321,64,128]{2,1,0:T(8,128)(2,1)S(1)} %get-tuple-element.30.high, bf16[321,64,128]{2,1,0:T(8,128)(2,1)S(1)} %get-tuple-element.31.low, f32[20,64,256]{2,1,0:T(8,128)S(1)} %collective-permute-done.16.refs_0_, ...), custom_call_target="tpu_custom_call" | custom-call | flops 8000000000 | bytes 10000000 | tf_op jit(solution)/shard_map/pallas_call | solution.py:268
  182.1 4.2 %collective-permute-start.21 = (f32[20,64,256]{2,1,0:T(8,128)S(1)}, f32[20,64,256]{2,1,0:T(8,128)S(1)}, u32[]{:S(2)}, u32[]{:S(2)}) collective-permute-start(f32[20,64,256]{2,1,0:T(8,128)S(1)} %shard_map.67), channel_id=1, source_target_pairs={{0,8},{1,9},{2,10},{3,11},{4,12},{5,13},{6,14},{7,15},{8,0},{9,1},... | collective-permute-start | bytes 3932168 | tf_op jit(solution)/shard_map/ppermute | solution.py:47
  186.3 2.7 %collective-permute-done.21 = f32[20,64,256]{2,1,0:T(8,128)S(1)} collective-permute-done((f32[20,64,256]{2,1,0:T(8,128)S(1)}, f32[20,64,256]{2,1,0:T(8,128)S(1)}, u32[]{:S(2)}, u32[]{:S(2)}) %collective-permute-start.21) | collective-permute-done | bytes 1310752 | tf_op jit(solution)/shard_map/ppermute | solution.py:47
  190.4 17.1 %collective-permute-done.22 = f32[20,64,256]{2,1,0:T(8,128)S(1)} collective-permute-done((f32[20,64,256]{2,1,0:T(8,128)S(1)}, f32[20,64,256]{2,1,0:T(8,128)S(1)}, u32[]{:S(2)}, u32[]{:S(2)}) %collective-permute-start.22) | collective-permute-done | bytes 1310752 | tf_op jit(solution)/shard_map/ppermute | solution.py:47
  (91 shorter events, 32.0 us)
Async XLA Ops:
  3.6 34.2 %all-to-all-start = ((f32[32,64,256]{2,1,0:T(8,128)}), f32[32,64,256]{2,1,0:T(8,128)S(1)}, u32[]{:S(2)}, u32[]{:S(2)}) async-start(f32[32,64,256]{2,1,0:T(8,128)} %bitcast.1), calls=%async_computation | async-start | bytes 4194304 | tf_op jit(solution)/shard_map/all_to_all | solution.py:332
  38.4 11.3 %collective-permute-start = (f32[20,64,256]{2,1,0:T(8,128)S(1)}, f32[20,64,256]{2,1,0:T(8,128)S(1)}, u32[]{:S(2)}, u32[]{:S(2)}) collective-permute-start(f32[20,64,256]{2,1,0:T(8,128)S(1)} %gather_fusion), channel_id=1, source_target_pairs={{0,8},{1,9},{2,10},{3,11},{4,12},{5,13},{6,14},{7,15},{8,0},{9,1},... | collective-permute-start | bytes 3932168 | tf_op jit(solution)/shard_map/ppermute | solution.py:47
  41.4 20.7 %collective-permute-start.5 = (f32[20,64,256]{2,1,0:T(8,128)S(1)}, f32[20,64,256]{2,1,0:T(8,128)S(1)}, u32[]{:S(2)}, u32[]{:S(2)}) collective-permute-start(f32[20,64,256]{2,1,0:T(8,128)S(1)} %gather_fusion), channel_id=1, source_target_pairs={{0,0},{1,9},{2,2},{3,11},{4,8},{5,1},{6,10},{7,3},{8,4},{9,13},{10... | collective-permute-start | bytes 3932168 | tf_op jit(solution)/shard_map/ppermute | solution.py:47
  45.9 16.1 %collective-permute-start.6 = (f32[20,64,256]{2,1,0:T(8,128)S(1)}, f32[20,64,256]{2,1,0:T(8,128)S(1)}, u32[]{:S(2)}, u32[]{:S(2)}) collective-permute-start(f32[20,64,256]{2,1,0:T(8,128)S(1)} %gather_fusion), channel_id=1, source_target_pairs={{0,2},{1,11},{2,0},{3,9},{12,14},{13,7},{14,12},{15,5},{16,18},{17... | collective-permute-start | bytes 3932168 | tf_op jit(solution)/shard_map/ppermute | solution.py:47
  46.7 32.4 %collective-permute-start.2 = (f32[20,64,256]{2,1,0:T(8,128)S(1)}, f32[20,64,256]{2,1,0:T(8,128)S(1)}, u32[]{:S(2)}, u32[]{:S(2)}) collective-permute-start(f32[20,64,256]{2,1,0:T(8,128)S(1)} %gather_fusion), channel_id=1, source_target_pairs={{0,16},{1,17},{2,18},{3,19},{4,20},{5,21},{6,22},{7,23},{8,24},{9,... | collective-permute-start | bytes 3932168 | tf_op jit(solution)/shard_map/ppermute | solution.py:47
  48.1 31.1 %collective-permute-start.1 = (f32[20,64,256]{2,1,0:T(8,128)S(1)}, f32[20,64,256]{2,1,0:T(8,128)S(1)}, u32[]{:S(2)}, u32[]{:S(2)}) collective-permute-start(f32[20,64,256]{2,1,0:T(8,128)S(1)} %gather_fusion), channel_id=1, source_target_pairs={{0,48},{1,49},{2,50},{3,51},{4,52},{5,53},{6,54},{7,55},{8,56},{9,... | collective-permute-start | bytes 3932168 | tf_op jit(solution)/shard_map/ppermute | solution.py:47
  62.1 37.7 %collective-permute-start.7 = (f32[20,64,256]{2,1,0:T(8,128)S(1)}, f32[20,64,256]{2,1,0:T(8,128)S(1)}, u32[]{:S(2)}, u32[]{:S(2)}) collective-permute-start(f32[20,64,256]{2,1,0:T(8,128)S(1)} %collective-permute-done.5.refs_0_), channel_id=1, source_target_pairs={{0,1},{1,2},{2,3},{3,0},{4,5},{5,6},{6,7},{7,4},{8,9},{9,10},{10,1... | collective-permute-start | bytes 3932168 | tf_op jit(solution)/shard_map/ppermute | solution.py:47
  67.0 32.8 %collective-permute-start.8 = (f32[20,64,256]{2,1,0:T(8,128)S(1)}, f32[20,64,256]{2,1,0:T(8,128)S(1)}, u32[]{:S(2)}, u32[]{:S(2)}) collective-permute-start(f32[20,64,256]{2,1,0:T(8,128)S(1)} %collective-permute-done.5.refs_0_), channel_id=1, source_target_pairs={{0,3},{1,0},{2,1},{3,2},{4,7},{5,4},{6,5},{7,6},{8,11},{9,8},{10,9... | collective-permute-start | bytes 3932168 | tf_op jit(solution)/shard_map/ppermute | solution.py:47
  67.0 32.8 %collective-permute-start.9 = (f32[20,64,256]{2,1,0:T(8,128)S(1)}, f32[20,64,256]{2,1,0:T(8,128)S(1)}, u32[]{:S(2)}, u32[]{:S(2)}) collective-permute-start(f32[20,64,256]{2,1,0:T(8,128)S(1)} %collective-permute-done.6.refs_3_), channel_id=1, source_target_pairs={{0,68},{2,70},{5,65},{7,67},{9,77},{11,79},{12,72},{14,74},{16,84}... | collective-permute-start | bytes 3932168 | tf_op jit(solution)/shard_map/ppermute | solution.py:47
  79.1 17.5 %collective-permute-start.3 = (f32[10,64,256]{2,1,0:T(8,128)S(1)}, f32[10,64,256]{2,1,0:T(8,128)S(1)}, u32[]{:S(2)}, u32[]{:S(2)}) collective-permute-start(f32[10,64,256]{2,1,0:T(8,128)S(1)} %slice.14), channel_id=1, source_target_pairs={{0,16},{1,17},{2,18},{3,19},{4,20},{5,21},{6,22},{7,23},{8,24},{9,... | collective-permute-start | bytes 1966088 | tf_op jit(solution)/shard_map/ppermute | solution.py:47
  79.3 17.3 %collective-permute-start.4 = (f32[10,64,256]{2,1,0:T(8,128)S(1)}, f32[10,64,256]{2,1,0:T(8,128)S(1)}, u32[]{:S(2)}, u32[]{:S(2)}) collective-permute-start(f32[10,64,256]{2,1,0:T(8,128)S(1)} %slice.15), channel_id=1, source_target_pairs={{0,48},{1,49},{2,50},{3,51},{4,52},{5,53},{6,54},{7,55},{8,56},{9,... | collective-permute-start | bytes 1966088 | tf_op jit(solution)/shard_map/ppermute | solution.py:47
  108.3 4.0 %collective-permute-start.10 = (f32[20,64,256]{2,1,0:T(8,128)}, f32[20,64,256]{2,1,0:T(8,128)}, u32[]{:S(2)}, u32[]{:S(2)}) collective-permute-start(f32[20,64,256]{2,1,0:T(8,128)} %shard_map.65), channel_id=1, source_target_pairs={{0,8},{1,9},{2,10},{3,11},{4,12},{5,13},{6,14},{7,15},{8,0},{9,1},... | collective-permute-start | bytes 3932168 | tf_op jit(solution)/shard_map/ppermute | solution.py:47
  114.7 17.7 %collective-permute-start.11 = (f32[20,64,256]{2,1,0:T(8,128)S(1)}, f32[20,64,256]{2,1,0:T(8,128)S(1)}, u32[]{:S(2)}, u32[]{:S(2)}) collective-permute-start(f32[20,64,256]{2,1,0:T(8,128)S(1)} %get-tuple-element.34), channel_id=1, source_target_pairs={{0,64},{1,65},{2,66},{3,67},{4,12},{5,13},{6,14},{7,15},{8,0},{9,1... | collective-permute-start | bytes 3932168 | tf_op jit(solution)/shard_map/ppermute | solution.py:47
  115.2 20.1 %collective-permute-start.13 = (f32[20,64,256]{2,1,0:T(8,128)S(1)}, f32[20,64,256]{2,1,0:T(8,128)S(1)}, u32[]{:S(2)}, u32[]{:S(2)}) collective-permute-start(f32[20,64,256]{2,1,0:T(8,128)S(1)} %get-tuple-element.34), channel_id=1, source_target_pairs={{0,32},{1,33},{2,34},{3,35},{12,44},{13,45},{14,46},{15,47},{16,48... | collective-permute-start | bytes 3932168 | tf_op jit(solution)/shard_map/ppermute | solution.py:47
  116.5 18.9 %collective-permute-start.15 = (f32[20,64,256]{2,1,0:T(8,128)S(1)}, f32[20,64,256]{2,1,0:T(8,128)S(1)}, u32[]{:S(2)}, u32[]{:S(2)}) collective-permute-start(f32[20,64,256]{2,1,0:T(8,128)S(1)} %get-tuple-element.35), channel_id=1, source_target_pairs={{0,2},{2,0},{5,7},{7,5},{9,11},{11,9},{12,14},{14,12},{16,18},{18,... | collective-permute-start | bytes 3932168 | tf_op jit(solution)/shard_map/ppermute | solution.py:47
  117.2 20.3 %collective-permute-start.16 = (f32[20,64,256]{2,1,0:T(8,128)S(1)}, f32[20,64,256]{2,1,0:T(8,128)S(1)}, u32[]{:S(2)}, u32[]{:S(2)}) collective-permute-start(f32[20,64,256]{2,1,0:T(8,128)S(1)} %get-tuple-element.35), channel_id=1, source_target_pairs={{0,68},{1,9},{2,70},{3,11},{4,12},{5,65},{6,14},{7,67},{8,0},{9,77... | collective-permute-start | bytes 3932168 | tf_op jit(solution)/shard_map/ppermute | solution.py:47
  137.5 17.7 %collective-permute-start.17 = (f32[20,64,256]{2,1,0:T(8,128)S(1)}, f32[20,64,256]{2,1,0:T(8,128)S(1)}, u32[]{:S(2)}, u32[]{:S(2)}) collective-permute-start(f32[20,64,256]{2,1,0:T(8,128)S(1)} %collective-permute-done.13.refs_2_), channel_id=1, source_target_pairs={{4,68},{5,69},{6,70},{7,71},{8,72},{9,73},{10,74},{11,75},{20,84},... | collective-permute-start | bytes 3932168 | tf_op jit(solution)/shard_map/ppermute | solution.py:47
  140.8 29.6 %collective-permute-start.12 = (f32[20,64,256]{2,1,0:T(8,128)S(1)}, f32[20,64,256]{2,1,0:T(8,128)S(1)}, u32[]{:S(2)}, u32[]{:S(2)}) collective-permute-start(f32[20,64,256]{2,1,0:T(8,128)S(1)} %collective-permute-done.11.refs_0_), channel_id=1, source_target_pairs={{0,48},{1,49},{2,50},{3,51},{4,52},{5,53},{6,54},{7,55},{8,56},{9,... | collective-permute-start | bytes 3932168 | tf_op jit(solution)/shard_map/ppermute | solution.py:47
  141.4 29.1 %collective-permute-start.14 = (f32[20,64,256]{2,1,0:T(8,128)S(1)}, f32[20,64,256]{2,1,0:T(8,128)S(1)}, u32[]{:S(2)}, u32[]{:S(2)}) collective-permute-start(f32[20,64,256]{2,1,0:T(8,128)S(1)} %collective-permute-done.11.refs_0_), channel_id=1, source_target_pairs={{0,16},{1,17},{2,18},{3,19},{4,20},{5,21},{6,22},{7,23},{8,24},{9,... | collective-permute-start | bytes 3932168 | tf_op jit(solution)/shard_map/ppermute | solution.py:47
  142.3 31.0 %collective-permute-start.18 = (f32[20,64,256]{2,1,0:T(8,128)S(1)}, f32[20,64,256]{2,1,0:T(8,128)S(1)}, u32[]{:S(2)}, u32[]{:S(2)}) collective-permute-start(f32[20,64,256]{2,1,0:T(8,128)S(1)} %collective-permute-done.16.refs_0_), channel_id=1, source_target_pairs={{0,1},{1,2},{2,3},{3,0},{4,5},{5,6},{6,7},{7,4},{8,9},{9,10},{10,1... | collective-permute-start | bytes 3932168 | tf_op jit(solution)/shard_map/ppermute | solution.py:47
  143.3 30.0 %collective-permute-start.19 = (f32[20,64,256]{2,1,0:T(8,128)S(1)}, f32[20,64,256]{2,1,0:T(8,128)S(1)}, u32[]{:S(2)}, u32[]{:S(2)}) collective-permute-start(f32[20,64,256]{2,1,0:T(8,128)S(1)} %collective-permute-done.16.refs_0_), channel_id=1, source_target_pairs={{0,3},{1,0},{2,1},{3,2},{4,7},{5,4},{6,5},{7,6},{8,11},{9,8},{10,9... | collective-permute-start | bytes 3932168 | tf_op jit(solution)/shard_map/ppermute | solution.py:47
  155.3 19.6 %collective-permute-start.20 = (f32[20,64,256]{2,1,0:T(8,128)S(1)}, f32[20,64,256]{2,1,0:T(8,128)S(1)}, u32[]{:S(2)}, u32[]{:S(2)}) collective-permute-start(f32[20,64,256]{2,1,0:T(8,128)S(1)} %collective-permute-done.15.refs_3_), channel_id=1, source_target_pairs={{0,68},{2,70},{5,65},{7,67},{9,77},{11,79},{12,72},{14,74},{16,84}... | collective-permute-start | bytes 3932168 | tf_op jit(solution)/shard_map/ppermute | solution.py:47
  182.1 6.9 %collective-permute-start.21 = (f32[20,64,256]{2,1,0:T(8,128)S(1)}, f32[20,64,256]{2,1,0:T(8,128)S(1)}, u32[]{:S(2)}, u32[]{:S(2)}) collective-permute-start(f32[20,64,256]{2,1,0:T(8,128)S(1)} %shard_map.67), channel_id=1, source_target_pairs={{0,8},{1,9},{2,10},{3,11},{4,12},{5,13},{6,14},{7,15},{8,0},{9,1},... | collective-permute-start | bytes 3932168 | tf_op jit(solution)/shard_map/ppermute | solution.py:47
  189.1 18.4 %collective-permute-start.22 = (f32[20,64,256]{2,1,0:T(8,128)S(1)}, f32[20,64,256]{2,1,0:T(8,128)S(1)}, u32[]{:S(2)}, u32[]{:S(2)}) collective-permute-start(f32[20,64,256]{2,1,0:T(8,128)S(1)} %add.229), channel_id=1, source_target_pairs={{0,64},{1,65},{2,66},{3,67},{12,76},{13,77},{14,78},{15,79},{16,80... | collective-permute-start | bytes 3932168 | tf_op jit(solution)/shard_map/ppermute | solution.py:47
  (3 other events, 26.8 us)

commit v4 on v3

--- a/solution.py
+++ b/solution.py
@@ -13,8 +13,8 @@
 N_SLOT = 4
 TABLE_STEP = 10
 ROW_STEP = 5
-TABLE_BYTES = 20 * 1024 * 1024
-PRODUCT_BYTES = 20 * 1024 * 1024
+TABLE_BYTES = 8 * 1024 * 1024
+PRODUCT_BYTES = 10 * 1024 * 1024
 
 
 def moves(target):
@@ -117,7 +117,7 @@
     above = step(own, dy=-1)
     left_below = step(left_now, dz=1)
     left_above = step(left_now, dz=-1)
-    pair = send(after(across, left_across, own, left), right_pass)
+    pair = send(after(across, own), right_pass)
     left_pair = send(after(left_across, pair), left_pass)
     return (left, left_below, left_above, left_across, left_pair), (own, above, across, below, pair)
 
@@ -201,12 +201,13 @@
     )(flags, *right)
 
 
-def product_kernel(rows, width, span, pick_ref, flag_ref, high, low, *refs):
+def product_kernel(begin, end, width, span, pick_ref, flag_ref, high, low, *refs):
     left = refs[:5]
     out_ref, left_buf, left_sem = refs[5:]
 
     def bring(place, src):
-        return pltpu.make_async_copy(src, left_buf.at[place], left_sem.at[place])
+        rows_here = src.at[pl.ds(begin, end - begin)]
+        return pltpu.make_async_copy(rows_here, left_buf.at[place], left_sem.at[place])
 
     for place in (0, 1, 2):
         bring(place, left[place]).start()
@@ -242,7 +243,7 @@
                             axis=1,
                         )
                     )
-            x = left_buf[place, row]
+            x = left_buf[place, row - begin]
             top = x.astype(jnp.bfloat16)
             rest = (x - top.astype(jnp.float32)).astype(jnp.bfloat16)
             both += jnp.dot(
@@ -253,32 +254,52 @@
             single += jnp.dot(
                 top, jnp.concatenate(low_rows, axis=0), preferred_element_type=jnp.float32
             )
-        out_ref[row] = both[:width] + both[width:] + single
-
-    @pl.loop(0, rows // ROW_STEP)
+        out_ref[row - begin] = both[:width] + both[width:] + single
+
+    @pl.loop(0, (end - begin) // ROW_STEP)
     def _(step):
         for j in range(ROW_STEP):
-            one_row(step * ROW_STEP + j)
-
-
-def product(left, right, picks, flags):
+            one_row(begin + step * ROW_STEP + j)
+
+
+def product(left, tables, picks, flags, begin, end):
     rows, width, wide = left[0].shape
     span = wide // width
-    high, low = (pltpu.with_memory_space_constraint(x, pltpu.VMEM) for x in table(right, flags))
+    near = [pltpu.with_memory_space_constraint(x, pltpu.VMEM) for x in tables]
     return pl.pallas_call(
-        functools.partial(product_kernel, rows, width, span),
-        out_shape=jax.ShapeDtypeStruct((rows, width, wide), jnp.float32),
+        functools.partial(product_kernel, begin, end, width, span),
+        out_shape=jax.ShapeDtypeStruct((end - begin, width, wide), jnp.float32),
         in_specs=[pl.BlockSpec(memory_space=pltpu.SMEM)] * 2
-        + [pl.BlockSpec(memory_space=pltpu.VMEM)] * 2
+        + [pl.BlockSpec(memory_space=pltpu.VMEM)] * len(near)
         + [pl.BlockSpec(memory_space=pl.ANY)] * len(left),
         out_specs=pl.BlockSpec(memory_space=pltpu.VMEM),
         scratch_shapes=[
-            pltpu.VMEM((4, rows, width, wide), jnp.float32),
+            pltpu.VMEM((4, end - begin, width, wide), jnp.float32),
             pltpu.SemaphoreType.DMA((4,)),
         ],
         compiler_params=pltpu.CompilerParams(vmem_limit_bytes=PRODUCT_BYTES),
         cost_estimate=pl.CostEstimate(flops=8 * 10**9, bytes_accessed=10**7, transcendentals=0),
-    )(picks, flags, high, low, *left)
+    )(picks, flags, *near, *left)
+
+
+def spread_kernel(layers, groups, cap, wide, src, dst):
+    for group in range(groups):
+        for slot in range(cap):
+            block = src[slot, :, group * wide : (group + 1) * wide]
+            for layer in range(layers):
+                dst[(layer * groups + group) * cap + slot] = block
+
+
+def spread(owner_blocks, layers, groups):
+    cap, width, total = owner_blocks.shape
+    wide = total // groups
+    return pl.pallas_call(
+        functools.partial(spread_kernel, layers, groups, cap, wide),
+        out_shape=jax.ShapeDtypeStruct((layers * groups * cap, width, wide), jnp.float32),
+        in_specs=[pl.BlockSpec(memory_space=pltpu.VMEM)],
+        out_specs=pl.BlockSpec(memory_space=pltpu.VMEM),
+        compiler_params=pltpu.CompilerParams(vmem_limit_bytes=PRODUCT_BYTES),
+    )(owner_blocks)
 
 
 def pick_table(block_cols, out_cols, grid_row, grid_col, core, y, z, rows, span):
@@ -325,10 +346,7 @@
     which = jnp.sum((ends[None, :] <= local[:, None]).astype(jnp.int32), axis=1)
     slot = local - (jnp.take(ends, which) - jnp.take(counts, which))
     source = which * cap + slot
-    grouped = owner_blocks.reshape(cap, width, N_GROUP, span * width).transpose(2, 0, 1, 3)
-    plain_send = jnp.tile(grouped, (N_LAYER, 1, 1, 1)).reshape(
-        N_LAYER * N_GROUP * cap, width, span * width
-    )
+    plain_send = spread(owner_blocks, N_LAYER, N_GROUP)
     plain_got = lax.all_to_all(
         plain_send, ("layer", "col"), split_axis=0, concat_axis=0, tiled=True
     )
@@ -347,7 +365,8 @@
 
     left, right = gather_first(density)
     mine = jnp.where(core == part, density, right[5])
-    partial_value = product(left, right, picks, flags)
+    tables = table(right, flags)
+    partial_value = product(left, tables, picks, flags, 0, rows)
     square = partial_value + swap_cores(partial_value)
     square = square * keep_wide
     unit = (own[:, None, :, None] * jnp.eye(width, dtype=jnp.float32)[None, :, None, :]).reshape(
@@ -357,13 +376,16 @@
     mixed = mix * unit + (4.0 - 2.0 * mix) * mine + (mix - 3.0) * square
 
     left, right = gather_second(square, mixed)
+    tables = table(right, flags)
 
     def output(layer, y, core, q, z):
         return (1 - layer, y, core, q, z) if core == layer ^ q else None
 
-    total = product(left, right, picks, flags)
-    total = total + swap_cores(total)
-    return jnp.where(core == part, total, send(total, output))
+    half = rows // 2
+    totals = [product(left, tables, picks, flags, begin, begin + half) for begin in (0, half)]
+    totals = [total + swap_cores(total) for total in totals]
+    outs = [jnp.where(core == part, total, send(total, output)) for total in totals]
+    return jnp.concatenate(outs, axis=0)
 
 
 def solution(mesh):

time: 210 us -> 204 us (0.971)
  starting transfers between devices: 52.6 us -> 49 us
  Pallas kernels: 21.8 us -> 25.2 us
  waiting for transfers between devices: 114 us -> 111 us
  local copies, waits for them, and re-layouts: 7.39 us -> 5.04 us
    ppermute x23 -> x25, waiting for transfers between devices: 99.3 us -> 95.7 us  [send(): return lax.ppermute(x, AXES, moves(target))]
    ppermute x23 -> x25, starting transfers between devices: 44 us -> 40.4 us  [send(): return lax.ppermute(x, AXES, moves(target))]
    pallas_call x2 -> x4, Pallas kernels: 15.7 us -> 19.1 us  [the longest x3 17.6 us: product(): pl.pallas_call(functools.partial(product_kernel, begin, end, width, span)...]
  transfers between devices with their start and end apart: 24 -> 26, of which waited for: 13 -> 13; matrix products, arithmetic and copies ran while one was open for 5% -> 6% of each run, Pallas kernels for 3% -> 5%
where the time goes in v4:
time: 204 us; the launch traced here: 203 us
  waiting for transfers between devices  111 us (54%)
  starting transfers between devices  49 us (24%)
  Pallas kernels  25.2 us (12%)
  other arithmetic  11.6 us (6%)
  local copies, waits for them, and re-layouts  5.04 us (2%)
    ppermute x25, waiting for transfers between devices, send(): return lax.ppermute(x, AXES, moves(target))  95.7 us
    ppermute x25, starting transfers between devices, send(): return lax.ppermute(x, AXES, moves(target))  40.4 us
    pallas_call x3, Pallas kernels, product(): pl.pallas_call(functools.partial(product_kernel, begin, end, width, span)...  17.6 us
    all_to_all x1, waiting for transfers between devices, body(): lax.all_to_all(plain_send, ('layer', 'col'), split_axis=0, concat_axis=0,...  14.9 us
    all_to_all x1, starting transfers between devices, body(): lax.all_to_all(plain_send, ('layer', 'col'), split_axis=0, concat_axis=0,...  8.56 us
    pallas_call x2, Pallas kernels, table(): pl.pallas_call(functools.partial(table_kernel, rows, width, span), out_sh...  6.09 us
    reduce_sum x1, other arithmetic, pick_table(): found = jnp.sum(hit[..., None] * right_cols[None, :, None], axis=3)  5.6 us
  transfers between devices with their start and end apart: 26, of which 13 were waited for; matrix products, arithmetic and copies ran while one was open for 6% of the time, Pallas kernels for 5%

profile of v4, /device:TPU:1, one launch (start us, length us, event | category | flops | bytes accessed | tf_op | source)
XLA Modules:
  0.0 202.6 jit_solution(16390262666835519694)
XLA Ops:
  2.7 8.6 %all-to-all-start = ((f32[32,64,256]{2,1,0:T(8,128)}), f32[32,64,256]{2,1,0:T(8,128)S(1)}, u32[]{:S(2)}, u32[]{:S(2)}) async-start(f32[32,64,256]{2,1,0:T(8,128)} %shard_map.64), calls=%async_computation | async-start | bytes 4194304 | tf_op jit(solution)/shard_map/all_to_all | solution.py:350
  14.2 5.6 %multiply_reduce_fusion = s32[20,4,4,4]{3,2,1,0:T(4,128)S(1)} fusion(s32[4,20,4]{1,2,0:T(4,128)S(1)} %multiply_reduce_fusion.2, s32[20,4,4,20]{3,2,1,0:T(4,128)S(1)} %fusion), kind=kLoop, calls=%fused_computation.6 | loop fusion | flops 49920 | bytes 32000 | tf_op jit(solution)/shard_map/reduce_sum | solution.py:320
  22.0 14.9 %all-to-all-done = f32[32,64,256]{2,1,0:T(8,128)S(1)} async-done(((f32[32,64,256]{2,1,0:T(8,128)}), f32[32,64,256]{2,1,0:T(8,128)S(1)}, u32[]{:S(2)}, u32[]{:S(2)}) %all-to-all-start) | async-done | bytes 2097184 | tf_op jit(solution)/shard_map/all_to_all | solution.py:350
  37.5 2.9 %collective-permute-start = (f32[20,64,256]{2,1,0:T(8,128)S(1)}, f32[20,64,256]{2,1,0:T(8,128)S(1)}, u32[]{:S(2)}, u32[]{:S(2)}) collective-permute-start(f32[20,64,256]{2,1,0:T(8,128)S(1)} %gather_fusion), channel_id=1, source_target_pairs={{0,8},{1,9},{2,10},{3,11},{4,12},{5,13},{6,14},{7,15},{8,0},{9,1},... | collective-permute-start | bytes 3932168 | tf_op jit(solution)/shard_map/ppermute | solution.py:47
  40.5 4.6 %collective-permute-start.5 = (f32[20,64,256]{2,1,0:T(8,128)S(1)}, f32[20,64,256]{2,1,0:T(8,128)S(1)}, u32[]{:S(2)}, u32[]{:S(2)}) collective-permute-start(f32[20,64,256]{2,1,0:T(8,128)S(1)} %gather_fusion), channel_id=1, source_target_pairs={{0,0},{1,9},{2,2},{3,11},{4,8},{5,1},{6,10},{7,3},{8,4},{9,13},{10... | collective-permute-start | bytes 3932168 | tf_op jit(solution)/shard_map/ppermute | solution.py:47
  48.8 12.3 %collective-permute-done.5.refs_0_ = f32[20,64,256]{2,1,0:T(8,128)S(1)} collective-permute-done((f32[20,64,256]{2,1,0:T(8,128)S(1)}, f32[20,64,256]{2,1,0:T(8,128)S(1)}, u32[]{:S(2)}, u32[]{:S(2)}) %collective-permute-start.5) | collective-permute-done | bytes 1310752 | tf_op jit(solution)/shard_map/ppermute | solution.py:47
  61.2 5.0 %collective-permute-start.7 = (f32[20,64,256]{2,1,0:T(8,128)S(1)}, f32[20,64,256]{2,1,0:T(8,128)S(1)}, u32[]{:S(2)}, u32[]{:S(2)}) collective-permute-start(f32[20,64,256]{2,1,0:T(8,128)S(1)} %collective-permute-done.5.refs_0_), channel_id=1, source_target_pairs={{0,1},{1,2},{2,3},{3,0},{4,5},{5,6},{6,7},{7,4},{8,9},{9,10},{10,1... | collective-permute-start | bytes 3932168 | tf_op jit(solution)/shard_map/ppermute | solution.py:47
  67.4 10.7 %collective-permute-done.2.refs_3_ = f32[20,64,256]{2,1,0:T(8,128)S(1)} collective-permute-done((f32[20,64,256]{2,1,0:T(8,128)S(1)}, f32[20,64,256]{2,1,0:T(8,128)S(1)}, u32[]{:S(2)}, u32[]{:S(2)}) %collective-permute-start.2) | collective-permute-done | bytes 1310752 | tf_op jit(solution)/shard_map/ppermute | solution.py:47
  78.4 2.7 %collective-permute-start.4 = (f32[10,64,256]{2,1,0:T(8,128)S(1)}, f32[10,64,256]{2,1,0:T(8,128)S(1)}, u32[]{:S(2)}, u32[]{:S(2)}) collective-permute-start(f32[10,64,256]{2,1,0:T(8,128)S(1)} %slice.15), channel_id=1, source_target_pairs={{0,48},{1,49},{2,50},{3,51},{4,52},{5,53},{6,54},{7,55},{8,56},{9,... | collective-permute-start | bytes 1966088 | tf_op jit(solution)/shard_map/ppermute | solution.py:47
  81.1 14.6 %collective-permute-done.3.refs_2_ = f32[10,64,256]{2,1,0:T(8,128)S(1)} collective-permute-done((f32[10,64,256]{2,1,0:T(8,128)S(1)}, f32[10,64,256]{2,1,0:T(8,128)S(1)}, u32[]{:S(2)}, u32[]{:S(2)}) %collective-permute-start.3) | collective-permute-done | bytes 655392 | tf_op jit(solution)/shard_map/ppermute | solution.py:47
  95.7 3.2 %shard_map.65 = (bf16[321,64,128]{2,1,0:T(8,128)(2,1)S(1)}, bf16[321,64,128]{2,1,0:T(8,128)(2,1)S(1)}) custom-call(s32[3]{0:T(128)S(1)} %add_convert_fusion.flag_ref, f32[20,64,256]{2,1,0:T(8,128)S(1)} %gather_fusion, f32[20,64,256]{2,1,0:T(8,128)S(1)} %collective-permute-done.1.refs_1_, f32[10,64,256]{2,1,0:T(8,128)S(1)} %collective-permute-done.3.refs_2_, ...), custom_call_target="tpu_custom_call" | custom-call | flops 4000000000 | bytes 10000000 | tf_op jit(solution)/shard_map/pallas_call | solution.py:189
  98.9 8.5 %shard_map.66 = f32[20,64,256]{2,1,0:T(8,128)} custom-call(s32[1280]{0:T(1024)S(1)} %add.221.pick_ref, s32[3]{0:T(128)S(1)} %add_convert_fusion.flag_ref, bf16[321,64,128]{2,1,0:T(8,128)(2,1)S(1)} %get-tuple-element.25.high, bf16[321,64,128]{2,1,0:T(8,128)(2,1)S(1)} %get-tuple-element.26.low, f32[20,64,256]{2,1,0:T(8,128)S(1)} %collective-permute-done.5.refs_0_, ...), custom_call_target="tpu_custom_call" | custom-call | flops 8000000000 | bytes 10000000 | tf_op jit(solution)/shard_map/pallas_call | solution.py:269
  111.6 2.4 %multiply_add_fusion = (f32[20,64,256]{2,1,0:T(8,128)S(1)}, f32[20,64,256]{2,1,0:T(8,128)S(1)}) fusion(f32[20,64,256]{2,1,0:T(8,128)S(1)} %gather_fusion, f32[20,64,256]{2,1,0:T(8,128)S(1)} %collective-permute-done.refs_5_, f32[]{:T(128)S(6)} %sub.64, f32[]{:T(128)S(6)} %sub.63, f32[64,256]{1,0:T(8,128)S(1)} %mul.176, f32[20,256]{1,0:T(8,128)S(1)} %mul.173, ...), kind=kLoop, calls=%fused_computation.4 | loop fusion | flops 2949120 | bytes 7970829 | tf_op jit(solution)/shard_map/add | solution.py:376
  115.7 2.8 %collective-permute-start.16 = (f32[20,64,256]{2,1,0:T(8,128)S(1)}, f32[20,64,256]{2,1,0:T(8,128)S(1)}, u32[]{:S(2)}, u32[]{:S(2)}) collective-permute-start(f32[20,64,256]{2,1,0:T(8,128)S(1)} %get-tuple-element.35), channel_id=1, source_target_pairs={{0,68},{1,9},{2,70},{3,11},{4,12},{5,65},{6,14},{7,67},{8,0},{9,77... | collective-permute-start | bytes 3932168 | tf_op jit(solution)/shard_map/ppermute | solution.py:47
  119.3 12.4 %collective-permute-done.11.refs_0_ = f32[20,64,256]{2,1,0:T(8,128)S(1)} collective-permute-done((f32[20,64,256]{2,1,0:T(8,128)S(1)}, f32[20,64,256]{2,1,0:T(8,128)S(1)}, u32[]{:S(2)}, u32[]{:S(2)}) %collective-permute-start.11) | collective-permute-done | bytes 1310752 | tf_op jit(solution)/shard_map/ppermute | solution.py:47
  131.7 2.9 %collective-permute-done.13.refs_2_ = f32[20,64,256]{2,1,0:T(8,128)S(1)} collective-permute-done((f32[20,64,256]{2,1,0:T(8,128)S(1)}, f32[20,64,256]{2,1,0:T(8,128)S(1)}, u32[]{:S(2)}, u32[]{:S(2)}) %collective-permute-start.13) | collective-permute-done | bytes 1310752 | tf_op jit(solution)/shard_map/ppermute | solution.py:47
  141.4 9.6 %collective-permute-done.15.refs_4_ = f32[20,64,256]{2,1,0:T(8,128)S(1)} collective-permute-done((f32[20,64,256]{2,1,0:T(8,128)S(1)}, f32[20,64,256]{2,1,0:T(8,128)S(1)}, u32[]{:S(2)}, u32[]{:S(2)}) %collective-permute-start.15) | collective-permute-done | bytes 1310752 | tf_op jit(solution)/shard_map/ppermute | solution.py:47
  152.2 13.9 %collective-permute-done.12.refs_1_ = f32[20,64,256]{2,1,0:T(8,128)S(1)} collective-permute-done((f32[20,64,256]{2,1,0:T(8,128)S(1)}, f32[20,64,256]{2,1,0:T(8,128)S(1)}, u32[]{:S(2)}, u32[]{:S(2)}) %collective-permute-start.12) | collective-permute-done | bytes 1310752 | tf_op jit(solution)/shard_map/ppermute | solution.py:47
  166.1 2.9 %shard_map.67 = (bf16[321,64,128]{2,1,0:T(8,128)(2,1)S(1)}, bf16[321,64,128]{2,1,0:T(8,128)(2,1)S(1)}) custom-call(s32[3]{0:T(128)S(1)} %add_convert_fusion.flag_ref, f32[20,64,256]{2,1,0:T(8,128)S(1)} %collective-permute-done.11.refs_0_, f32[20,64,256]{2,1,0:T(8,128)S(1)} %collective-permute-done.12.refs_1_, ...), custom_call_target="tpu_custom_call" | custom-call | flops 4000000000 | bytes 10000000 | tf_op jit(solution)/shard_map/pallas_call | solution.py:189
  170.8 4.6 %shard_map.69 = f32[10,64,256]{2,1,0:T(8,128)S(1)} custom-call(s32[1280]{0:T(1024)S(1)} %add.221.pick_ref, s32[3]{0:T(128)S(1)} %add_convert_fusion.flag_ref, bf16[321,64,128]{2,1,0:T(8,128)(2,1)S(1)} %get-tuple-element.30.high, bf16[321,64,128]{2,1,0:T(8,128)(2,1)S(1)} %get-tuple-element.31.low, f32[20,64,256]{2,1,0:T(8,128)S(1)} %collective-permute-done.16.refs_0_, ...), custom_call_target="tpu_custom_call" | custom-call | flops 8000000000 | bytes 10000000 | tf_op jit(solution)/shard_map/pallas_call | solution.py:269
  175.4 2.9 %collective-permute-start.23 = (f32[10,64,256]{2,1,0:T(8,128)S(1)}, f32[10,64,256]{2,1,0:T(8,128)S(1)}, u32[]{:S(2)}, u32[]{:S(2)}) collective-permute-start(f32[10,64,256]{2,1,0:T(8,128)S(1)} %shard_map.69), channel_id=1, source_target_pairs={{0,8},{1,9},{2,10},{3,11},{4,12},{5,13},{6,14},{7,15},{8,0},{9,1},... | collective-permute-start | bytes 1966088 | tf_op jit(solution)/shard_map/ppermute | solution.py:47
  178.3 4.6 %shard_map.68 = f32[10,64,256]{2,1,0:T(8,128)S(1)} custom-call(s32[1280]{0:T(1024)S(1)} %add.221.pick_ref, s32[3]{0:T(128)S(1)} %add_convert_fusion.flag_ref, bf16[321,64,128]{2,1,0:T(8,128)(2,1)S(1)} %get-tuple-element.30.high, bf16[321,64,128]{2,1,0:T(8,128)(2,1)S(1)} %get-tuple-element.31.low, f32[20,64,256]{2,1,0:T(8,128)S(1)} %collective-permute-done.16.refs_0_, ...), custom_call_target="tpu_custom_call" | custom-call | flops 8000000000 | bytes 10000000 | tf_op jit(solution)/shard_map/pallas_call | solution.py:269
  186.4 8.0 %collective-permute-done.24 = f32[10,64,256]{2,1,0:T(8,128)S(1)} collective-permute-done((f32[10,64,256]{2,1,0:T(8,128)S(1)}, f32[10,64,256]{2,1,0:T(8,128)S(1)}, u32[]{:S(2)}, u32[]{:S(2)}) %collective-permute-start.24) | collective-permute-done | bytes 655392 | tf_op jit(solution)/shard_map/ppermute | solution.py:47
  194.5 6.9 %collective-permute-done.22 = f32[10,64,256]{2,1,0:T(8,128)S(1)} collective-permute-done((f32[10,64,256]{2,1,0:T(8,128)S(1)}, f32[10,64,256]{2,1,0:T(8,128)S(1)}, u32[]{:S(2)}, u32[]{:S(2)}) %collective-permute-start.22) | collective-permute-done | bytes 655392 | tf_op jit(solution)/shard_map/ppermute | solution.py:47
  (98 shorter events, 34.1 us)
Async XLA Ops:
  2.7 34.2 %all-to-all-start = ((f32[32,64,256]{2,1,0:T(8,128)}), f32[32,64,256]{2,1,0:T(8,128)S(1)}, u32[]{:S(2)}, u32[]{:S(2)}) async-start(f32[32,64,256]{2,1,0:T(8,128)} %shard_map.64), calls=%async_computation | async-start | bytes 4194304 | tf_op jit(solution)/shard_map/all_to_all | solution.py:350
  37.5 11.3 %collective-permute-start = (f32[20,64,256]{2,1,0:T(8,128)S(1)}, f32[20,64,256]{2,1,0:T(8,128)S(1)}, u32[]{:S(2)}, u32[]{:S(2)}) collective-permute-start(f32[20,64,256]{2,1,0:T(8,128)S(1)} %gather_fusion), channel_id=1, source_target_pairs={{0,8},{1,9},{2,10},{3,11},{4,12},{5,13},{6,14},{7,15},{8,0},{9,1},... | collective-permute-start | bytes 3932168 | tf_op jit(solution)/shard_map/ppermute | solution.py:47
  40.5 20.7 %collective-permute-start.5 = (f32[20,64,256]{2,1,0:T(8,128)S(1)}, f32[20,64,256]{2,1,0:T(8,128)S(1)}, u32[]{:S(2)}, u32[]{:S(2)}) collective-permute-start(f32[20,64,256]{2,1,0:T(8,128)S(1)} %gather_fusion), channel_id=1, source_target_pairs={{0,0},{1,9},{2,2},{3,11},{4,8},{5,1},{6,10},{7,3},{8,4},{9,13},{10... | collective-permute-start | bytes 3932168 | tf_op jit(solution)/shard_map/ppermute | solution.py:47
  45.0 16.1 %collective-permute-start.6 = (f32[20,64,256]{2,1,0:T(8,128)S(1)}, f32[20,64,256]{2,1,0:T(8,128)S(1)}, u32[]{:S(2)}, u32[]{:S(2)}) collective-permute-start(f32[20,64,256]{2,1,0:T(8,128)S(1)} %gather_fusion), channel_id=1, source_target_pairs={{0,2},{1,11},{2,0},{3,9},{12,14},{13,7},{14,12},{15,5},{16,18},{17... | collective-permute-start | bytes 3932168 | tf_op jit(solution)/shard_map/ppermute | solution.py:47
  45.8 32.4 %collective-permute-start.2 = (f32[20,64,256]{2,1,0:T(8,128)S(1)}, f32[20,64,256]{2,1,0:T(8,128)S(1)}, u32[]{:S(2)}, u32[]{:S(2)}) collective-permute-start(f32[20,64,256]{2,1,0:T(8,128)S(1)} %gather_fusion), channel_id=1, source_target_pairs={{0,16},{1,17},{2,18},{3,19},{4,20},{5,21},{6,22},{7,23},{8,24},{9,... | collective-permute-start | bytes 3932168 | tf_op jit(solution)/shard_map/ppermute | solution.py:47
  47.2 31.1 %collective-permute-start.1 = (f32[20,64,256]{2,1,0:T(8,128)S(1)}, f32[20,64,256]{2,1,0:T(8,128)S(1)}, u32[]{:S(2)}, u32[]{:S(2)}) collective-permute-start(f32[20,64,256]{2,1,0:T(8,128)S(1)} %gather_fusion), channel_id=1, source_target_pairs={{0,48},{1,49},{2,50},{3,51},{4,52},{5,53},{6,54},{7,55},{8,56},{9,... | collective-permute-start | bytes 3932168 | tf_op jit(solution)/shard_map/ppermute | solution.py:47
  61.2 37.7 %collective-permute-start.7 = (f32[20,64,256]{2,1,0:T(8,128)S(1)}, f32[20,64,256]{2,1,0:T(8,128)S(1)}, u32[]{:S(2)}, u32[]{:S(2)}) collective-permute-start(f32[20,64,256]{2,1,0:T(8,128)S(1)} %collective-permute-done.5.refs_0_), channel_id=1, source_target_pairs={{0,1},{1,2},{2,3},{3,0},{4,5},{5,6},{6,7},{7,4},{8,9},{9,10},{10,1... | collective-permute-start | bytes 3932168 | tf_op jit(solution)/shard_map/ppermute | solution.py:47
  66.1 32.8 %collective-permute-start.8 = (f32[20,64,256]{2,1,0:T(8,128)S(1)}, f32[20,64,256]{2,1,0:T(8,128)S(1)}, u32[]{:S(2)}, u32[]{:S(2)}) collective-permute-start(f32[20,64,256]{2,1,0:T(8,128)S(1)} %collective-permute-done.5.refs_0_), channel_id=1, source_target_pairs={{0,3},{1,0},{2,1},{3,2},{4,7},{5,4},{6,5},{7,6},{8,11},{9,8},{10,9... | collective-permute-start | bytes 3932168 | tf_op jit(solution)/shard_map/ppermute | solution.py:47
  66.1 32.8 %collective-permute-start.9 = (f32[20,64,256]{2,1,0:T(8,128)S(1)}, f32[20,64,256]{2,1,0:T(8,128)S(1)}, u32[]{:S(2)}, u32[]{:S(2)}) collective-permute-start(f32[20,64,256]{2,1,0:T(8,128)S(1)} %collective-permute-done.6.refs_3_), channel_id=1, source_target_pairs={{0,68},{2,70},{5,65},{7,67},{9,77},{11,79},{12,72},{14,74},{16,84}... | collective-permute-start | bytes 3932168 | tf_op jit(solution)/shard_map/ppermute | solution.py:47
  78.2 17.5 %collective-permute-start.3 = (f32[10,64,256]{2,1,0:T(8,128)S(1)}, f32[10,64,256]{2,1,0:T(8,128)S(1)}, u32[]{:S(2)}, u32[]{:S(2)}) collective-permute-start(f32[10,64,256]{2,1,0:T(8,128)S(1)} %slice.14), channel_id=1, source_target_pairs={{0,16},{1,17},{2,18},{3,19},{4,20},{5,21},{6,22},{7,23},{8,24},{9,... | collective-permute-start | bytes 1966088 | tf_op jit(solution)/shard_map/ppermute | solution.py:47
  78.4 17.3 %collective-permute-start.4 = (f32[10,64,256]{2,1,0:T(8,128)S(1)}, f32[10,64,256]{2,1,0:T(8,128)S(1)}, u32[]{:S(2)}, u32[]{:S(2)}) collective-permute-start(f32[10,64,256]{2,1,0:T(8,128)S(1)} %slice.15), channel_id=1, source_target_pairs={{0,48},{1,49},{2,50},{3,51},{4,52},{5,53},{6,54},{7,55},{8,56},{9,... | collective-permute-start | bytes 1966088 | tf_op jit(solution)/shard_map/ppermute | solution.py:47
  114.0 17.7 %collective-permute-start.11 = (f32[20,64,256]{2,1,0:T(8,128)S(1)}, f32[20,64,256]{2,1,0:T(8,128)S(1)}, u32[]{:S(2)}, u32[]{:S(2)}) collective-permute-start(f32[20,64,256]{2,1,0:T(8,128)S(1)} %get-tuple-element.34), channel_id=1, source_target_pairs={{0,64},{1,65},{2,66},{3,67},{4,12},{5,13},{6,14},{7,15},{8,0},{9,1... | collective-permute-start | bytes 3932168 | tf_op jit(solution)/shard_map/ppermute | solution.py:47
  114.4 20.1 %collective-permute-start.13 = (f32[20,64,256]{2,1,0:T(8,128)S(1)}, f32[20,64,256]{2,1,0:T(8,128)S(1)}, u32[]{:S(2)}, u32[]{:S(2)}) collective-permute-start(f32[20,64,256]{2,1,0:T(8,128)S(1)} %get-tuple-element.34), channel_id=1, source_target_pairs={{0,32},{1,33},{2,34},{3,35},{12,44},{13,45},{14,46},{15,47},{16,48... | collective-permute-start | bytes 3932168 | tf_op jit(solution)/shard_map/ppermute | solution.py:47
  115.7 23.0 %collective-permute-start.16 = (f32[20,64,256]{2,1,0:T(8,128)S(1)}, f32[20,64,256]{2,1,0:T(8,128)S(1)}, u32[]{:S(2)}, u32[]{:S(2)}) collective-permute-start(f32[20,64,256]{2,1,0:T(8,128)S(1)} %get-tuple-element.35), channel_id=1, source_target_pairs={{0,68},{1,9},{2,70},{3,11},{4,12},{5,65},{6,14},{7,67},{8,0},{9,77... | collective-permute-start | bytes 3932168 | tf_op jit(solution)/shard_map/ppermute | solution.py:47
  118.6 20.9 %collective-permute-start.19 = (f32[20,64,256]{2,1,0:T(8,128)S(1)}, f32[20,64,256]{2,1,0:T(8,128)S(1)}, u32[]{:S(2)}, u32[]{:S(2)}) collective-permute-start(f32[20,64,256]{2,1,0:T(8,128)S(1)} %get-tuple-element.35), channel_id=1, source_target_pairs={{0,2},{2,0},{5,7},{7,5},{9,11},{11,9},{12,14},{14,12},{16,18},{18,... | collective-permute-start | bytes 3932168 | tf_op jit(solution)/shard_map/ppermute | solution.py:47
  134.6 16.3 %collective-permute-start.15 = (f32[20,64,256]{2,1,0:T(8,128)S(1)}, f32[20,64,256]{2,1,0:T(8,128)S(1)}, u32[]{:S(2)}, u32[]{:S(2)}) collective-permute-start(f32[20,64,256]{2,1,0:T(8,128)S(1)} %collective-permute-done.13.refs_2_), channel_id=1, source_target_pairs={{4,68},{5,69},{6,70},{7,71},{8,72},{9,73},{10,74},{11,75},{20,84},... | collective-permute-start | bytes 3932168 | tf_op jit(solution)/shard_map/ppermute | solution.py:47
  136.5 29.7 %collective-permute-start.12 = (f32[20,64,256]{2,1,0:T(8,128)S(1)}, f32[20,64,256]{2,1,0:T(8,128)S(1)}, u32[]{:S(2)}, u32[]{:S(2)}) collective-permute-start(f32[20,64,256]{2,1,0:T(8,128)S(1)} %collective-permute-done.11.refs_0_), channel_id=1, source_target_pairs={{0,48},{1,49},{2,50},{3,51},{4,52},{5,53},{6,54},{7,55},{8,56},{9,... | collective-permute-start | bytes 3932168 | tf_op jit(solution)/shard_map/ppermute | solution.py:47
  136.6 29.6 %collective-permute-start.14 = (f32[20,64,256]{2,1,0:T(8,128)S(1)}, f32[20,64,256]{2,1,0:T(8,128)S(1)}, u32[]{:S(2)}, u32[]{:S(2)}) collective-permute-start(f32[20,64,256]{2,1,0:T(8,128)S(1)} %collective-permute-done.11.refs_0_), channel_id=1, source_target_pairs={{0,16},{1,17},{2,18},{3,19},{4,20},{5,21},{6,22},{7,23},{8,24},{9,... | collective-permute-start | bytes 3932168 | tf_op jit(solution)/shard_map/ppermute | solution.py:47
  138.7 30.3 %collective-permute-start.17 = (f32[20,64,256]{2,1,0:T(8,128)S(1)}, f32[20,64,256]{2,1,0:T(8,128)S(1)}, u32[]{:S(2)}, u32[]{:S(2)}) collective-permute-start(f32[20,64,256]{2,1,0:T(8,128)S(1)} %collective-permute-done.16.refs_0_), channel_id=1, source_target_pairs={{0,1},{1,2},{2,3},{3,0},{4,5},{5,6},{6,7},{7,4},{8,9},{9,10},{10,1... | collective-permute-start | bytes 3932168 | tf_op jit(solution)/shard_map/ppermute | solution.py:47
  139.5 29.5 %collective-permute-start.18 = (f32[20,64,256]{2,1,0:T(8,128)S(1)}, f32[20,64,256]{2,1,0:T(8,128)S(1)}, u32[]{:S(2)}, u32[]{:S(2)}) collective-permute-start(f32[20,64,256]{2,1,0:T(8,128)S(1)} %collective-permute-done.16.refs_0_), channel_id=1, source_target_pairs={{0,3},{1,0},{2,1},{3,2},{4,7},{5,4},{6,5},{7,6},{8,11},{9,8},{10,9... | collective-permute-start | bytes 3932168 | tf_op jit(solution)/shard_map/ppermute | solution.py:47
  150.9 19.8 %collective-permute-start.20 = (f32[20,64,256]{2,1,0:T(8,128)S(1)}, f32[20,64,256]{2,1,0:T(8,128)S(1)}, u32[]{:S(2)}, u32[]{:S(2)}) collective-permute-start(f32[20,64,256]{2,1,0:T(8,128)S(1)} %collective-permute-done.19.refs_3_), channel_id=1, source_target_pairs={{0,68},{2,70},{5,65},{7,67},{9,77},{11,79},{12,72},{14,74},{16,84}... | collective-permute-start | bytes 3932168 | tf_op jit(solution)/shard_map/ppermute | solution.py:47
  175.4 7.6 %collective-permute-start.23 = (f32[10,64,256]{2,1,0:T(8,128)S(1)}, f32[10,64,256]{2,1,0:T(8,128)S(1)}, u32[]{:S(2)}, u32[]{:S(2)}) collective-permute-start(f32[10,64,256]{2,1,0:T(8,128)S(1)} %shard_map.69), channel_id=1, source_target_pairs={{0,8},{1,9},{2,10},{3,11},{4,12},{5,13},{6,14},{7,15},{8,0},{9,1},... | collective-permute-start | bytes 1966088 | tf_op jit(solution)/shard_map/ppermute | solution.py:47
  183.1 11.3 %collective-permute-start.24 = (f32[10,64,256]{2,1,0:T(8,128)S(1)}, f32[10,64,256]{2,1,0:T(8,128)S(1)}, u32[]{:S(2)}, u32[]{:S(2)}) collective-permute-start(f32[10,64,256]{2,1,0:T(8,128)S(1)} %add.233), channel_id=1, source_target_pairs={{0,64},{1,65},{2,66},{3,67},{12,76},{13,77},{14,78},{15,79},{16,80... | collective-permute-start | bytes 1966088 | tf_op jit(solution)/shard_map/ppermute | solution.py:47
  185.1 16.3 %collective-permute-start.22 = (f32[10,64,256]{2,1,0:T(8,128)S(1)}, f32[10,64,256]{2,1,0:T(8,128)S(1)}, u32[]{:S(2)}, u32[]{:S(2)}) collective-permute-start(f32[10,64,256]{2,1,0:T(8,128)S(1)} %add.232), channel_id=1, source_target_pairs={{0,64},{1,65},{2,66},{3,67},{12,76},{13,77},{14,78},{15,79},{16,80... | collective-permute-start | bytes 1966088 | tf_op jit(solution)/shard_map/ppermute | solution.py:47
  (6 other events, 34.4 us)

commit v5 on v4

--- a/solution.py
+++ b/solution.py
@@ -122,58 +122,53 @@
     return (left, left_below, left_above, left_across, left_pair), (own, above, across, below, pair)
 
 
-def table_kernel(rows, width, span, flag_ref, *refs):
-    right = refs[:-4]
-    high, low, right_buf, right_sem = refs[-4:]
-
-    def bring(place, src):
-        return pltpu.make_async_copy(src, right_buf.at[place], right_sem.at[place])
-
-    for place in (1, 3):
-        bring(place, right[place]).start()
-
-    half = right[2].shape[0]
-    if half < rows:
-        first = pltpu.make_async_copy(right[2], right_buf.at[2, pl.ds(0, half)], right_sem.at[2])
-        second = pltpu.make_async_copy(right[4], right_buf.at[2, pl.ds(half, half)], right_sem.at[4])
-        first.start()
-        second.start()
-
-        @pl.when(flag_ref[2] == 0)
-        def _():
-            bring(0, right[0]).start()
-
-        @pl.when(flag_ref[2] == 1)
-        def _():
-            bring(0, right[5]).start()
-    else:
-        bring(0, right[0]).start()
-
-        @pl.when(flag_ref[1] == 1)
-        def _():
-            bring(2, right[2]).start()
-
-        @pl.when(flag_ref[1] == 0)
-        def _():
-            bring(2, right[4]).start()
-
-    none = 4 * rows * span
-    high[none] = jnp.zeros(high.shape[1:], high.dtype)
-    low[none] = jnp.zeros(low.shape[1:], low.dtype)
-
-    for place in (1, 3, 0, 2):
-        if place == 2 and half < rows:
-            first.wait()
-            second.wait()
+def table_kernel(rows, width, span, jobs, count, fresh, flag_ref, *refs):
+    source = refs[:count]
+    high, low, buf, sem = refs[-4:]
+    half = rows // 2
+    starts = []
+    for job, (place, names, flag) in enumerate(jobs):
+        whole = pltpu.make_async_copy(source[names[0]], buf.at[job], sem.at[job, 0])
+        if len(names) == 1:
+            whole.start()
+            starts.append([whole])
+        elif flag is None:
+            parts = [
+                pltpu.make_async_copy(
+                    source[name], buf.at[job, pl.ds(part * half, half)], sem.at[job, part]
+                )
+                for part, name in enumerate(names)
+            ]
+            for copy in parts:
+                copy.start()
+            starts.append(parts)
         else:
-            bring(place, right[place]).wait()
+
+            @pl.when(flag_ref[flag] == 1)
+            def _():
+                whole.start()
+
+            @pl.when(flag_ref[flag] == 0)
+            def _():
+                pltpu.make_async_copy(source[names[1]], buf.at[job], sem.at[job, 0]).start()
+
+            starts.append([whole])
+
+    if fresh:
+        none = 4 * rows * span
+        high[none] = jnp.zeros(high.shape[1:], high.dtype)
+        low[none] = jnp.zeros(low.shape[1:], low.dtype)
+
+    for job, (place, names, flag) in enumerate(jobs):
+        for copy in starts[job]:
+            copy.wait()
 
         @pl.loop(0, rows // TABLE_STEP)
         def _(step):
             for j in range(TABLE_STEP):
                 row = step * TABLE_STEP + j
                 at = (place * rows + row) * span
-                x = right_buf[place, row]
+                x = buf[job, row]
                 for v in range(2):
                     piece = x[:, v * 2 * width : (v + 1) * 2 * width]
                     for swap, part in enumerate((piece, pltpu.roll(piece, width, 1))):
@@ -182,34 +177,38 @@
                         low[at + 2 * v + swap] = (part - top.astype(jnp.float32)).astype(jnp.bfloat16)
 
 
-def table(right, flags):
-    rows, width, wide = right[0].shape
+def table(panels, jobs, flags, rows, before=()):
+    width, wide = panels[0].shape[1:]
     span = wide // width
+    count = len(panels)
     kind = pltpu.VMEM((4 * rows * span + 1, width, 2 * width), jnp.bfloat16)
+    near = [pltpu.with_memory_space_constraint(x, pltpu.VMEM) for x in before]
     return pl.pallas_call(
-        functools.partial(table_kernel, rows, width, span),
+        functools.partial(table_kernel, rows, width, span, jobs, count, not before),
         out_shape=(kind, kind),
         in_specs=[pl.BlockSpec(memory_space=pltpu.SMEM)]
-        + [pl.BlockSpec(memory_space=pl.ANY)] * len(right),
+        + [pl.BlockSpec(memory_space=pl.ANY)] * count
+        + [pl.BlockSpec(memory_space=pltpu.VMEM)] * len(before),
         out_specs=(pl.BlockSpec(memory_space=pltpu.VMEM),) * 2,
         scratch_shapes=[
-            pltpu.VMEM((4, rows, width, wide), jnp.float32),
-            pltpu.SemaphoreType.DMA((5,)),
+            pltpu.VMEM((len(jobs), rows, width, wide), jnp.float32),
+            pltpu.SemaphoreType.DMA((len(jobs), 2)),
         ],
+        input_output_aliases={1 + count + i: i for i in range(len(before))},
         compiler_params=pltpu.CompilerParams(vmem_limit_bytes=TABLE_BYTES),
-        cost_estimate=pl.CostEstimate(flops=4 * 10**9, bytes_accessed=10**7, transcendentals=0),
-    )(flags, *right)
-
-
-def product_kernel(begin, end, width, span, pick_ref, flag_ref, high, low, *refs):
+        cost_estimate=pl.CostEstimate(flops=2 * 10**9, bytes_accessed=10**7, transcendentals=0),
+    )(flags, *panels, *near)
+
+
+def product_kernel(first, begin, end, width, span, pick_ref, flag_ref, high, low, *refs):
     left = refs[:5]
     out_ref, left_buf, left_sem = refs[5:]
 
     def bring(place, src):
         rows_here = src.at[pl.ds(begin, end - begin)]
-        return pltpu.make_async_copy(rows_here, left_buf.at[place], left_sem.at[place])
-
-    for place in (0, 1, 2):
+        return pltpu.make_async_copy(rows_here, left_buf.at[place - first], left_sem.at[place - first])
+
+    for place in range(first, 3):
         bring(place, left[place]).start()
 
     @pl.when(flag_ref[0] == 1)
@@ -220,8 +219,8 @@
     def _():
         bring(3, left[4]).start()
 
-    for place in range(4):
-        bring(place, left[0]).wait()
+    for place in range(first, 4):
+        bring(place, left[3]).wait()
 
     lane = lax.broadcasted_iota(jnp.int32, (width, 2 * width), 1) < width
 
@@ -243,7 +242,7 @@
                             axis=1,
                         )
                     )
-            x = left_buf[place, row - begin]
+            x = left[place][row] if place < first else left_buf[place - first, row - begin]
             top = x.astype(jnp.bfloat16)
             rest = (x - top.astype(jnp.float32)).astype(jnp.bfloat16)
             both += jnp.dot(
@@ -262,24 +261,24 @@
             one_row(begin + step * ROW_STEP + j)
 
 
-def product(left, tables, picks, flags, begin, end):
+def product(left, tables, picks, flags, begin, end, first=0):
     rows, width, wide = left[0].shape
     span = wide // width
-    near = [pltpu.with_memory_space_constraint(x, pltpu.VMEM) for x in tables]
+    near = [pltpu.with_memory_space_constraint(x, pltpu.VMEM) for x in (*tables, *left[:first])]
     return pl.pallas_call(
-        functools.partial(product_kernel, begin, end, width, span),
+        functools.partial(product_kernel, first, begin, end, width, span),
         out_shape=jax.ShapeDtypeStruct((end - begin, width, wide), jnp.float32),
         in_specs=[pl.BlockSpec(memory_space=pltpu.SMEM)] * 2
         + [pl.BlockSpec(memory_space=pltpu.VMEM)] * len(near)
-        + [pl.BlockSpec(memory_space=pl.ANY)] * len(left),
+        + [pl.BlockSpec(memory_space=pl.ANY)] * (5 - first),
         out_specs=pl.BlockSpec(memory_space=pltpu.VMEM),
         scratch_shapes=[
-            pltpu.VMEM((4, end - begin, width, wide), jnp.float32),
-            pltpu.SemaphoreType.DMA((4,)),
+            pltpu.VMEM((4 - first, end - begin, width, wide), jnp.float32),
+            pltpu.SemaphoreType.DMA((4 - first,)),
         ],
         compiler_params=pltpu.CompilerParams(vmem_limit_bytes=PRODUCT_BYTES),
         cost_estimate=pl.CostEstimate(flops=8 * 10**9, bytes_accessed=10**7, transcendentals=0),
-    )(picks, flags, *near, *left)
+    )(picks, flags, *near, *left[first:])
 
 
 def spread_kernel(layers, groups, cap, wide, src, dst):
@@ -365,7 +364,10 @@
 
     left, right = gather_first(density)
     mine = jnp.where(core == part, density, right[5])
-    tables = table(right, flags)
+    density, above, first, below, second, swapped = right
+    jobs = ((0, (0, 1), 2), (1, (2,), None), (3, (3,), None))
+    tables = table((swapped, density, above, below), jobs, flags, rows)
+    tables = table((first, second), ((2, (0, 1), None),), flags, rows, tables)
     partial_value = product(left, tables, picks, flags, 0, rows)
     square = partial_value + swap_cores(partial_value)
     square = square * keep_wide
@@ -376,13 +378,16 @@
     mixed = mix * unit + (4.0 - 2.0 * mix) * mine + (mix - 3.0) * square
 
     left, right = gather_second(square, mixed)
-    tables = table(right, flags)
+    own_right, above, across, below, pair = right
+    jobs = ((0, (0,), None), (2, (1, 2), 1))
+    tables = table((own_right, across, pair), jobs, flags, rows)
+    tables = table((above, below), ((1, (0,), None), (3, (1,), None)), flags, rows, tables)
 
     def output(layer, y, core, q, z):
         return (1 - layer, y, core, q, z) if core == layer ^ q else None
 
     half = rows // 2
-    totals = [product(left, tables, picks, flags, begin, begin + half) for begin in (0, half)]
+    totals = [product(left, tables, picks, flags, begin, begin + half, 3) for begin in (0, half)]
     totals = [total + swap_cores(total) for total in totals]
     outs = [jnp.where(core == part, total, send(total, output)) for total in totals]
     return jnp.concatenate(outs, axis=0)

time: 204 us -> 201 us (0.985)
  waiting for transfers between devices: 111 us -> 108 us
    ppermute x25, waiting for transfers between devices: 95.7 us -> 92.8 us  [send(): return lax.ppermute(x, AXES, moves(target))]
    pallas_call x5 -> x7, Pallas kernels: 23.7 us -> 23.6 us  [the longest x3 16.3 us: product(): pl.pallas_call(functools.partial(product_kernel, first, begin, end, width...]
  transfers between devices with their start and end apart: 26 -> 26, of which waited for: 13 -> 14; matrix products, arithmetic and copies ran while one was open for 6% -> 6% of each run, Pallas kernels for 5% -> 6%
where the time goes in v5:
time: 201 us; the launch traced here: 200 us
  waiting for transfers between devices  108 us (54%)
  starting transfers between devices  49 us (24%)
  Pallas kernels  25.1 us (12%)
  other arithmetic  11.6 us (6%)
  local copies, waits for them, and re-layouts  5.04 us (3%)
    ppermute x25, waiting for transfers between devices, send(): return lax.ppermute(x, AXES, moves(target))  92.8 us
    ppermute x25, starting transfers between devices, send(): return lax.ppermute(x, AXES, moves(target))  40.4 us
    pallas_call x3, Pallas kernels, product(): pl.pallas_call(functools.partial(product_kernel, first, begin, end, width...  16.3 us
    all_to_all x1, waiting for transfers between devices, body(): lax.all_to_all(plain_send, ('layer', 'col'), split_axis=0, concat_axis=0,...  14.9 us
    all_to_all x1, starting transfers between devices, body(): lax.all_to_all(plain_send, ('layer', 'col'), split_axis=0, concat_axis=0,...  8.56 us
    pallas_call x4, Pallas kernels, table(): pl.pallas_call(functools.partial(table_kernel, rows, width, span, jobs, c...  7.23 us
    reduce_sum x1, other arithmetic, pick_table(): found = jnp.sum(hit[..., None] * right_cols[None, :, None], axis=3)  5.6 us
  transfers between devices with their start and end apart: 26, of which 14 were waited for; matrix products, arithmetic and copies ran while one was open for 6% of the time, Pallas kernels for 6%

profile of v5, /device:TPU:1, one launch (start us, length us, event | category | flops | bytes accessed | tf_op | source)
XLA Modules:
  0.0 199.6 jit_solution(8996451566890535128)
XLA Ops:
  2.7 8.6 %all-to-all-start = ((f32[32,64,256]{2,1,0:T(8,128)}), f32[32,64,256]{2,1,0:T(8,128)S(1)}, u32[]{:S(2)}, u32[]{:S(2)}) async-start(f32[32,64,256]{2,1,0:T(8,128)} %shard_map.64), calls=%async_computation | async-start | bytes 4194304 | tf_op jit(solution)/shard_map/all_to_all | solution.py:349
  14.2 5.6 %multiply_reduce_fusion = s32[20,4,4,4]{3,2,1,0:T(4,128)S(1)} fusion(s32[4,20,4]{1,2,0:T(4,128)S(1)} %multiply_reduce_fusion.2, s32[20,4,4,20]{3,2,1,0:T(4,128)S(1)} %fusion), kind=kLoop, calls=%fused_computation.6 | loop fusion | flops 49920 | bytes 32000 | tf_op jit(solution)/shard_map/reduce_sum | solution.py:319
  22.0 14.9 %all-to-all-done = f32[32,64,256]{2,1,0:T(8,128)S(1)} async-done(((f32[32,64,256]{2,1,0:T(8,128)}), f32[32,64,256]{2,1,0:T(8,128)S(1)}, u32[]{:S(2)}, u32[]{:S(2)}) %all-to-all-start) | async-done | bytes 2097184 | tf_op jit(solution)/shard_map/all_to_all | solution.py:349
  37.5 2.9 %collective-permute-start = (f32[20,64,256]{2,1,0:T(8,128)S(1)}, f32[20,64,256]{2,1,0:T(8,128)S(1)}, u32[]{:S(2)}, u32[]{:S(2)}) collective-permute-start(f32[20,64,256]{2,1,0:T(8,128)S(1)} %gather_fusion), channel_id=1, source_target_pairs={{0,8},{1,9},{2,10},{3,11},{4,12},{5,13},{6,14},{7,15},{8,0},{9,1},... | collective-permute-start | bytes 3932168 | tf_op jit(solution)/shard_map/ppermute | solution.py:47
  40.5 4.6 %collective-permute-start.5 = (f32[20,64,256]{2,1,0:T(8,128)S(1)}, f32[20,64,256]{2,1,0:T(8,128)S(1)}, u32[]{:S(2)}, u32[]{:S(2)}) collective-permute-start(f32[20,64,256]{2,1,0:T(8,128)S(1)} %gather_fusion), channel_id=1, source_target_pairs={{0,0},{1,9},{2,2},{3,11},{4,8},{5,1},{6,10},{7,3},{8,4},{9,13},{10... | collective-permute-start | bytes 3932168 | tf_op jit(solution)/shard_map/ppermute | solution.py:47
  48.8 12.3 %collective-permute-done.5.refs_0_ = f32[20,64,256]{2,1,0:T(8,128)S(1)} collective-permute-done((f32[20,64,256]{2,1,0:T(8,128)S(1)}, f32[20,64,256]{2,1,0:T(8,128)S(1)}, u32[]{:S(2)}, u32[]{:S(2)}) %collective-permute-start.5) | collective-permute-done | bytes 1310752 | tf_op jit(solution)/shard_map/ppermute | solution.py:47
  61.2 5.0 %collective-permute-start.7 = (f32[20,64,256]{2,1,0:T(8,128)S(1)}, f32[20,64,256]{2,1,0:T(8,128)S(1)}, u32[]{:S(2)}, u32[]{:S(2)}) collective-permute-start(f32[20,64,256]{2,1,0:T(8,128)S(1)} %collective-permute-done.5.refs_0_), channel_id=1, source_target_pairs={{0,1},{1,2},{2,3},{3,0},{4,5},{5,6},{6,7},{7,4},{8,9},{9,10},{10,1... | collective-permute-start | bytes 3932168 | tf_op jit(solution)/shard_map/ppermute | solution.py:47
  67.4 10.7 %collective-permute-done.1.refs_3_ = f32[20,64,256]{2,1,0:T(8,128)S(1)} collective-permute-done((f32[20,64,256]{2,1,0:T(8,128)S(1)}, f32[20,64,256]{2,1,0:T(8,128)S(1)}, u32[]{:S(2)}, u32[]{:S(2)}) %collective-permute-start.1) | collective-permute-done | bytes 1310752 | tf_op jit(solution)/shard_map/ppermute | solution.py:47
  78.4 2.7 %collective-permute-start.4 = (f32[10,64,256]{2,1,0:T(8,128)S(1)}, f32[10,64,256]{2,1,0:T(8,128)S(1)}, u32[]{:S(2)}, u32[]{:S(2)}) collective-permute-start(f32[10,64,256]{2,1,0:T(8,128)S(1)} %slice.15), channel_id=1, source_target_pairs={{0,48},{1,49},{2,50},{3,51},{4,52},{5,53},{6,54},{7,55},{8,56},{9,... | collective-permute-start | bytes 1966088 | tf_op jit(solution)/shard_map/ppermute | solution.py:47
  81.1 2.3 %shard_map.65 = (bf16[321,64,128]{2,1,0:T(8,128)(2,1)S(1)}, bf16[321,64,128]{2,1,0:T(8,128)(2,1)S(1)}) custom-call(s32[3]{0:T(128)S(1)} %add_convert_fusion.flag_ref, f32[20,64,256]{2,1,0:T(8,128)S(1)} %collective-permute-done.refs_0_, f32[20,64,256]{2,1,0:T(8,128)S(1)} %gather_fusion, f32[20,64,256]{2,1,0:T(8,128)S(1)} %collective-permute-done.3.refs_2_, ...), custom_call_target="tpu_custom_call" | custom-call | flops 2000000000 | bytes 10000000 | tf_op jit(solution)/shard_map/pallas_call | solution.py:186
  83.4 12.3 %collective-permute-done.2.refs_0_ = f32[10,64,256]{2,1,0:T(8,128)S(1)} collective-permute-done((f32[10,64,256]{2,1,0:T(8,128)S(1)}, f32[10,64,256]{2,1,0:T(8,128)S(1)}, u32[]{:S(2)}, u32[]{:S(2)}) %collective-permute-start.2) | collective-permute-done | bytes 655392 | tf_op jit(solution)/shard_map/ppermute | solution.py:47
  97.2 8.5 %shard_map.67 = f32[20,64,256]{2,1,0:T(8,128)} custom-call(s32[1280]{0:T(1024)S(1)} %add.221.pick_ref, s32[3]{0:T(128)S(1)} %add_convert_fusion.flag_ref, bf16[321,64,128]{2,1,0:T(8,128)(2,1)S(1)} %get-tuple-element.31.high, bf16[321,64,128]{2,1,0:T(8,128)(2,1)S(1)} %get-tuple-element.32.low, f32[20,64,256]{2,1,0:T(8,128)S(1)} %collective-permute-done.5.refs_0_, ...), custom_call_target="tpu_custom_call" | custom-call | flops 8000000000 | bytes 10000000 | tf_op jit(solution)/shard_map/pallas_call | solution.py:268
  109.9 2.4 %multiply_add_fusion = (f32[20,64,256]{2,1,0:T(8,128)S(1)}, f32[20,64,256]{2,1,0:T(8,128)S(1)}) fusion(f32[20,64,256]{2,1,0:T(8,128)S(1)} %gather_fusion, f32[20,64,256]{2,1,0:T(8,128)S(1)} %collective-permute-done.refs_0_, f32[]{:T(128)S(6)} %sub.64, f32[]{:T(128)S(6)} %sub.63, f32[64,256]{1,0:T(8,128)S(1)} %mul.176, f32[20,256]{1,0:T(8,128)S(1)} %mul.173, ...), kind=kLoop, calls=%fused_computation.4 | loop fusion | flops 2949120 | bytes 7970829 | tf_op jit(solution)/shard_map/add | solution.py:378
  114.0 2.8 %collective-permute-start.16 = (f32[20,64,256]{2,1,0:T(8,128)S(1)}, f32[20,64,256]{2,1,0:T(8,128)S(1)}, u32[]{:S(2)}, u32[]{:S(2)}) collective-permute-start(f32[20,64,256]{2,1,0:T(8,128)S(1)} %get-tuple-element.43), channel_id=1, source_target_pairs={{0,68},{1,9},{2,70},{3,11},{4,12},{5,65},{6,14},{7,67},{8,0},{9,77... | collective-permute-start | bytes 3932168 | tf_op jit(solution)/shard_map/ppermute | solution.py:47
  117.6 12.4 %collective-permute-done.11.refs_0_ = f32[20,64,256]{2,1,0:T(8,128)S(1)} collective-permute-done((f32[20,64,256]{2,1,0:T(8,128)S(1)}, f32[20,64,256]{2,1,0:T(8,128)S(1)}, u32[]{:S(2)}, u32[]{:S(2)}) %collective-permute-start.11) | collective-permute-done | bytes 1310752 | tf_op jit(solution)/shard_map/ppermute | solution.py:47
  129.9 2.9 %collective-permute-done.14.refs_1_ = f32[20,64,256]{2,1,0:T(8,128)S(1)} collective-permute-done((f32[20,64,256]{2,1,0:T(8,128)S(1)}, f32[20,64,256]{2,1,0:T(8,128)S(1)}, u32[]{:S(2)}, u32[]{:S(2)}) %collective-permute-start.14) | collective-permute-done | bytes 1310752 | tf_op jit(solution)/shard_map/ppermute | solution.py:47
  139.6 9.5 %collective-permute-done.15.refs_2_ = f32[20,64,256]{2,1,0:T(8,128)S(1)} collective-permute-done((f32[20,64,256]{2,1,0:T(8,128)S(1)}, f32[20,64,256]{2,1,0:T(8,128)S(1)}, u32[]{:S(2)}, u32[]{:S(2)}) %collective-permute-start.15) | collective-permute-done | bytes 1310752 | tf_op jit(solution)/shard_map/ppermute | solution.py:47
  152.2 12.2 %collective-permute-done.12.refs_0_ = f32[20,64,256]{2,1,0:T(8,128)S(1)} collective-permute-done((f32[20,64,256]{2,1,0:T(8,128)S(1)}, f32[20,64,256]{2,1,0:T(8,128)S(1)}, u32[]{:S(2)}, u32[]{:S(2)}) %collective-permute-start.12) | collective-permute-done | bytes 1310752 | tf_op jit(solution)/shard_map/ppermute | solution.py:47
  166.2 2.8 %collective-permute-done.20.refs_4_ = f32[20,64,256]{2,1,0:T(8,128)S(1)} collective-permute-done((f32[20,64,256]{2,1,0:T(8,128)S(1)}, f32[20,64,256]{2,1,0:T(8,128)S(1)}, u32[]{:S(2)}, u32[]{:S(2)}) %collective-permute-start.20) | collective-permute-done | bytes 1310752 | tf_op jit(solution)/shard_map/ppermute | solution.py:47
  169.0 4.0 %shard_map.71 = f32[10,64,256]{2,1,0:T(8,128)S(1)} custom-call(s32[1280]{0:T(1024)S(1)} %add.221.pick_ref, s32[3]{0:T(128)S(1)} %add_convert_fusion.flag_ref, bf16[321,64,128]{2,1,0:T(8,128)(2,1)S(1)} %get-tuple-element.38.high, bf16[321,64,128]{2,1,0:T(8,128)(2,1)S(1)} %get-tuple-element.39.low, f32[20,64,256]{2,1,0:T(8,128)S(1)} %collective-permute-done.16.refs_0_, ...), custom_call_target="tpu_custom_call" | custom-call | flops 8000000000 | bytes 10000000 | tf_op jit(solution)/shard_map/pallas_call | solution.py:268
  173.0 2.9 %collective-permute-start.23 = (f32[10,64,256]{2,1,0:T(8,128)S(1)}, f32[10,64,256]{2,1,0:T(8,128)S(1)}, u32[]{:S(2)}, u32[]{:S(2)}) collective-permute-start(f32[10,64,256]{2,1,0:T(8,128)S(1)} %shard_map.71), channel_id=1, source_target_pairs={{0,8},{1,9},{2,10},{3,11},{4,12},{5,13},{6,14},{7,15},{8,0},{9,1},... | collective-permute-start | bytes 1966088 | tf_op jit(solution)/shard_map/ppermute | solution.py:47
  175.9 3.9 %shard_map.70 = f32[10,64,256]{2,1,0:T(8,128)S(1)} custom-call(s32[1280]{0:T(1024)S(1)} %add.221.pick_ref, s32[3]{0:T(128)S(1)} %add_convert_fusion.flag_ref, bf16[321,64,128]{2,1,0:T(8,128)(2,1)S(1)} %get-tuple-element.38.high, bf16[321,64,128]{2,1,0:T(8,128)(2,1)S(1)} %get-tuple-element.39.low, f32[20,64,256]{2,1,0:T(8,128)S(1)} %collective-permute-done.16.refs_0_, ...), custom_call_target="tpu_custom_call" | custom-call | flops 8000000000 | bytes 10000000 | tf_op jit(solution)/shard_map/pallas_call | solution.py:268
  183.4 8.0 %collective-permute-done.24 = f32[10,64,256]{2,1,0:T(8,128)S(1)} collective-permute-done((f32[10,64,256]{2,1,0:T(8,128)S(1)}, f32[10,64,256]{2,1,0:T(8,128)S(1)}, u32[]{:S(2)}, u32[]{:S(2)}) %collective-permute-start.24) | collective-permute-done | bytes 655392 | tf_op jit(solution)/shard_map/ppermute | solution.py:47
  191.4 6.9 %collective-permute-done.22 = f32[10,64,256]{2,1,0:T(8,128)S(1)} collective-permute-done((f32[10,64,256]{2,1,0:T(8,128)S(1)}, f32[10,64,256]{2,1,0:T(8,128)S(1)}, u32[]{:S(2)}, u32[]{:S(2)}) %collective-permute-start.22) | collective-permute-done | bytes 655392 | tf_op jit(solution)/shard_map/ppermute | solution.py:47
  (100 shorter events, 37.4 us)
Async XLA Ops:
  2.7 34.2 %all-to-all-start = ((f32[32,64,256]{2,1,0:T(8,128)}), f32[32,64,256]{2,1,0:T(8,128)S(1)}, u32[]{:S(2)}, u32[]{:S(2)}) async-start(f32[32,64,256]{2,1,0:T(8,128)} %shard_map.64), calls=%async_computation | async-start | bytes 4194304 | tf_op jit(solution)/shard_map/all_to_all | solution.py:349
  37.5 11.3 %collective-permute-start = (f32[20,64,256]{2,1,0:T(8,128)S(1)}, f32[20,64,256]{2,1,0:T(8,128)S(1)}, u32[]{:S(2)}, u32[]{:S(2)}) collective-permute-start(f32[20,64,256]{2,1,0:T(8,128)S(1)} %gather_fusion), channel_id=1, source_target_pairs={{0,8},{1,9},{2,10},{3,11},{4,12},{5,13},{6,14},{7,15},{8,0},{9,1},... | collective-permute-start | bytes 3932168 | tf_op jit(solution)/shard_map/ppermute | solution.py:47
  40.5 20.7 %collective-permute-start.5 = (f32[20,64,256]{2,1,0:T(8,128)S(1)}, f32[20,64,256]{2,1,0:T(8,128)S(1)}, u32[]{:S(2)}, u32[]{:S(2)}) collective-permute-start(f32[20,64,256]{2,1,0:T(8,128)S(1)} %gather_fusion), channel_id=1, source_target_pairs={{0,0},{1,9},{2,2},{3,11},{4,8},{5,1},{6,10},{7,3},{8,4},{9,13},{10... | collective-permute-start | bytes 3932168 | tf_op jit(solution)/shard_map/ppermute | solution.py:47
  45.0 16.1 %collective-permute-start.6 = (f32[20,64,256]{2,1,0:T(8,128)S(1)}, f32[20,64,256]{2,1,0:T(8,128)S(1)}, u32[]{:S(2)}, u32[]{:S(2)}) collective-permute-start(f32[20,64,256]{2,1,0:T(8,128)S(1)} %gather_fusion), channel_id=1, source_target_pairs={{0,2},{1,11},{2,0},{3,9},{12,14},{13,7},{14,12},{15,5},{16,18},{17... | collective-permute-start | bytes 3932168 | tf_op jit(solution)/shard_map/ppermute | solution.py:47
  45.8 32.4 %collective-permute-start.1 = (f32[20,64,256]{2,1,0:T(8,128)S(1)}, f32[20,64,256]{2,1,0:T(8,128)S(1)}, u32[]{:S(2)}, u32[]{:S(2)}) collective-permute-start(f32[20,64,256]{2,1,0:T(8,128)S(1)} %gather_fusion), channel_id=1, source_target_pairs={{0,16},{1,17},{2,18},{3,19},{4,20},{5,21},{6,22},{7,23},{8,24},{9,... | collective-permute-start | bytes 3932168 | tf_op jit(solution)/shard_map/ppermute | solution.py:47
  47.2 31.1 %collective-permute-start.3 = (f32[20,64,256]{2,1,0:T(8,128)S(1)}, f32[20,64,256]{2,1,0:T(8,128)S(1)}, u32[]{:S(2)}, u32[]{:S(2)}) collective-permute-start(f32[20,64,256]{2,1,0:T(8,128)S(1)} %gather_fusion), channel_id=1, source_target_pairs={{0,48},{1,49},{2,50},{3,51},{4,52},{5,53},{6,54},{7,55},{8,56},{9,... | collective-permute-start | bytes 3932168 | tf_op jit(solution)/shard_map/ppermute | solution.py:47
  61.2 36.0 %collective-permute-start.7 = (f32[20,64,256]{2,1,0:T(8,128)S(1)}, f32[20,64,256]{2,1,0:T(8,128)S(1)}, u32[]{:S(2)}, u32[]{:S(2)}) collective-permute-start(f32[20,64,256]{2,1,0:T(8,128)S(1)} %collective-permute-done.5.refs_0_), channel_id=1, source_target_pairs={{0,1},{1,2},{2,3},{3,0},{4,5},{5,6},{6,7},{7,4},{8,9},{9,10},{10,1... | collective-permute-start | bytes 3932168 | tf_op jit(solution)/shard_map/ppermute | solution.py:47
  66.1 31.0 %collective-permute-start.8 = (f32[20,64,256]{2,1,0:T(8,128)S(1)}, f32[20,64,256]{2,1,0:T(8,128)S(1)}, u32[]{:S(2)}, u32[]{:S(2)}) collective-permute-start(f32[20,64,256]{2,1,0:T(8,128)S(1)} %collective-permute-done.5.refs_0_), channel_id=1, source_target_pairs={{0,3},{1,0},{2,1},{3,2},{4,7},{5,4},{6,5},{7,6},{8,11},{9,8},{10,9... | collective-permute-start | bytes 3932168 | tf_op jit(solution)/shard_map/ppermute | solution.py:47
  66.1 31.0 %collective-permute-start.9 = (f32[20,64,256]{2,1,0:T(8,128)S(1)}, f32[20,64,256]{2,1,0:T(8,128)S(1)}, u32[]{:S(2)}, u32[]{:S(2)}) collective-permute-start(f32[20,64,256]{2,1,0:T(8,128)S(1)} %collective-permute-done.6.refs_3_), channel_id=1, source_target_pairs={{0,68},{2,70},{5,65},{7,67},{9,77},{11,79},{12,72},{14,74},{16,84}... | collective-permute-start | bytes 3932168 | tf_op jit(solution)/shard_map/ppermute | solution.py:47
  78.2 17.5 %collective-permute-start.2 = (f32[10,64,256]{2,1,0:T(8,128)S(1)}, f32[10,64,256]{2,1,0:T(8,128)S(1)}, u32[]{:S(2)}, u32[]{:S(2)}) collective-permute-start(f32[10,64,256]{2,1,0:T(8,128)S(1)} %slice.14), channel_id=1, source_target_pairs={{0,16},{1,17},{2,18},{3,19},{4,20},{5,21},{6,22},{7,23},{8,24},{9,... | collective-permute-start | bytes 1966088 | tf_op jit(solution)/shard_map/ppermute | solution.py:47
  78.4 17.3 %collective-permute-start.4 = (f32[10,64,256]{2,1,0:T(8,128)S(1)}, f32[10,64,256]{2,1,0:T(8,128)S(1)}, u32[]{:S(2)}, u32[]{:S(2)}) collective-permute-start(f32[10,64,256]{2,1,0:T(8,128)S(1)} %slice.15), channel_id=1, source_target_pairs={{0,48},{1,49},{2,50},{3,51},{4,52},{5,53},{6,54},{7,55},{8,56},{9,... | collective-permute-start | bytes 1966088 | tf_op jit(solution)/shard_map/ppermute | solution.py:47
  112.2 17.7 %collective-permute-start.11 = (f32[20,64,256]{2,1,0:T(8,128)S(1)}, f32[20,64,256]{2,1,0:T(8,128)S(1)}, u32[]{:S(2)}, u32[]{:S(2)}) collective-permute-start(f32[20,64,256]{2,1,0:T(8,128)S(1)} %get-tuple-element.42), channel_id=1, source_target_pairs={{0,64},{1,65},{2,66},{3,67},{4,12},{5,13},{6,14},{7,15},{8,0},{9,1... | collective-permute-start | bytes 3932168 | tf_op jit(solution)/shard_map/ppermute | solution.py:47
  112.7 20.1 %collective-permute-start.14 = (f32[20,64,256]{2,1,0:T(8,128)S(1)}, f32[20,64,256]{2,1,0:T(8,128)S(1)}, u32[]{:S(2)}, u32[]{:S(2)}) collective-permute-start(f32[20,64,256]{2,1,0:T(8,128)S(1)} %get-tuple-element.42), channel_id=1, source_target_pairs={{0,32},{1,33},{2,34},{3,35},{12,44},{13,45},{14,46},{15,47},{16,48... | collective-permute-start | bytes 3932168 | tf_op jit(solution)/shard_map/ppermute | solution.py:47
  114.0 23.0 %collective-permute-start.16 = (f32[20,64,256]{2,1,0:T(8,128)S(1)}, f32[20,64,256]{2,1,0:T(8,128)S(1)}, u32[]{:S(2)}, u32[]{:S(2)}) collective-permute-start(f32[20,64,256]{2,1,0:T(8,128)S(1)} %get-tuple-element.43), channel_id=1, source_target_pairs={{0,68},{1,9},{2,70},{3,11},{4,12},{5,65},{6,14},{7,67},{8,0},{9,77... | collective-permute-start | bytes 3932168 | tf_op jit(solution)/shard_map/ppermute | solution.py:47
  116.8 20.9 %collective-permute-start.19 = (f32[20,64,256]{2,1,0:T(8,128)S(1)}, f32[20,64,256]{2,1,0:T(8,128)S(1)}, u32[]{:S(2)}, u32[]{:S(2)}) collective-permute-start(f32[20,64,256]{2,1,0:T(8,128)S(1)} %get-tuple-element.43), channel_id=1, source_target_pairs={{0,2},{2,0},{5,7},{7,5},{9,11},{11,9},{12,14},{14,12},{16,18},{18,... | collective-permute-start | bytes 3932168 | tf_op jit(solution)/shard_map/ppermute | solution.py:47
  132.8 16.3 %collective-permute-start.15 = (f32[20,64,256]{2,1,0:T(8,128)S(1)}, f32[20,64,256]{2,1,0:T(8,128)S(1)}, u32[]{:S(2)}, u32[]{:S(2)}) collective-permute-start(f32[20,64,256]{2,1,0:T(8,128)S(1)} %collective-permute-done.14.refs_1_), channel_id=1, source_target_pairs={{4,68},{5,69},{6,70},{7,71},{8,72},{9,73},{10,74},{11,75},{20,84},... | collective-permute-start | bytes 3932168 | tf_op jit(solution)/shard_map/ppermute | solution.py:47
  134.7 29.7 %collective-permute-start.12 = (f32[20,64,256]{2,1,0:T(8,128)S(1)}, f32[20,64,256]{2,1,0:T(8,128)S(1)}, u32[]{:S(2)}, u32[]{:S(2)}) collective-permute-start(f32[20,64,256]{2,1,0:T(8,128)S(1)} %collective-permute-done.11.refs_0_), channel_id=1, source_target_pairs={{0,48},{1,49},{2,50},{3,51},{4,52},{5,53},{6,54},{7,55},{8,56},{9,... | collective-permute-start | bytes 3932168 | tf_op jit(solution)/shard_map/ppermute | solution.py:47
  134.8 29.6 %collective-permute-start.13 = (f32[20,64,256]{2,1,0:T(8,128)S(1)}, f32[20,64,256]{2,1,0:T(8,128)S(1)}, u32[]{:S(2)}, u32[]{:S(2)}) collective-permute-start(f32[20,64,256]{2,1,0:T(8,128)S(1)} %collective-permute-done.11.refs_0_), channel_id=1, source_target_pairs={{0,16},{1,17},{2,18},{3,19},{4,20},{5,21},{6,22},{7,23},{8,24},{9,... | collective-permute-start | bytes 3932168 | tf_op jit(solution)/shard_map/ppermute | solution.py:47
  136.9 29.3 %collective-permute-start.17 = (f32[20,64,256]{2,1,0:T(8,128)S(1)}, f32[20,64,256]{2,1,0:T(8,128)S(1)}, u32[]{:S(2)}, u32[]{:S(2)}) collective-permute-start(f32[20,64,256]{2,1,0:T(8,128)S(1)} %collective-permute-done.16.refs_0_), channel_id=1, source_target_pairs={{0,1},{1,2},{2,3},{3,0},{4,5},{5,6},{6,7},{7,4},{8,9},{9,10},{10,1... | collective-permute-start | bytes 3932168 | tf_op jit(solution)/shard_map/ppermute | solution.py:47
  137.7 28.5 %collective-permute-start.18 = (f32[20,64,256]{2,1,0:T(8,128)S(1)}, f32[20,64,256]{2,1,0:T(8,128)S(1)}, u32[]{:S(2)}, u32[]{:S(2)}) collective-permute-start(f32[20,64,256]{2,1,0:T(8,128)S(1)} %collective-permute-done.16.refs_0_), channel_id=1, source_target_pairs={{0,3},{1,0},{2,1},{3,2},{4,7},{5,4},{6,5},{7,6},{8,11},{9,8},{10,9... | collective-permute-start | bytes 3932168 | tf_op jit(solution)/shard_map/ppermute | solution.py:47
  149.2 19.8 %collective-permute-start.20 = (f32[20,64,256]{2,1,0:T(8,128)S(1)}, f32[20,64,256]{2,1,0:T(8,128)S(1)}, u32[]{:S(2)}, u32[]{:S(2)}) collective-permute-start(f32[20,64,256]{2,1,0:T(8,128)S(1)} %collective-permute-done.19.refs_3_), channel_id=1, source_target_pairs={{0,68},{2,70},{5,65},{7,67},{9,77},{11,79},{12,72},{14,74},{16,84}... | collective-permute-start | bytes 3932168 | tf_op jit(solution)/shard_map/ppermute | solution.py:47
  173.0 6.9 %collective-permute-start.23 = (f32[10,64,256]{2,1,0:T(8,128)S(1)}, f32[10,64,256]{2,1,0:T(8,128)S(1)}, u32[]{:S(2)}, u32[]{:S(2)}) collective-permute-start(f32[10,64,256]{2,1,0:T(8,128)S(1)} %shard_map.71), channel_id=1, source_target_pairs={{0,8},{1,9},{2,10},{3,11},{4,12},{5,13},{6,14},{7,15},{8,0},{9,1},... | collective-permute-start | bytes 1966088 | tf_op jit(solution)/shard_map/ppermute | solution.py:47
  180.0 11.3 %collective-permute-start.24 = (f32[10,64,256]{2,1,0:T(8,128)S(1)}, f32[10,64,256]{2,1,0:T(8,128)S(1)}, u32[]{:S(2)}, u32[]{:S(2)}) collective-permute-start(f32[10,64,256]{2,1,0:T(8,128)S(1)} %add.233), channel_id=1, source_target_pairs={{0,64},{1,65},{2,66},{3,67},{12,76},{13,77},{14,78},{15,79},{16,80... | collective-permute-start | bytes 1966088 | tf_op jit(solution)/shard_map/ppermute | solution.py:47
  182.1 16.3 %collective-permute-start.22 = (f32[10,64,256]{2,1,0:T(8,128)S(1)}, f32[10,64,256]{2,1,0:T(8,128)S(1)}, u32[]{:S(2)}, u32[]{:S(2)}) collective-permute-start(f32[10,64,256]{2,1,0:T(8,128)S(1)} %add.232), channel_id=1, source_target_pairs={{0,64},{1,65},{2,66},{3,67},{12,76},{13,77},{14,78},{15,79},{16,80... | collective-permute-start | bytes 1966088 | tf_op jit(solution)/shard_map/ppermute | solution.py:47
  (6 other events, 34.4 us)

commit v6 on v5

--- a/solution.py
+++ b/solution.py
@@ -13,8 +13,9 @@
 N_SLOT = 4
 TABLE_STEP = 10
 ROW_STEP = 5
-TABLE_BYTES = 8 * 1024 * 1024
-PRODUCT_BYTES = 10 * 1024 * 1024
+SPREAD_BYTES = 4 * 1024 * 1024
+TABLE_BYTES = 5 * 1024 * 1024
+PRODUCT_BYTES = 7 * 1024 * 1024
 
 
 def moves(target):
@@ -81,7 +82,7 @@
     left = send(density, left_own)
     across = send(density, left_across)
     swapped = swap_cores(density)
-    left_now = after(left, across, swapped)
+    left_now = after(left, swapped)
     left_below = step(left_now, dz=1)
     left_above = step(left_now, dz=-1)
     left_pair = send(across, left_pass)
@@ -297,7 +298,7 @@
         out_shape=jax.ShapeDtypeStruct((layers * groups * cap, width, wide), jnp.float32),
         in_specs=[pl.BlockSpec(memory_space=pltpu.VMEM)],
         out_specs=pl.BlockSpec(memory_space=pltpu.VMEM),
-        compiler_params=pltpu.CompilerParams(vmem_limit_bytes=PRODUCT_BYTES),
+        compiler_params=pltpu.CompilerParams(vmem_limit_bytes=SPREAD_BYTES),
     )(owner_blocks)
 
 
@@ -368,7 +369,7 @@
     jobs = ((0, (0, 1), 2), (1, (2,), None), (3, (3,), None))
     tables = table((swapped, density, above, below), jobs, flags, rows)
     tables = table((first, second), ((2, (0, 1), None),), flags, rows, tables)
-    partial_value = product(left, tables, picks, flags, 0, rows)
+    partial_value = product(left, tables, picks, flags, 0, rows, 3)
     square = partial_value + swap_cores(partial_value)
     square = square * keep_wide
     unit = (own[:, None, :, None] * jnp.eye(width, dtype=jnp.float32)[None, :, None, :]).reshape(

time: 201 us -> 201 us (level)
  starting transfers between devices: 49 us -> 46.8 us
    ppermute x25, waiting for transfers between devices: 92.8 us -> 95 us  [send(): return lax.ppermute(x, AXES, moves(target))]
    ppermute x25, starting transfers between devices: 40.4 us -> 38.2 us  [send(): return lax.ppermute(x, AXES, moves(target))]
where the time goes in v6:
time: 201 us; the launch traced here: 199 us
  waiting for transfers between devices  110 us (55%)
  starting transfers between devices  46.8 us (23%)
  Pallas kernels  24.7 us (12%)
  other arithmetic  11.6 us (6%)
  local copies, waits for them, and re-layouts  5.07 us (3%)
    ppermute x25, waiting for transfers between devices, send(): return lax.ppermute(x, AXES, moves(target))  95 us
    ppermute x25, starting transfers between devices, send(): return lax.ppermute(x, AXES, moves(target))  38.2 us
    pallas_call x3, Pallas kernels, product(): pl.pallas_call(functools.partial(product_kernel, first, begin, end, width...  16 us
    all_to_all x1, waiting for transfers between devices, body(): lax.all_to_all(plain_send, ('layer', 'col'), split_axis=0, concat_axis=0,...  14.9 us
    all_to_all x1, starting transfers between devices, body(): lax.all_to_all(plain_send, ('layer', 'col'), split_axis=0, concat_axis=0,...  8.56 us
    pallas_call x4, Pallas kernels, table(): pl.pallas_call(functools.partial(table_kernel, rows, width, span, jobs, c...  7.23 us
    reduce_sum x1, other arithmetic, pick_table(): found = jnp.sum(hit[..., None] * right_cols[None, :, None], axis=3)  5.6 us
  transfers between devices with their start and end apart: 26, of which 14 were waited for; matrix products, arithmetic and copies ran while one was open for 6% of the time, Pallas kernels for 6%

profile of v6, /device:TPU:1, one launch (start us, length us, event | category | flops | bytes accessed | tf_op | source)
XLA Modules:
  0.0 199.3 jit_solution(5308556165922686066)
XLA Ops:
  2.7 8.6 %all-to-all-start = ((f32[32,64,256]{2,1,0:T(8,128)}), f32[32,64,256]{2,1,0:T(8,128)S(1)}, u32[]{:S(2)}, u32[]{:S(2)}) async-start(f32[32,64,256]{2,1,0:T(8,128)} %shard_map.64), calls=%async_computation | async-start | bytes 4194304 | tf_op jit(solution)/shard_map/all_to_all | solution.py:350
  14.2 5.6 %multiply_reduce_fusion = s32[20,4,4,4]{3,2,1,0:T(4,128)S(1)} fusion(s32[4,20,4]{1,2,0:T(4,128)S(1)} %multiply_reduce_fusion.2, s32[20,4,4,20]{3,2,1,0:T(4,128)S(1)} %fusion), kind=kLoop, calls=%fused_computation.6 | loop fusion | flops 49920 | bytes 32000 | tf_op jit(solution)/shard_map/reduce_sum | solution.py:320
  22.0 14.9 %all-to-all-done = f32[32,64,256]{2,1,0:T(8,128)S(1)} async-done(((f32[32,64,256]{2,1,0:T(8,128)}), f32[32,64,256]{2,1,0:T(8,128)S(1)}, u32[]{:S(2)}, u32[]{:S(2)}) %all-to-all-start) | async-done | bytes 2097184 | tf_op jit(solution)/shard_map/all_to_all | solution.py:350
  37.5 2.9 %collective-permute-start = (f32[20,64,256]{2,1,0:T(8,128)S(1)}, f32[20,64,256]{2,1,0:T(8,128)S(1)}, u32[]{:S(2)}, u32[]{:S(2)}) collective-permute-start(f32[20,64,256]{2,1,0:T(8,128)S(1)} %gather_fusion), channel_id=1, source_target_pairs={{0,8},{1,9},{2,10},{3,11},{4,12},{5,13},{6,14},{7,15},{8,0},{9,1},... | collective-permute-start | bytes 3932168 | tf_op jit(solution)/shard_map/ppermute | solution.py:48
  40.5 4.6 %collective-permute-start.5 = (f32[20,64,256]{2,1,0:T(8,128)S(1)}, f32[20,64,256]{2,1,0:T(8,128)S(1)}, u32[]{:S(2)}, u32[]{:S(2)}) collective-permute-start(f32[20,64,256]{2,1,0:T(8,128)S(1)} %gather_fusion), channel_id=1, source_target_pairs={{0,0},{1,9},{2,2},{3,11},{4,8},{5,1},{6,10},{7,3},{8,4},{9,13},{10... | collective-permute-start | bytes 3932168 | tf_op jit(solution)/shard_map/ppermute | solution.py:48
  48.8 12.3 %collective-permute-done.5.refs_0_ = f32[20,64,256]{2,1,0:T(8,128)S(1)} collective-permute-done((f32[20,64,256]{2,1,0:T(8,128)S(1)}, f32[20,64,256]{2,1,0:T(8,128)S(1)}, u32[]{:S(2)}, u32[]{:S(2)}) %collective-permute-start.5) | collective-permute-done | bytes 1310752 | tf_op jit(solution)/shard_map/ppermute | solution.py:48
  61.2 2.7 %collective-permute-start.7 = (f32[20,64,256]{2,1,0:T(8,128)S(1)}, f32[20,64,256]{2,1,0:T(8,128)S(1)}, u32[]{:S(2)}, u32[]{:S(2)}) collective-permute-start(f32[20,64,256]{2,1,0:T(8,128)S(1)} %collective-permute-done.5.refs_0_), channel_id=1, source_target_pairs={{0,3},{1,0},{2,1},{3,2},{4,7},{5,4},{6,5},{7,6},{8,11},{9,8},{10,9... | collective-permute-start | bytes 3932168 | tf_op jit(solution)/shard_map/ppermute | solution.py:48
  65.2 13.0 %collective-permute-done.1.refs_3_ = f32[20,64,256]{2,1,0:T(8,128)S(1)} collective-permute-done((f32[20,64,256]{2,1,0:T(8,128)S(1)}, f32[20,64,256]{2,1,0:T(8,128)S(1)}, u32[]{:S(2)}, u32[]{:S(2)}) %collective-permute-start.1) | collective-permute-done | bytes 1310752 | tf_op jit(solution)/shard_map/ppermute | solution.py:48
  78.4 2.7 %collective-permute-start.4 = (f32[10,64,256]{2,1,0:T(8,128)S(1)}, f32[10,64,256]{2,1,0:T(8,128)S(1)}, u32[]{:S(2)}, u32[]{:S(2)}) collective-permute-start(f32[10,64,256]{2,1,0:T(8,128)S(1)} %slice.15), channel_id=1, source_target_pairs={{0,48},{1,49},{2,50},{3,51},{4,52},{5,53},{6,54},{7,55},{8,56},{9,... | collective-permute-start | bytes 1966088 | tf_op jit(solution)/shard_map/ppermute | solution.py:48
  81.1 2.3 %shard_map.65 = (bf16[321,64,128]{2,1,0:T(8,128)(2,1)S(1)}, bf16[321,64,128]{2,1,0:T(8,128)(2,1)S(1)}) custom-call(s32[3]{0:T(128)S(1)} %add_convert_fusion.flag_ref, f32[20,64,256]{2,1,0:T(8,128)S(1)} %collective-permute-done.refs_0_, f32[20,64,256]{2,1,0:T(8,128)S(1)} %gather_fusion, f32[20,64,256]{2,1,0:T(8,128)S(1)} %collective-permute-done.3.refs_2_, ...), custom_call_target="tpu_custom_call" | custom-call | flops 2000000000 | bytes 10000000 | tf_op jit(solution)/shard_map/pallas_call | solution.py:187
  83.4 12.3 %collective-permute-done.2.refs_0_ = f32[10,64,256]{2,1,0:T(8,128)S(1)} collective-permute-done((f32[10,64,256]{2,1,0:T(8,128)S(1)}, f32[10,64,256]{2,1,0:T(8,128)S(1)}, u32[]{:S(2)}, u32[]{:S(2)}) %collective-permute-start.2) | collective-permute-done | bytes 655392 | tf_op jit(solution)/shard_map/ppermute | solution.py:48
  97.2 8.2 %shard_map.67 = f32[20,64,256]{2,1,0:T(8,128)} custom-call(s32[1280]{0:T(1024)S(1)} %add.221.pick_ref, s32[3]{0:T(128)S(1)} %add_convert_fusion.flag_ref, bf16[321,64,128]{2,1,0:T(8,128)(2,1)S(1)} %get-tuple-element.31.high, bf16[321,64,128]{2,1,0:T(8,128)(2,1)S(1)} %get-tuple-element.32.low, f32[20,64,256]{2,1,0:T(8,128)S(1)} %collective-permute-done.5.refs_0_, ...), custom_call_target="tpu_custom_call" | custom-call | flops 8000000000 | bytes 10000000 | tf_op jit(solution)/shard_map/pallas_call | solution.py:269
  109.6 2.4 %multiply_add_fusion = (f32[20,64,256]{2,1,0:T(8,128)S(1)}, f32[20,64,256]{2,1,0:T(8,128)S(1)}) fusion(f32[20,64,256]{2,1,0:T(8,128)S(1)} %gather_fusion, f32[20,64,256]{2,1,0:T(8,128)S(1)} %collective-permute-done.refs_0_, f32[]{:T(128)S(6)} %sub.64, f32[]{:T(128)S(6)} %sub.63, f32[64,256]{1,0:T(8,128)S(1)} %mul.176, f32[20,256]{1,0:T(8,128)S(1)} %mul.173, ...), kind=kLoop, calls=%fused_computation.4 | loop fusion | flops 2949120 | bytes 7970829 | tf_op jit(solution)/shard_map/add | solution.py:379
  113.7 2.9 %collective-permute-start.16 = (f32[20,64,256]{2,1,0:T(8,128)S(1)}, f32[20,64,256]{2,1,0:T(8,128)S(1)}, u32[]{:S(2)}, u32[]{:S(2)}) collective-permute-start(f32[20,64,256]{2,1,0:T(8,128)S(1)} %get-tuple-element.43), channel_id=1, source_target_pairs={{0,68},{1,9},{2,70},{3,11},{4,12},{5,65},{6,14},{7,67},{8,0},{9,77... | collective-permute-start | bytes 3932168 | tf_op jit(solution)/shard_map/ppermute | solution.py:48
  117.3 12.3 %collective-permute-done.11.refs_0_ = f32[20,64,256]{2,1,0:T(8,128)S(1)} collective-permute-done((f32[20,64,256]{2,1,0:T(8,128)S(1)}, f32[20,64,256]{2,1,0:T(8,128)S(1)}, u32[]{:S(2)}, u32[]{:S(2)}) %collective-permute-start.11) | collective-permute-done | bytes 1310752 | tf_op jit(solution)/shard_map/ppermute | solution.py:48
  129.6 2.9 %collective-permute-done.14.refs_1_ = f32[20,64,256]{2,1,0:T(8,128)S(1)} collective-permute-done((f32[20,64,256]{2,1,0:T(8,128)S(1)}, f32[20,64,256]{2,1,0:T(8,128)S(1)}, u32[]{:S(2)}, u32[]{:S(2)}) %collective-permute-start.14) | collective-permute-done | bytes 1310752 | tf_op jit(solution)/shard_map/ppermute | solution.py:48
  139.3 9.6 %collective-permute-done.15.refs_2_ = f32[20,64,256]{2,1,0:T(8,128)S(1)} collective-permute-done((f32[20,64,256]{2,1,0:T(8,128)S(1)}, f32[20,64,256]{2,1,0:T(8,128)S(1)}, u32[]{:S(2)}, u32[]{:S(2)}) %collective-permute-start.15) | collective-permute-done | bytes 1310752 | tf_op jit(solution)/shard_map/ppermute | solution.py:48
  151.9 12.2 %collective-permute-done.12.refs_0_ = f32[20,64,256]{2,1,0:T(8,128)S(1)} collective-permute-done((f32[20,64,256]{2,1,0:T(8,128)S(1)}, f32[20,64,256]{2,1,0:T(8,128)S(1)}, u32[]{:S(2)}, u32[]{:S(2)}) %collective-permute-start.12) | collective-permute-done | bytes 1310752 | tf_op jit(solution)/shard_map/ppermute | solution.py:48
  165.9 2.8 %collective-permute-done.20.refs_4_ = f32[20,64,256]{2,1,0:T(8,128)S(1)} collective-permute-done((f32[20,64,256]{2,1,0:T(8,128)S(1)}, f32[20,64,256]{2,1,0:T(8,128)S(1)}, u32[]{:S(2)}, u32[]{:S(2)}) %collective-permute-start.20) | collective-permute-done | bytes 1310752 | tf_op jit(solution)/shard_map/ppermute | solution.py:48
  168.8 4.0 %shard_map.71 = f32[10,64,256]{2,1,0:T(8,128)S(1)} custom-call(s32[1280]{0:T(1024)S(1)} %add.221.pick_ref, s32[3]{0:T(128)S(1)} %add_convert_fusion.flag_ref, bf16[321,64,128]{2,1,0:T(8,128)(2,1)S(1)} %get-tuple-element.38.high, bf16[321,64,128]{2,1,0:T(8,128)(2,1)S(1)} %get-tuple-element.39.low, f32[20,64,256]{2,1,0:T(8,128)S(1)} %collective-permute-done.16.refs_0_, ...), custom_call_target="tpu_custom_call" | custom-call | flops 8000000000 | bytes 10000000 | tf_op jit(solution)/shard_map/pallas_call | solution.py:269
  172.7 2.9 %collective-permute-start.23 = (f32[10,64,256]{2,1,0:T(8,128)S(1)}, f32[10,64,256]{2,1,0:T(8,128)S(1)}, u32[]{:S(2)}, u32[]{:S(2)}) collective-permute-start(f32[10,64,256]{2,1,0:T(8,128)S(1)} %shard_map.71), channel_id=1, source_target_pairs={{0,8},{1,9},{2,10},{3,11},{4,12},{5,13},{6,14},{7,15},{8,0},{9,1},... | collective-permute-start | bytes 1966088 | tf_op jit(solution)/shard_map/ppermute | solution.py:48
  175.6 3.9 %shard_map.70 = f32[10,64,256]{2,1,0:T(8,128)S(1)} custom-call(s32[1280]{0:T(1024)S(1)} %add.221.pick_ref, s32[3]{0:T(128)S(1)} %add_convert_fusion.flag_ref, bf16[321,64,128]{2,1,0:T(8,128)(2,1)S(1)} %get-tuple-element.38.high, bf16[321,64,128]{2,1,0:T(8,128)(2,1)S(1)} %get-tuple-element.39.low, f32[20,64,256]{2,1,0:T(8,128)S(1)} %collective-permute-done.16.refs_0_, ...), custom_call_target="tpu_custom_call" | custom-call | flops 8000000000 | bytes 10000000 | tf_op jit(solution)/shard_map/pallas_call | solution.py:269
  183.1 8.0 %collective-permute-done.24 = f32[10,64,256]{2,1,0:T(8,128)S(1)} collective-permute-done((f32[10,64,256]{2,1,0:T(8,128)S(1)}, f32[10,64,256]{2,1,0:T(8,128)S(1)}, u32[]{:S(2)}, u32[]{:S(2)}) %collective-permute-start.24) | collective-permute-done | bytes 655392 | tf_op jit(solution)/shard_map/ppermute | solution.py:48
  191.2 6.9 %collective-permute-done.22 = f32[10,64,256]{2,1,0:T(8,128)S(1)} collective-permute-done((f32[10,64,256]{2,1,0:T(8,128)S(1)}, f32[10,64,256]{2,1,0:T(8,128)S(1)}, u32[]{:S(2)}, u32[]{:S(2)}) %collective-permute-start.22) | collective-permute-done | bytes 655392 | tf_op jit(solution)/shard_map/ppermute | solution.py:48
  (100 shorter events, 37.4 us)
Async XLA Ops:
  2.7 34.2 %all-to-all-start = ((f32[32,64,256]{2,1,0:T(8,128)}), f32[32,64,256]{2,1,0:T(8,128)S(1)}, u32[]{:S(2)}, u32[]{:S(2)}) async-start(f32[32,64,256]{2,1,0:T(8,128)} %shard_map.64), calls=%async_computation | async-start | bytes 4194304 | tf_op jit(solution)/shard_map/all_to_all | solution.py:350
  37.5 11.3 %collective-permute-start = (f32[20,64,256]{2,1,0:T(8,128)S(1)}, f32[20,64,256]{2,1,0:T(8,128)S(1)}, u32[]{:S(2)}, u32[]{:S(2)}) collective-permute-start(f32[20,64,256]{2,1,0:T(8,128)S(1)} %gather_fusion), channel_id=1, source_target_pairs={{0,8},{1,9},{2,10},{3,11},{4,12},{5,13},{6,14},{7,15},{8,0},{9,1},... | collective-permute-start | bytes 3932168 | tf_op jit(solution)/shard_map/ppermute | solution.py:48
  40.5 20.7 %collective-permute-start.5 = (f32[20,64,256]{2,1,0:T(8,128)S(1)}, f32[20,64,256]{2,1,0:T(8,128)S(1)}, u32[]{:S(2)}, u32[]{:S(2)}) collective-permute-start(f32[20,64,256]{2,1,0:T(8,128)S(1)} %gather_fusion), channel_id=1, source_target_pairs={{0,0},{1,9},{2,2},{3,11},{4,8},{5,1},{6,10},{7,3},{8,4},{9,13},{10... | collective-permute-start | bytes 3932168 | tf_op jit(solution)/shard_map/ppermute | solution.py:48
  45.0 18.8 %collective-permute-start.8 = (f32[20,64,256]{2,1,0:T(8,128)S(1)}, f32[20,64,256]{2,1,0:T(8,128)S(1)}, u32[]{:S(2)}, u32[]{:S(2)}) collective-permute-start(f32[20,64,256]{2,1,0:T(8,128)S(1)} %gather_fusion), channel_id=1, source_target_pairs={{0,2},{1,11},{2,0},{3,9},{12,14},{13,7},{14,12},{15,5},{16,18},{17... | collective-permute-start | bytes 3932168 | tf_op jit(solution)/shard_map/ppermute | solution.py:48
  45.8 32.4 %collective-permute-start.1 = (f32[20,64,256]{2,1,0:T(8,128)S(1)}, f32[20,64,256]{2,1,0:T(8,128)S(1)}, u32[]{:S(2)}, u32[]{:S(2)}) collective-permute-start(f32[20,64,256]{2,1,0:T(8,128)S(1)} %gather_fusion), channel_id=1, source_target_pairs={{0,16},{1,17},{2,18},{3,19},{4,20},{5,21},{6,22},{7,23},{8,24},{9,... | collective-permute-start | bytes 3932168 | tf_op jit(solution)/shard_map/ppermute | solution.py:48
  47.2 31.2 %collective-permute-start.3 = (f32[20,64,256]{2,1,0:T(8,128)S(1)}, f32[20,64,256]{2,1,0:T(8,128)S(1)}, u32[]{:S(2)}, u32[]{:S(2)}) collective-permute-start(f32[20,64,256]{2,1,0:T(8,128)S(1)} %gather_fusion), channel_id=1, source_target_pairs={{0,48},{1,49},{2,50},{3,51},{4,52},{5,53},{6,54},{7,55},{8,56},{9,... | collective-permute-start | bytes 3932168 | tf_op jit(solution)/shard_map/ppermute | solution.py:48
  61.2 36.0 %collective-permute-start.6 = (f32[20,64,256]{2,1,0:T(8,128)S(1)}, f32[20,64,256]{2,1,0:T(8,128)S(1)}, u32[]{:S(2)}, u32[]{:S(2)}) collective-permute-start(f32[20,64,256]{2,1,0:T(8,128)S(1)} %collective-permute-done.5.refs_0_), channel_id=1, source_target_pairs={{0,1},{1,2},{2,3},{3,0},{4,5},{5,6},{6,7},{7,4},{8,9},{9,10},{10,1... | collective-permute-start | bytes 3932168 | tf_op jit(solution)/shard_map/ppermute | solution.py:48
  61.2 36.0 %collective-permute-start.7 = (f32[20,64,256]{2,1,0:T(8,128)S(1)}, f32[20,64,256]{2,1,0:T(8,128)S(1)}, u32[]{:S(2)}, u32[]{:S(2)}) collective-permute-start(f32[20,64,256]{2,1,0:T(8,128)S(1)} %collective-permute-done.5.refs_0_), channel_id=1, source_target_pairs={{0,3},{1,0},{2,1},{3,2},{4,7},{5,4},{6,5},{7,6},{8,11},{9,8},{10,9... | collective-permute-start | bytes 3932168 | tf_op jit(solution)/shard_map/ppermute | solution.py:48
  63.9 33.3 %collective-permute-start.9 = (f32[20,64,256]{2,1,0:T(8,128)S(1)}, f32[20,64,256]{2,1,0:T(8,128)S(1)}, u32[]{:S(2)}, u32[]{:S(2)}) collective-permute-start(f32[20,64,256]{2,1,0:T(8,128)S(1)} %collective-permute-done.8.refs_3_), channel_id=1, source_target_pairs={{0,68},{2,70},{5,65},{7,67},{9,77},{11,79},{12,72},{14,74},{16,84}... | collective-permute-start | bytes 3932168 | tf_op jit(solution)/shard_map/ppermute | solution.py:48
  78.2 17.5 %collective-permute-start.2 = (f32[10,64,256]{2,1,0:T(8,128)S(1)}, f32[10,64,256]{2,1,0:T(8,128)S(1)}, u32[]{:S(2)}, u32[]{:S(2)}) collective-permute-start(f32[10,64,256]{2,1,0:T(8,128)S(1)} %slice.14), channel_id=1, source_target_pairs={{0,16},{1,17},{2,18},{3,19},{4,20},{5,21},{6,22},{7,23},{8,24},{9,... | collective-permute-start | bytes 1966088 | tf_op jit(solution)/shard_map/ppermute | solution.py:48
  78.4 17.3 %collective-permute-start.4 = (f32[10,64,256]{2,1,0:T(8,128)S(1)}, f32[10,64,256]{2,1,0:T(8,128)S(1)}, u32[]{:S(2)}, u32[]{:S(2)}) collective-permute-start(f32[10,64,256]{2,1,0:T(8,128)S(1)} %slice.15), channel_id=1, source_target_pairs={{0,48},{1,49},{2,50},{3,51},{4,52},{5,53},{6,54},{7,55},{8,56},{9,... | collective-permute-start | bytes 1966088 | tf_op jit(solution)/shard_map/ppermute | solution.py:48
  112.0 17.7 %collective-permute-start.11 = (f32[20,64,256]{2,1,0:T(8,128)S(1)}, f32[20,64,256]{2,1,0:T(8,128)S(1)}, u32[]{:S(2)}, u32[]{:S(2)}) collective-permute-start(f32[20,64,256]{2,1,0:T(8,128)S(1)} %get-tuple-element.42), channel_id=1, source_target_pairs={{0,64},{1,65},{2,66},{3,67},{4,12},{5,13},{6,14},{7,15},{8,0},{9,1... | collective-permute-start | bytes 3932168 | tf_op jit(solution)/shard_map/ppermute | solution.py:48
  112.4 20.1 %collective-permute-start.14 = (f32[20,64,256]{2,1,0:T(8,128)S(1)}, f32[20,64,256]{2,1,0:T(8,128)S(1)}, u32[]{:S(2)}, u32[]{:S(2)}) collective-permute-start(f32[20,64,256]{2,1,0:T(8,128)S(1)} %get-tuple-element.42), channel_id=1, source_target_pairs={{0,32},{1,33},{2,34},{3,35},{12,44},{13,45},{14,46},{15,47},{16,48... | collective-permute-start | bytes 3932168 | tf_op jit(solution)/shard_map/ppermute | solution.py:48
  113.7 23.0 %collective-permute-start.16 = (f32[20,64,256]{2,1,0:T(8,128)S(1)}, f32[20,64,256]{2,1,0:T(8,128)S(1)}, u32[]{:S(2)}, u32[]{:S(2)}) collective-permute-start(f32[20,64,256]{2,1,0:T(8,128)S(1)} %get-tuple-element.43), channel_id=1, source_target_pairs={{0,68},{1,9},{2,70},{3,11},{4,12},{5,65},{6,14},{7,67},{8,0},{9,77... | collective-permute-start | bytes 3932168 | tf_op jit(solution)/shard_map/ppermute | solution.py:48
  116.5 20.9 %collective-permute-start.19 = (f32[20,64,256]{2,1,0:T(8,128)S(1)}, f32[20,64,256]{2,1,0:T(8,128)S(1)}, u32[]{:S(2)}, u32[]{:S(2)}) collective-permute-start(f32[20,64,256]{2,1,0:T(8,128)S(1)} %get-tuple-element.43), channel_id=1, source_target_pairs={{0,2},{2,0},{5,7},{7,5},{9,11},{11,9},{12,14},{14,12},{16,18},{18,... | collective-permute-start | bytes 3932168 | tf_op jit(solution)/shard_map/ppermute | solution.py:48
  132.5 16.4 %collective-permute-start.15 = (f32[20,64,256]{2,1,0:T(8,128)S(1)}, f32[20,64,256]{2,1,0:T(8,128)S(1)}, u32[]{:S(2)}, u32[]{:S(2)}) collective-permute-start(f32[20,64,256]{2,1,0:T(8,128)S(1)} %collective-permute-done.14.refs_1_), channel_id=1, source_target_pairs={{4,68},{5,69},{6,70},{7,71},{8,72},{9,73},{10,74},{11,75},{20,84},... | collective-permute-start | bytes 3932168 | tf_op jit(solution)/shard_map/ppermute | solution.py:48
  134.5 29.7 %collective-permute-start.12 = (f32[20,64,256]{2,1,0:T(8,128)S(1)}, f32[20,64,256]{2,1,0:T(8,128)S(1)}, u32[]{:S(2)}, u32[]{:S(2)}) collective-permute-start(f32[20,64,256]{2,1,0:T(8,128)S(1)} %collective-permute-done.11.refs_0_), channel_id=1, source_target_pairs={{0,48},{1,49},{2,50},{3,51},{4,52},{5,53},{6,54},{7,55},{8,56},{9,... | collective-permute-start | bytes 3932168 | tf_op jit(solution)/shard_map/ppermute | solution.py:48
  134.5 29.6 %collective-permute-start.13 = (f32[20,64,256]{2,1,0:T(8,128)S(1)}, f32[20,64,256]{2,1,0:T(8,128)S(1)}, u32[]{:S(2)}, u32[]{:S(2)}) collective-permute-start(f32[20,64,256]{2,1,0:T(8,128)S(1)} %collective-permute-done.11.refs_0_), channel_id=1, source_target_pairs={{0,16},{1,17},{2,18},{3,19},{4,20},{5,21},{6,22},{7,23},{8,24},{9,... | collective-permute-start | bytes 3932168 | tf_op jit(solution)/shard_map/ppermute | solution.py:48
  136.7 29.3 %collective-permute-start.17 = (f32[20,64,256]{2,1,0:T(8,128)S(1)}, f32[20,64,256]{2,1,0:T(8,128)S(1)}, u32[]{:S(2)}, u32[]{:S(2)}) collective-permute-start(f32[20,64,256]{2,1,0:T(8,128)S(1)} %collective-permute-done.16.refs_0_), channel_id=1, source_target_pairs={{0,1},{1,2},{2,3},{3,0},{4,5},{5,6},{6,7},{7,4},{8,9},{9,10},{10,1... | collective-permute-start | bytes 3932168 | tf_op jit(solution)/shard_map/ppermute | solution.py:48
  137.5 28.5 %collective-permute-start.18 = (f32[20,64,256]{2,1,0:T(8,128)S(1)}, f32[20,64,256]{2,1,0:T(8,128)S(1)}, u32[]{:S(2)}, u32[]{:S(2)}) collective-permute-start(f32[20,64,256]{2,1,0:T(8,128)S(1)} %collective-permute-done.16.refs_0_), channel_id=1, source_target_pairs={{0,3},{1,0},{2,1},{3,2},{4,7},{5,4},{6,5},{7,6},{8,11},{9,8},{10,9... | collective-permute-start | bytes 3932168 | tf_op jit(solution)/shard_map/ppermute | solution.py:48
  148.9 19.8 %collective-permute-start.20 = (f32[20,64,256]{2,1,0:T(8,128)S(1)}, f32[20,64,256]{2,1,0:T(8,128)S(1)}, u32[]{:S(2)}, u32[]{:S(2)}) collective-permute-start(f32[20,64,256]{2,1,0:T(8,128)S(1)} %collective-permute-done.19.refs_3_), channel_id=1, source_target_pairs={{0,68},{2,70},{5,65},{7,67},{9,77},{11,79},{12,72},{14,74},{16,84}... | collective-permute-start | bytes 3932168 | tf_op jit(solution)/shard_map/ppermute | solution.py:48
  172.7 6.9 %collective-permute-start.23 = (f32[10,64,256]{2,1,0:T(8,128)S(1)}, f32[10,64,256]{2,1,0:T(8,128)S(1)}, u32[]{:S(2)}, u32[]{:S(2)}) collective-permute-start(f32[10,64,256]{2,1,0:T(8,128)S(1)} %shard_map.71), channel_id=1, source_target_pairs={{0,8},{1,9},{2,10},{3,11},{4,12},{5,13},{6,14},{7,15},{8,0},{9,1},... | collective-permute-start | bytes 1966088 | tf_op jit(solution)/shard_map/ppermute | solution.py:48
  179.7 11.3 %collective-permute-start.24 = (f32[10,64,256]{2,1,0:T(8,128)S(1)}, f32[10,64,256]{2,1,0:T(8,128)S(1)}, u32[]{:S(2)}, u32[]{:S(2)}) collective-permute-start(f32[10,64,256]{2,1,0:T(8,128)S(1)} %add.233), channel_id=1, source_target_pairs={{0,64},{1,65},{2,66},{3,67},{12,76},{13,77},{14,78},{15,79},{16,80... | collective-permute-start | bytes 1966088 | tf_op jit(solution)/shard_map/ppermute | solution.py:48
  181.8 16.3 %collective-permute-start.22 = (f32[10,64,256]{2,1,0:T(8,128)S(1)}, f32[10,64,256]{2,1,0:T(8,128)S(1)}, u32[]{:S(2)}, u32[]{:S(2)}) collective-permute-start(f32[10,64,256]{2,1,0:T(8,128)S(1)} %add.232), channel_id=1, source_target_pairs={{0,64},{1,65},{2,66},{3,67},{12,76},{13,77},{14,78},{15,79},{16,80... | collective-permute-start | bytes 1966088 | tf_op jit(solution)/shard_map/ppermute | solution.py:48
  (6 other events, 34.4 us)

commit v7 on v6

--- a/solution.py
+++ b/solution.py
@@ -85,9 +85,9 @@
     left_now = after(left, swapped)
     left_below = step(left_now, dz=1)
     left_above = step(left_now, dz=-1)
-    left_pair = send(across, left_pass)
     first = step(below[:half], dy=1)
     second = step(above[half:], dy=-1)
+    left_pair = send(after(across, below, above), left_pass)
     return (left, left_below, left_above, across, left_pair), (density, above, first, below, second, swapped)
 
 

time: 201 us -> 199 us (0.990)
  no operation moved by 1% of the time
where the time goes in v7:
time: 199 us; the launch traced here: 198 us
  waiting for transfers between devices  110 us (55%)
  starting transfers between devices  45.6 us (23%)
  Pallas kernels  24.7 us (12%)
  other arithmetic  11.6 us (6%)
  local copies, waits for them, and re-layouts  5.07 us (3%)
    ppermute x25, waiting for transfers between devices, send(): return lax.ppermute(x, AXES, moves(target))  95 us
    ppermute x25, starting transfers between devices, send(): return lax.ppermute(x, AXES, moves(target))  37.1 us
    pallas_call x3, Pallas kernels, product(): pl.pallas_call(functools.partial(product_kernel, first, begin, end, width...  16 us
    all_to_all x1, waiting for transfers between devices, body(): lax.all_to_all(plain_send, ('layer', 'col'), split_axis=0, concat_axis=0,...  14.9 us
    all_to_all x1, starting transfers between devices, body(): lax.all_to_all(plain_send, ('layer', 'col'), split_axis=0, concat_axis=0,...  8.56 us
    pallas_call x4, Pallas kernels, table(): pl.pallas_call(functools.partial(table_kernel, rows, width, span, jobs, c...  7.23 us
    reduce_sum x1, other arithmetic, pick_table(): found = jnp.sum(hit[..., None] * right_cols[None, :, None], axis=3)  5.6 us
  transfers between devices with their start and end apart: 26, of which 14 were waited for; matrix products, arithmetic and copies ran while one was open for 6% of the time, Pallas kernels for 6%

profile of v7, /device:TPU:1, one launch (start us, length us, event | category | flops | bytes accessed | tf_op | source)
XLA Modules:
  0.0 198.2 jit_solution(11318834828245227226)
XLA Ops:
  2.7 8.6 %all-to-all-start = ((f32[32,64,256]{2,1,0:T(8,128)}), f32[32,64,256]{2,1,0:T(8,128)S(1)}, u32[]{:S(2)}, u32[]{:S(2)}) async-start(f32[32,64,256]{2,1,0:T(8,128)} %shard_map.64), calls=%async_computation | async-start | bytes 4194304 | tf_op jit(solution)/shard_map/all_to_all | solution.py:350
  14.2 5.6 %multiply_reduce_fusion = s32[20,4,4,4]{3,2,1,0:T(4,128)S(1)} fusion(s32[4,20,4]{1,2,0:T(4,128)S(1)} %multiply_reduce_fusion.2, s32[20,4,4,20]{3,2,1,0:T(4,128)S(1)} %fusion), kind=kLoop, calls=%fused_computation.6 | loop fusion | flops 49920 | bytes 32000 | tf_op jit(solution)/shard_map/reduce_sum | solution.py:320
  22.0 14.9 %all-to-all-done = f32[32,64,256]{2,1,0:T(8,128)S(1)} async-done(((f32[32,64,256]{2,1,0:T(8,128)}), f32[32,64,256]{2,1,0:T(8,128)S(1)}, u32[]{:S(2)}, u32[]{:S(2)}) %all-to-all-start) | async-done | bytes 2097184 | tf_op jit(solution)/shard_map/all_to_all | solution.py:350
  37.5 2.9 %collective-permute-start = (f32[20,64,256]{2,1,0:T(8,128)S(1)}, f32[20,64,256]{2,1,0:T(8,128)S(1)}, u32[]{:S(2)}, u32[]{:S(2)}) collective-permute-start(f32[20,64,256]{2,1,0:T(8,128)S(1)} %gather_fusion), channel_id=1, source_target_pairs={{0,8},{1,9},{2,10},{3,11},{4,12},{5,13},{6,14},{7,15},{8,0},{9,1},... | collective-permute-start | bytes 3932168 | tf_op jit(solution)/shard_map/ppermute | solution.py:48
  40.5 4.6 %collective-permute-start.5 = (f32[20,64,256]{2,1,0:T(8,128)S(1)}, f32[20,64,256]{2,1,0:T(8,128)S(1)}, u32[]{:S(2)}, u32[]{:S(2)}) collective-permute-start(f32[20,64,256]{2,1,0:T(8,128)S(1)} %gather_fusion), channel_id=1, source_target_pairs={{0,0},{1,9},{2,2},{3,11},{4,8},{5,1},{6,10},{7,3},{8,4},{9,13},{10... | collective-permute-start | bytes 3932168 | tf_op jit(solution)/shard_map/ppermute | solution.py:48
  48.7 12.5 %collective-permute-done.5.refs_0_ = f32[20,64,256]{2,1,0:T(8,128)S(1)} collective-permute-done((f32[20,64,256]{2,1,0:T(8,128)S(1)}, f32[20,64,256]{2,1,0:T(8,128)S(1)}, u32[]{:S(2)}, u32[]{:S(2)}) %collective-permute-start.5) | collective-permute-done | bytes 1310752 | tf_op jit(solution)/shard_map/ppermute | solution.py:48
  61.2 2.7 %collective-permute-start.7 = (f32[20,64,256]{2,1,0:T(8,128)S(1)}, f32[20,64,256]{2,1,0:T(8,128)S(1)}, u32[]{:S(2)}, u32[]{:S(2)}) collective-permute-start(f32[20,64,256]{2,1,0:T(8,128)S(1)} %collective-permute-done.5.refs_0_), channel_id=1, source_target_pairs={{0,3},{1,0},{2,1},{3,2},{4,7},{5,4},{6,5},{7,6},{8,11},{9,8},{10,9... | collective-permute-start | bytes 3932168 | tf_op jit(solution)/shard_map/ppermute | solution.py:48
  63.9 13.3 %collective-permute-done.1.refs_3_ = f32[20,64,256]{2,1,0:T(8,128)S(1)} collective-permute-done((f32[20,64,256]{2,1,0:T(8,128)S(1)}, f32[20,64,256]{2,1,0:T(8,128)S(1)}, u32[]{:S(2)}, u32[]{:S(2)}) %collective-permute-start.1) | collective-permute-done | bytes 1310752 | tf_op jit(solution)/shard_map/ppermute | solution.py:48
  78.7 2.7 %collective-permute-start.4 = (f32[10,64,256]{2,1,0:T(8,128)S(1)}, f32[10,64,256]{2,1,0:T(8,128)S(1)}, u32[]{:S(2)}, u32[]{:S(2)}) collective-permute-start(f32[10,64,256]{2,1,0:T(8,128)S(1)} %slice.15), channel_id=1, source_target_pairs={{0,48},{1,49},{2,50},{3,51},{4,52},{5,53},{6,54},{7,55},{8,56},{9,... | collective-permute-start | bytes 1966088 | tf_op jit(solution)/shard_map/ppermute | solution.py:48
  81.4 2.3 %shard_map.65 = (bf16[321,64,128]{2,1,0:T(8,128)(2,1)S(1)}, bf16[321,64,128]{2,1,0:T(8,128)(2,1)S(1)}) custom-call(s32[3]{0:T(128)S(1)} %add_convert_fusion.flag_ref, f32[20,64,256]{2,1,0:T(8,128)S(1)} %collective-permute-done.refs_0_, f32[20,64,256]{2,1,0:T(8,128)S(1)} %gather_fusion, f32[20,64,256]{2,1,0:T(8,128)S(1)} %collective-permute-done.3.refs_2_, ...), custom_call_target="tpu_custom_call" | custom-call | flops 2000000000 | bytes 10000000 | tf_op jit(solution)/shard_map/pallas_call | solution.py:187
  83.8 11.3 %collective-permute-done.2.refs_0_ = f32[10,64,256]{2,1,0:T(8,128)S(1)} collective-permute-done((f32[10,64,256]{2,1,0:T(8,128)S(1)}, f32[10,64,256]{2,1,0:T(8,128)S(1)}, u32[]{:S(2)}, u32[]{:S(2)}) %collective-permute-start.2) | collective-permute-done | bytes 655392 | tf_op jit(solution)/shard_map/ppermute | solution.py:48
  97.2 8.1 %shard_map.67 = f32[20,64,256]{2,1,0:T(8,128)} custom-call(s32[1280]{0:T(1024)S(1)} %add.221.pick_ref, s32[3]{0:T(128)S(1)} %add_convert_fusion.flag_ref, bf16[321,64,128]{2,1,0:T(8,128)(2,1)S(1)} %get-tuple-element.32.high, bf16[321,64,128]{2,1,0:T(8,128)(2,1)S(1)} %get-tuple-element.33.low, f32[20,64,256]{2,1,0:T(8,128)S(1)} %collective-permute-done.5.refs_0_, ...), custom_call_target="tpu_custom_call" | custom-call | flops 8000000000 | bytes 10000000 | tf_op jit(solution)/shard_map/pallas_call | solution.py:269
  109.9 2.4 %multiply_add_fusion = (f32[20,64,256]{2,1,0:T(8,128)S(1)}, f32[20,64,256]{2,1,0:T(8,128)S(1)}) fusion(f32[20,64,256]{2,1,0:T(8,128)S(1)} %gather_fusion, f32[20,64,256]{2,1,0:T(8,128)S(1)} %collective-permute-done.refs_0_, f32[]{:T(128)S(6)} %sub.64, f32[]{:T(128)S(6)} %sub.63, f32[64,256]{1,0:T(8,128)S(1)} %mul.176, f32[20,256]{1,0:T(8,128)S(1)} %mul.173, ...), kind=kLoop, calls=%fused_computation.4 | loop fusion | flops 2949120 | bytes 7970829 | tf_op jit(solution)/shard_map/add | solution.py:379
  114.0 3.4 %collective-permute-start.16 = (f32[20,64,256]{2,1,0:T(8,128)S(1)}, f32[20,64,256]{2,1,0:T(8,128)S(1)}, u32[]{:S(2)}, u32[]{:S(2)}) collective-permute-start(f32[20,64,256]{2,1,0:T(8,128)S(1)} %get-tuple-element.45), channel_id=1, source_target_pairs={{0,68},{1,9},{2,70},{3,11},{4,12},{5,65},{6,14},{7,67},{8,0},{9,77... | collective-permute-start | bytes 3932168 | tf_op jit(solution)/shard_map/ppermute | solution.py:48
  118.1 11.0 %collective-permute-done.11.refs_0_ = f32[20,64,256]{2,1,0:T(8,128)S(1)} collective-permute-done((f32[20,64,256]{2,1,0:T(8,128)S(1)}, f32[20,64,256]{2,1,0:T(8,128)S(1)}, u32[]{:S(2)}, u32[]{:S(2)}) %collective-permute-start.11) | collective-permute-done | bytes 1310752 | tf_op jit(solution)/shard_map/ppermute | solution.py:48
  129.1 3.8 %collective-permute-done.14.refs_1_ = f32[20,64,256]{2,1,0:T(8,128)S(1)} collective-permute-done((f32[20,64,256]{2,1,0:T(8,128)S(1)}, f32[20,64,256]{2,1,0:T(8,128)S(1)}, u32[]{:S(2)}, u32[]{:S(2)}) %collective-permute-start.14) | collective-permute-done | bytes 1310752 | tf_op jit(solution)/shard_map/ppermute | solution.py:48
  135.8 2.7 %collective-permute-start.18 = (f32[20,64,256]{2,1,0:T(8,128)S(1)}, f32[20,64,256]{2,1,0:T(8,128)S(1)}, u32[]{:S(2)}, u32[]{:S(2)}) collective-permute-start(f32[20,64,256]{2,1,0:T(8,128)S(1)} %collective-permute-done.16.refs_0_), channel_id=1, source_target_pairs={{0,3},{1,0},{2,1},{3,2},{4,7},{5,4},{6,5},{7,6},{8,11},{9,8},{10,9... | collective-permute-start | bytes 3932168 | tf_op jit(solution)/shard_map/ppermute | solution.py:48
  138.5 10.2 %collective-permute-done.15.refs_2_ = f32[20,64,256]{2,1,0:T(8,128)S(1)} collective-permute-done((f32[20,64,256]{2,1,0:T(8,128)S(1)}, f32[20,64,256]{2,1,0:T(8,128)S(1)}, u32[]{:S(2)}, u32[]{:S(2)}) %collective-permute-start.15) | collective-permute-done | bytes 1310752 | tf_op jit(solution)/shard_map/ppermute | solution.py:48
  151.7 13.2 %collective-permute-done.12.refs_0_ = f32[20,64,256]{2,1,0:T(8,128)S(1)} collective-permute-done((f32[20,64,256]{2,1,0:T(8,128)S(1)}, f32[20,64,256]{2,1,0:T(8,128)S(1)}, u32[]{:S(2)}, u32[]{:S(2)}) %collective-permute-start.12) | collective-permute-done | bytes 1310752 | tf_op jit(solution)/shard_map/ppermute | solution.py:48
  168.2 4.0 %shard_map.71 = f32[10,64,256]{2,1,0:T(8,128)S(1)} custom-call(s32[1280]{0:T(1024)S(1)} %add.221.pick_ref, s32[3]{0:T(128)S(1)} %add_convert_fusion.flag_ref, bf16[321,64,128]{2,1,0:T(8,128)(2,1)S(1)} %get-tuple-element.40.high, bf16[321,64,128]{2,1,0:T(8,128)(2,1)S(1)} %get-tuple-element.41.low, f32[20,64,256]{2,1,0:T(8,128)S(1)} %collective-permute-done.16.refs_0_, ...), custom_call_target="tpu_custom_call" | custom-call | flops 8000000000 | bytes 10000000 | tf_op jit(solution)/shard_map/pallas_call | solution.py:269
  172.2 2.3 %collective-permute-start.23 = (f32[10,64,256]{2,1,0:T(8,128)S(1)}, f32[10,64,256]{2,1,0:T(8,128)S(1)}, u32[]{:S(2)}, u32[]{:S(2)}) collective-permute-start(f32[10,64,256]{2,1,0:T(8,128)S(1)} %shard_map.71), channel_id=1, source_target_pairs={{0,8},{1,9},{2,10},{3,11},{4,12},{5,13},{6,14},{7,15},{8,0},{9,1},... | collective-permute-start | bytes 1966088 | tf_op jit(solution)/shard_map/ppermute | solution.py:48
  174.5 3.9 %shard_map.70 = f32[10,64,256]{2,1,0:T(8,128)S(1)} custom-call(s32[1280]{0:T(1024)S(1)} %add.221.pick_ref, s32[3]{0:T(128)S(1)} %add_convert_fusion.flag_ref, bf16[321,64,128]{2,1,0:T(8,128)(2,1)S(1)} %get-tuple-element.40.high, bf16[321,64,128]{2,1,0:T(8,128)(2,1)S(1)} %get-tuple-element.41.low, f32[20,64,256]{2,1,0:T(8,128)S(1)} %collective-permute-done.16.refs_0_, ...), custom_call_target="tpu_custom_call" | custom-call | flops 8000000000 | bytes 10000000 | tf_op jit(solution)/shard_map/pallas_call | solution.py:269
  182.0 8.0 %collective-permute-done.24 = f32[10,64,256]{2,1,0:T(8,128)S(1)} collective-permute-done((f32[10,64,256]{2,1,0:T(8,128)S(1)}, f32[10,64,256]{2,1,0:T(8,128)S(1)}, u32[]{:S(2)}, u32[]{:S(2)}) %collective-permute-start.24) | collective-permute-done | bytes 655392 | tf_op jit(solution)/shard_map/ppermute | solution.py:48
  190.0 6.9 %collective-permute-done.22 = f32[10,64,256]{2,1,0:T(8,128)S(1)} collective-permute-done((f32[10,64,256]{2,1,0:T(8,128)S(1)}, f32[10,64,256]{2,1,0:T(8,128)S(1)}, u32[]{:S(2)}, u32[]{:S(2)}) %collective-permute-start.22) | collective-permute-done | bytes 655392 | tf_op jit(solution)/shard_map/ppermute | solution.py:48
  (100 shorter events, 35.8 us)
Async XLA Ops:
  2.7 34.2 %all-to-all-start = ((f32[32,64,256]{2,1,0:T(8,128)}), f32[32,64,256]{2,1,0:T(8,128)S(1)}, u32[]{:S(2)}, u32[]{:S(2)}) async-start(f32[32,64,256]{2,1,0:T(8,128)} %shard_map.64), calls=%async_computation | async-start | bytes 4194304 | tf_op jit(solution)/shard_map/all_to_all | solution.py:350
  37.5 11.1 %collective-permute-start = (f32[20,64,256]{2,1,0:T(8,128)S(1)}, f32[20,64,256]{2,1,0:T(8,128)S(1)}, u32[]{:S(2)}, u32[]{:S(2)}) collective-permute-start(f32[20,64,256]{2,1,0:T(8,128)S(1)} %gather_fusion), channel_id=1, source_target_pairs={{0,8},{1,9},{2,10},{3,11},{4,12},{5,13},{6,14},{7,15},{8,0},{9,1},... | collective-permute-start | bytes 3932168 | tf_op jit(solution)/shard_map/ppermute | solution.py:48
  40.5 20.7 %collective-permute-start.5 = (f32[20,64,256]{2,1,0:T(8,128)S(1)}, f32[20,64,256]{2,1,0:T(8,128)S(1)}, u32[]{:S(2)}, u32[]{:S(2)}) collective-permute-start(f32[20,64,256]{2,1,0:T(8,128)S(1)} %gather_fusion), channel_id=1, source_target_pairs={{0,0},{1,9},{2,2},{3,11},{4,8},{5,1},{6,10},{7,3},{8,4},{9,13},{10... | collective-permute-start | bytes 3932168 | tf_op jit(solution)/shard_map/ppermute | solution.py:48
  45.0 32.1 %collective-permute-start.1 = (f32[20,64,256]{2,1,0:T(8,128)S(1)}, f32[20,64,256]{2,1,0:T(8,128)S(1)}, u32[]{:S(2)}, u32[]{:S(2)}) collective-permute-start(f32[20,64,256]{2,1,0:T(8,128)S(1)} %gather_fusion), channel_id=1, source_target_pairs={{0,16},{1,17},{2,18},{3,19},{4,20},{5,21},{6,22},{7,23},{8,24},{9,... | collective-permute-start | bytes 3932168 | tf_op jit(solution)/shard_map/ppermute | solution.py:48
  46.4 30.8 %collective-permute-start.3 = (f32[20,64,256]{2,1,0:T(8,128)S(1)}, f32[20,64,256]{2,1,0:T(8,128)S(1)}, u32[]{:S(2)}, u32[]{:S(2)}) collective-permute-start(f32[20,64,256]{2,1,0:T(8,128)S(1)} %gather_fusion), channel_id=1, source_target_pairs={{0,48},{1,49},{2,50},{3,51},{4,52},{5,53},{6,54},{7,55},{8,56},{9,... | collective-permute-start | bytes 3932168 | tf_op jit(solution)/shard_map/ppermute | solution.py:48
  47.9 29.3 %collective-permute-start.8 = (f32[20,64,256]{2,1,0:T(8,128)S(1)}, f32[20,64,256]{2,1,0:T(8,128)S(1)}, u32[]{:S(2)}, u32[]{:S(2)}) collective-permute-start(f32[20,64,256]{2,1,0:T(8,128)S(1)} %gather_fusion), channel_id=1, source_target_pairs={{0,2},{1,11},{2,0},{3,9},{12,14},{13,7},{14,12},{15,5},{16,18},{17... | collective-permute-start | bytes 3932168 | tf_op jit(solution)/shard_map/ppermute | solution.py:48
  61.2 36.0 %collective-permute-start.6 = (f32[20,64,256]{2,1,0:T(8,128)S(1)}, f32[20,64,256]{2,1,0:T(8,128)S(1)}, u32[]{:S(2)}, u32[]{:S(2)}) collective-permute-start(f32[20,64,256]{2,1,0:T(8,128)S(1)} %collective-permute-done.5.refs_0_), channel_id=1, source_target_pairs={{0,1},{1,2},{2,3},{3,0},{4,5},{5,6},{6,7},{7,4},{8,9},{9,10},{10,1... | collective-permute-start | bytes 3932168 | tf_op jit(solution)/shard_map/ppermute | solution.py:48
  61.2 36.0 %collective-permute-start.7 = (f32[20,64,256]{2,1,0:T(8,128)S(1)}, f32[20,64,256]{2,1,0:T(8,128)S(1)}, u32[]{:S(2)}, u32[]{:S(2)}) collective-permute-start(f32[20,64,256]{2,1,0:T(8,128)S(1)} %collective-permute-done.5.refs_0_), channel_id=1, source_target_pairs={{0,3},{1,0},{2,1},{3,2},{4,7},{5,4},{6,5},{7,6},{8,11},{9,8},{10,9... | collective-permute-start | bytes 3932168 | tf_op jit(solution)/shard_map/ppermute | solution.py:48
  77.2 20.0 %collective-permute-start.9 = (f32[20,64,256]{2,1,0:T(8,128)S(1)}, f32[20,64,256]{2,1,0:T(8,128)S(1)}, u32[]{:S(2)}, u32[]{:S(2)}) collective-permute-start(f32[20,64,256]{2,1,0:T(8,128)S(1)} %collective-permute-done.8.refs_3_), channel_id=1, source_target_pairs={{0,68},{2,70},{5,65},{7,67},{9,77},{11,79},{12,72},{14,74},{16,84}... | collective-permute-start | bytes 3932168 | tf_op jit(solution)/shard_map/ppermute | solution.py:48
  78.5 16.5 %collective-permute-start.2 = (f32[10,64,256]{2,1,0:T(8,128)S(1)}, f32[10,64,256]{2,1,0:T(8,128)S(1)}, u32[]{:S(2)}, u32[]{:S(2)}) collective-permute-start(f32[10,64,256]{2,1,0:T(8,128)S(1)} %slice.14), channel_id=1, source_target_pairs={{0,16},{1,17},{2,18},{3,19},{4,20},{5,21},{6,22},{7,23},{8,24},{9,... | collective-permute-start | bytes 1966088 | tf_op jit(solution)/shard_map/ppermute | solution.py:48
  78.7 16.4 %collective-permute-start.4 = (f32[10,64,256]{2,1,0:T(8,128)S(1)}, f32[10,64,256]{2,1,0:T(8,128)S(1)}, u32[]{:S(2)}, u32[]{:S(2)}) collective-permute-start(f32[10,64,256]{2,1,0:T(8,128)S(1)} %slice.15), channel_id=1, source_target_pairs={{0,48},{1,49},{2,50},{3,51},{4,52},{5,53},{6,54},{7,55},{8,56},{9,... | collective-permute-start | bytes 1966088 | tf_op jit(solution)/shard_map/ppermute | solution.py:48
  112.3 16.8 %collective-permute-start.11 = (f32[20,64,256]{2,1,0:T(8,128)S(1)}, f32[20,64,256]{2,1,0:T(8,128)S(1)}, u32[]{:S(2)}, u32[]{:S(2)}) collective-permute-start(f32[20,64,256]{2,1,0:T(8,128)S(1)} %get-tuple-element.44), channel_id=1, source_target_pairs={{0,64},{1,65},{2,66},{3,67},{4,12},{5,13},{6,14},{7,15},{8,0},{9,1... | collective-permute-start | bytes 3932168 | tf_op jit(solution)/shard_map/ppermute | solution.py:48
  112.7 20.1 %collective-permute-start.14 = (f32[20,64,256]{2,1,0:T(8,128)S(1)}, f32[20,64,256]{2,1,0:T(8,128)S(1)}, u32[]{:S(2)}, u32[]{:S(2)}) collective-permute-start(f32[20,64,256]{2,1,0:T(8,128)S(1)} %get-tuple-element.44), channel_id=1, source_target_pairs={{0,32},{1,33},{2,34},{3,35},{12,44},{13,45},{14,46},{15,47},{16,48... | collective-permute-start | bytes 3932168 | tf_op jit(solution)/shard_map/ppermute | solution.py:48
  114.0 21.8 %collective-permute-start.16 = (f32[20,64,256]{2,1,0:T(8,128)S(1)}, f32[20,64,256]{2,1,0:T(8,128)S(1)}, u32[]{:S(2)}, u32[]{:S(2)}) collective-permute-start(f32[20,64,256]{2,1,0:T(8,128)S(1)} %get-tuple-element.45), channel_id=1, source_target_pairs={{0,68},{1,9},{2,70},{3,11},{4,12},{5,65},{6,14},{7,67},{8,0},{9,77... | collective-permute-start | bytes 3932168 | tf_op jit(solution)/shard_map/ppermute | solution.py:48
  117.4 18.4 %collective-permute-start.19 = (f32[20,64,256]{2,1,0:T(8,128)S(1)}, f32[20,64,256]{2,1,0:T(8,128)S(1)}, u32[]{:S(2)}, u32[]{:S(2)}) collective-permute-start(f32[20,64,256]{2,1,0:T(8,128)S(1)} %get-tuple-element.45), channel_id=1, source_target_pairs={{0,2},{2,0},{5,7},{7,5},{9,11},{11,9},{12,14},{14,12},{16,18},{18,... | collective-permute-start | bytes 3932168 | tf_op jit(solution)/shard_map/ppermute | solution.py:48
  132.9 15.8 %collective-permute-start.15 = (f32[20,64,256]{2,1,0:T(8,128)S(1)}, f32[20,64,256]{2,1,0:T(8,128)S(1)}, u32[]{:S(2)}, u32[]{:S(2)}) collective-permute-start(f32[20,64,256]{2,1,0:T(8,128)S(1)} %collective-permute-done.14.refs_1_), channel_id=1, source_target_pairs={{4,68},{5,69},{6,70},{7,71},{8,72},{9,73},{10,74},{11,75},{20,84},... | collective-permute-start | bytes 3932168 | tf_op jit(solution)/shard_map/ppermute | solution.py:48
  134.2 30.7 %collective-permute-start.12 = (f32[20,64,256]{2,1,0:T(8,128)S(1)}, f32[20,64,256]{2,1,0:T(8,128)S(1)}, u32[]{:S(2)}, u32[]{:S(2)}) collective-permute-start(f32[20,64,256]{2,1,0:T(8,128)S(1)} %collective-permute-done.11.refs_0_), channel_id=1, source_target_pairs={{0,48},{1,49},{2,50},{3,51},{4,52},{5,53},{6,54},{7,55},{8,56},{9,... | collective-permute-start | bytes 3932168 | tf_op jit(solution)/shard_map/ppermute | solution.py:48
  134.3 30.6 %collective-permute-start.13 = (f32[20,64,256]{2,1,0:T(8,128)S(1)}, f32[20,64,256]{2,1,0:T(8,128)S(1)}, u32[]{:S(2)}, u32[]{:S(2)}) collective-permute-start(f32[20,64,256]{2,1,0:T(8,128)S(1)} %collective-permute-done.11.refs_0_), channel_id=1, source_target_pairs={{0,16},{1,17},{2,18},{3,19},{4,20},{5,21},{6,22},{7,23},{8,24},{9,... | collective-permute-start | bytes 3932168 | tf_op jit(solution)/shard_map/ppermute | solution.py:48
  135.8 30.9 %collective-permute-start.17 = (f32[20,64,256]{2,1,0:T(8,128)S(1)}, f32[20,64,256]{2,1,0:T(8,128)S(1)}, u32[]{:S(2)}, u32[]{:S(2)}) collective-permute-start(f32[20,64,256]{2,1,0:T(8,128)S(1)} %collective-permute-done.16.refs_0_), channel_id=1, source_target_pairs={{0,1},{1,2},{2,3},{3,0},{4,5},{5,6},{6,7},{7,4},{8,9},{9,10},{10,1... | collective-permute-start | bytes 3932168 | tf_op jit(solution)/shard_map/ppermute | solution.py:48
  135.8 30.9 %collective-permute-start.18 = (f32[20,64,256]{2,1,0:T(8,128)S(1)}, f32[20,64,256]{2,1,0:T(8,128)S(1)}, u32[]{:S(2)}, u32[]{:S(2)}) collective-permute-start(f32[20,64,256]{2,1,0:T(8,128)S(1)} %collective-permute-done.16.refs_0_), channel_id=1, source_target_pairs={{0,3},{1,0},{2,1},{3,2},{4,7},{5,4},{6,5},{7,6},{8,11},{9,8},{10,9... | collective-permute-start | bytes 3932168 | tf_op jit(solution)/shard_map/ppermute | solution.py:48
  148.7 19.6 %collective-permute-start.20 = (f32[20,64,256]{2,1,0:T(8,128)S(1)}, f32[20,64,256]{2,1,0:T(8,128)S(1)}, u32[]{:S(2)}, u32[]{:S(2)}) collective-permute-start(f32[20,64,256]{2,1,0:T(8,128)S(1)} %collective-permute-done.19.refs_3_), channel_id=1, source_target_pairs={{0,68},{2,70},{5,65},{7,67},{9,77},{11,79},{12,72},{14,74},{16,84}... | collective-permute-start | bytes 3932168 | tf_op jit(solution)/shard_map/ppermute | solution.py:48
  172.2 6.3 %collective-permute-start.23 = (f32[10,64,256]{2,1,0:T(8,128)S(1)}, f32[10,64,256]{2,1,0:T(8,128)S(1)}, u32[]{:S(2)}, u32[]{:S(2)}) collective-permute-start(f32[10,64,256]{2,1,0:T(8,128)S(1)} %shard_map.71), channel_id=1, source_target_pairs={{0,8},{1,9},{2,10},{3,11},{4,12},{5,13},{6,14},{7,15},{8,0},{9,1},... | collective-permute-start | bytes 1966088 | tf_op jit(solution)/shard_map/ppermute | solution.py:48
  178.6 11.3 %collective-permute-start.24 = (f32[10,64,256]{2,1,0:T(8,128)S(1)}, f32[10,64,256]{2,1,0:T(8,128)S(1)}, u32[]{:S(2)}, u32[]{:S(2)}) collective-permute-start(f32[10,64,256]{2,1,0:T(8,128)S(1)} %add.233), channel_id=1, source_target_pairs={{0,64},{1,65},{2,66},{3,67},{12,76},{13,77},{14,78},{15,79},{16,80... | collective-permute-start | bytes 1966088 | tf_op jit(solution)/shard_map/ppermute | solution.py:48
  180.7 16.3 %collective-permute-start.22 = (f32[10,64,256]{2,1,0:T(8,128)S(1)}, f32[10,64,256]{2,1,0:T(8,128)S(1)}, u32[]{:S(2)}, u32[]{:S(2)}) collective-permute-start(f32[10,64,256]{2,1,0:T(8,128)S(1)} %add.232), channel_id=1, source_target_pairs={{0,64},{1,65},{2,66},{3,67},{12,76},{13,77},{14,78},{15,79},{16,80... | collective-permute-start | bytes 1966088 | tf_op jit(solution)/shard_map/ppermute | solution.py:48
  (6 other events, 34.8 us)
